TPU v7x, 128 devices: a whole 4x4x4 slice. The times are simulated.
128 devices in a mesh: mp: 2 (over core), tx: 8 (over y, z_lo), ty: 8 (over x, z_hi).
Axes of the slice: x: 4, y: 4, z: 4 (z_hi: 2, z_lo: 2; z = z_hi * 2 + z_lo), core: 2. Of those that a mesh axis runs over, the one named last changes fastest.
Arguments:
- state: float32 [2, 16, 256, 3600], P('mp', None, 'tx', 'ty'), may hold values from -6 to 6
- diffusion: float32 [2, 256, 3600], P('mp', 'tx', 'ty'), may hold values from 0.03 to 0.22
- exchange_rate: float32 [2, 256, 3600], P('mp', 'tx', 'ty'), may hold values from 0.05 to 0.5
- land_mask: int32 [256, 3600], P('tx', 'ty'), may hold values 0 or 1
- fold_map: int32 [3600], P('ty'), may hold values from 0 to 3599, each once
- entry_tile: int32 [2, 8, 384, 1], P('mp', 'tx', 'ty'), may hold values from 0 to 63; in each aligned block of 48 rows (0 to 47, 48 to 95, ..., all dimensions but the last counted through in order) at most 3 rows name the same one
- entry_source: int32 [2, 8, 384], P('mp', 'tx', 'ty'), may hold values from 0 to 31
- entry_dest: int32 [2, 8, 384], P('mp', 'tx', 'ty'), may hold values from 0 to 31
- entry_weight: bfloat16 [2, 8, 384, 450, 450], P('mp', 'tx', 'ty'), may hold values from -0.1875 to 0.1875
Outputs:
- new_state: float32 [2, 16, 256, 3600], P('mp', None, 'tx', 'ty')
Inputs may be any that keep to these rules, and one draw needn't show every extreme that they name: `entry_tile`: in each model, the blocks of one tile name each destination tile at most 3 times; some destination tile is named exactly 3 times. `fold_map`: a permutation.
All inputs are finite; a program needn't handle non-finite values. No bound on the sum of `land_mask` on one device may be relied on, other than what follows from the above.
Results may differ from a plain program's by a relative error of at most 0.0011.
Values sent between devices are 32-bit elements; how exact they have to be, the bound alone decides.
No kernel may reach another device: no remote copies, remote signals or barrier semaphores. Data moves between devices by JAX's collectives and lax.ppermute only.
A program may use at most 128 MiB of HBM per device.

v0:
```python
import jax
import jax.numpy as jnp
from jax import lax
from jax.sharding import PartitionSpec as P


def partner(value, axis, stride):
    mask = 2**stride
    pairs = [(source, source ^ mask) for source in range(lax.axis_size(axis))]
    return lax.ppermute(value, axis, pairs)


def extended(block, sides, width, periodic):
    for axis, dim in sides:
        count = lax.axis_size(axis)
        forward = [(i, i + 1) for i in range(count - 1)]
        if periodic:
            forward.append((count - 1, 0))
        backward = [(target, source) for source, target in forward]
        low = lax.ppermute(
            lax.slice_in_dim(block, block.shape[dim] - width, None, axis=dim), axis, forward
        )
        high = lax.ppermute(lax.slice_in_dim(block, 0, width, axis=dim), axis, backward)
        block = jnp.concatenate([low, block, high], axis=dim)
    return block


def other_side(pair):
    return partner((pair[0], pair[1]), "mp", 0)


def route_blocks(pair):
    buffer, labels = pair
    return (
        lax.all_to_all(buffer, ("tx", "ty"), split_axis=0, concat_axis=0, tiled=True),
        lax.all_to_all(labels, ("tx", "ty"), split_axis=0, concat_axis=0, tiled=True),
    )


def one_sweep(field, coef, fold_map, fold_here):
    zonal = extended(field, (("ty", 2),), 1, True)
    merid = extended(field, (("tx", 1),), 1, False)
    whole_row = lax.all_gather(field[:, -1, :], "ty", axis=1, tiled=True)
    folded = jnp.take(whole_row, fold_map, axis=1)
    rows = field.shape[1]
    north = jnp.where(fold_here, folded, merid[:, rows + 1])
    above = jnp.concatenate([merid[:, 2 : rows + 1], north[:, None]], axis=1)
    below = merid[:, :rows]
    east = zonal[:, :, 2:]
    west = zonal[:, :, :-2]
    return field + coef * (above + below + east + west - 4.0 * field)


def body(
    state,
    diffusion,
    exchange_rate,
    land_mask,
    fold_map,
    entry_tile,
    entry_source,
    entry_dest,
    entry_weight,
):
    field = state[0]
    levels, rows, cols = field.shape
    rows_x = lax.axis_size("tx")
    rows_y = lax.axis_size("ty")
    tiles = rows_x * rows_y
    entries = entry_source.shape[2]
    slots_per = 4 * entries // tiles
    ocean = lax.axis_index("mp") == 1
    sent = field.astype(jnp.bfloat16)
    picked = jnp.take(sent, entry_source[0, 0], axis=1)
    contrib = jnp.einsum(
        "eij,lej->eli", entry_weight[0, 0], picked, preferred_element_type=jnp.float32
    )
    target_tile = entry_tile[0, 0, :, 0]
    onehot = (target_tile[:, None] == jnp.arange(tiles, dtype=jnp.int32)[None, :]).astype(jnp.int32)
    running = jnp.cumsum(onehot, axis=0)
    rank = jnp.sum(onehot * running, axis=1) - 1
    slot = target_tile * slots_per + rank
    buffer = jnp.zeros((tiles * slots_per, levels, cols), jnp.float32).at[slot].set(contrib)
    labels = (
        jnp.full((tiles * slots_per,), -1.0, jnp.float32)
        .at[slot]
        .set(entry_dest[0, 0].astype(jnp.float32))
    )
    buffer = buffer.reshape(tiles, slots_per, levels, cols)
    labels = labels.reshape(tiles, slots_per)
    arrived, arrived_rows = other_side(route_blocks((buffer, labels)))
    arrived = arrived.reshape(tiles * slots_per, levels, cols)
    row_ids = arrived_rows.reshape(tiles * slots_per).astype(jnp.int32)
    row_ids = jnp.where(row_ids < 0, rows, row_ids)
    summed = jax.ops.segment_sum(arrived, row_ids, num_segments=rows + 1)
    received = jnp.transpose(summed[:rows], (1, 0, 2))
    sea = land_mask.astype(jnp.float32)
    active = jnp.where(ocean, sea, jnp.ones_like(sea))
    coef = diffusion[0] * active
    fold_here = jnp.logical_and(ocean, lax.axis_index("tx") == rows_x - 1)
    moved = field
    for step_number in range(2):
        step_coef = coef if step_number == 0 else jnp.where(ocean, jnp.zeros_like(coef), coef)
        moved = one_sweep(moved, step_coef, fold_map, fold_here)
    result = moved + exchange_rate[0] * active * (received - field)
    return result[None]


def solution(mesh):
    in_specs = (
        P("mp", None, "tx", "ty"),
        P("mp", "tx", "ty"),
        P("mp", "tx", "ty"),
        P("tx", "ty"),
        P("ty"),
        P("mp", "tx", "ty", None),
        P("mp", "tx", "ty"),
        P("mp", "tx", "ty"),
        P("mp", "tx", "ty", None, None),
    )
    out_specs = P("mp", None, "tx", "ty")
    return jax.shard_map(body, mesh=mesh, in_specs=in_specs, out_specs=out_specs, check_vma=False)
```

profile of v0, /device:TPU:8, one launch (start us, length us, event | category | flops | bytes accessed | tf_op | source)
XLA Modules:
  0.0 298.2 jit_solution(3240912599341124791)
XLA Ops:
  3.6 1.3 bitcast_convert_fusion
  5.9 27.6 %fusion = f32[48,16,450]{2,1,0:T(8,128)S(1)} fusion(bf16[48,450,450]{2,0,1:T(8,128)(2,1)} %bitcast.58, bf16[48,16,450]{2,1,0:T(8,128)(2,1)S(1)} %gather_fusion, pred[48]{0:T(512)(128)(4,1)S(1)} %compare_and_fusion.1), kind=kOutput, calls=%fused_computation.6 | convolution fusion | flops 311385600 | bytes 21513648 | tf_op jit(solution)/shard_map/eij,lej->eli/dot_general | solution.py:75
  33.5 3.5 %broadcast_in_dim.61 = f32[192,16,450]{2,1,0:T(8,128)} broadcast(f32[]{:T(128)} %constant.33.clone.1), dimensions={} | broadcast | bytes 5529604 | tf_op jit(solution)/shard_map/broadcast_in_dim | solution.py:83
  36.9 6.6 %scatter_fusion = f32[192,16,450]{2,1,0:T(8,128)} fusion(f32[192,16,450]{2,1,0:T(8,128)} %broadcast_in_dim.61, s32[48]{0:T(128)S(1)} %fusion.24, f32[48,16,450]{2,1,0:T(8,128)S(1)} %fusion), kind=kCustom, calls=%fused_computation.4 | custom fusion | bytes 4147392 | tf_op jit(solution)/shard_map/scatter | solution.py:83
  43.6 85.6 %all_to_all.17 = f32[64,3,16,450]{3,2,1,0:T(8,128)} all-to-all(f32[64,3,16,450]{3,2,1,0:T(8,128)} %bitcast.59), channel_id=1, replica_groups=mesh['mp'=2,'tx'=8,'ty'=8] {'tx','ty'}, dimensions={0} | all-to-all | bytes 11059200 | tf_op jit(solution)/shard_map/all_to_all | solution.py:35
  129.2 2.7 collective-permute-start
  132.0 3.1 %collective-permute-start.1 = (f32[16,1,450]{2,1,0:T(1,128)S(1)}, f32[16,1,450]{2,1,0:T(1,128)}, u32[]{:S(2)}, u32[]{:S(2)}) collective-permute-start(f32[16,1,450]{2,1,0:T(1,128)S(1)} %get-tuple-element.13), channel_id=1, source_target_pairs={{0,8},{8,16},{16,24},{24,32},{32,40},{40,48},{48,56},{1,9},{9,17},... | collective-permute-start | bytes 86408 | tf_op jit(solution)/shard_map/ppermute | solution.py:20
  135.2 1.9 collective-permute-start.2
  138.7 6.7 %all-to-all-start = ((f32[64,1,3]{2,1,0:T(1,128)}), f32[64,1,3]{2,1,0:T(1,128)S(1)}, u32[]{:S(2)}, u32[]{:S(2)}) async-start(f32[64,1,3]{2,1,0:T(1,128)} %bitcast.15), calls=%async_computation | async-start | bytes 65536 | tf_op jit(solution)/shard_map/all_to_all | solution.py:36
  145.6 8.3 %all-to-all-done = f32[64,1,3]{2,1,0:T(1,128)S(1)} async-done(((f32[64,1,3]{2,1,0:T(1,128)}), f32[64,1,3]{2,1,0:T(1,128)S(1)}, u32[]{:S(2)}, u32[]{:S(2)}) %all-to-all-start) | async-done | bytes 800 | tf_op jit(solution)/shard_map/all_to_all | solution.py:36
  153.9 45.5 %all-gather = f32[16,1,3600]{0,1,2:T(1,128)} all-gather(f32[16,1,450]{0,1,2:T(1,128)S(1)} %copy.111), channel_id=2, replica_groups=mesh['mp'=2,'tx'=8,'ty'=8] {'ty'}, dimensions={2}, use_global_device_ids=true | all-gather | bytes 259200 | tf_op jit(solution)/shard_map/all_gather | solution.py:43
  199.6 2.7 gather_fusion.1
  202.9 9.7 %collective-permute-done.3 = f32[16,32,1]{2,1,0:T(8,128)} collective-permute-done((f32[16,32,1]{2,1,0:T(8,128)S(1)}, f32[16,32,1]{2,1,0:T(8,128)}, u32[]{:S(2)}, u32[]{:S(2)}) %collective-permute-start.3) | collective-permute-done | bytes 2080 | tf_op jit(solution)/shard_map/ppermute | solution.py:20
  212.6 1.7 fusion.13
  214.5 2.4 collective-permute-start.5
  216.9 4.4 %collective-permute-start.4 = (f32[16,1,450]{2,0,1:T(8,128)S(1)}, f32[16,1,450]{2,0,1:T(8,128)S(1)}, u32[]{:S(2)}, u32[]{:S(2)}) collective-permute-start(f32[16,1,450]{2,0,1:T(8,128)S(1)} %copy.123), channel_id=1, source_target_pairs={{8,0},{16,8},{24,16},{32,24},{40,32},{48,40},{56,48},{9,1},{17,9},... | collective-permute-start | bytes 86408 | tf_op jit(solution)/shard_map/ppermute | solution.py:23
  221.3 0.9 fusion.30
  222.2 44.3 %all-gather.1 = f32[16,1,3600]{0,1,2:T(1,128)} all-gather(f32[16,1,450]{0,1,2:T(1,128)S(1)} %copy.115), channel_id=3, replica_groups=mesh['mp'=2,'tx'=8,'ty'=8] {'ty'}, dimensions={2}, use_global_device_ids=true | all-gather | bytes 259200 | tf_op jit(solution)/shard_map/all_gather | solution.py:43
  266.5 1.2 slice.85
  267.6 2.7 gather_fusion.2
  270.4 1.5 collective-permute-start.6
  271.9 2.1 collective-permute-start.7
  274.2 20.1 %scatter_fusion.1 = f32[33,16,450]{2,1,0:T(8,128)S(1)} fusion(f32[33,16,450]{2,1,0:T(8,128)S(1)} %broadcast_in_dim.58, s32[192]{0:T(256)S(1)} %bitcast.67, f32[192,16,450]{2,1,0:T(8,128)} %bitcast.24), kind=kCustom, calls=%fused_computation.5 | custom fusion | flops 1382400 | bytes 16589568 | tf_op jit(solution)/shard_map/scatter-add | solution.py:95
  294.5 3.7 %fusion.7 = f32[1,16,32,450]{3,2,1,0:T(8,128)} fusion(f32[16,32,450]{2,1,0:T(8,128)S(1)} %fusion.13, f32[16,32,1]{2,1,0:T(8,128)} %collective-permute-done.7, f32[16,32,1]{2,1,0:T(8,128)} %collective-permute-done.6, f32[16,1,450]{2,1,0:T(1,128)S(1)} %collective-permute-done.5, f32[16,1,450]{2,1,0:T(1,128)S(1)} %broadcast_in_dim.57, ...), kind=kLoop, calls=%fused_computation.14 | loop fusion | flops 3225600 | bytes 4756096 | tf_op jit(solution)/shard_map/broadcast_in_dim | solution.py:106
  (61 shorter events, 7.8 us)
Async XLA Ops:
  43.6 85.6 %copy-start = (f32[1,16,32,450]{3,2,1,0:T(8,128)S(1)}, f32[1,16,32,450]{3,2,1,0:T(8,128)}, u32[]{:S(2)}) copy-start(f32[1,16,32,450]{3,2,1,0:T(8,128)} %param.11) | copy-start | bytes 2764804
  43.6 93.6 %copy-start.6 = (s32[1,1,48]{2,1,0:T(1,128)S(1)}, s32[1,1,48]{2,1,0:T(1,128)}, u32[]{:S(2)}) copy-start(s32[1,1,48]{2,1,0:T(1,128)} %param.18) | copy-start | bytes 580
  43.6 101.8 %copy-start.5 = (s32[450]{0:T(512)S(1)}, s32[450]{0:T(512)}, u32[]{:S(2)}) copy-start(s32[450]{0:T(512)} %param.15) | copy-start | bytes 5404
  43.6 101.8 %copy-start.2 = (s32[32,450]{1,0:T(8,128)S(1)}, s32[32,450]{1,0:T(8,128)}, u32[]{:S(2)}) copy-start(s32[32,450]{1,0:T(8,128)} %param.14) | copy-start | bytes 172804
  43.6 101.8 %copy-start.3 = (f32[1,32,450]{2,1,0:T(8,128)S(1)}, f32[1,32,450]{2,1,0:T(8,128)}, u32[]{:S(2)}) copy-start(f32[1,32,450]{2,1,0:T(8,128)} %param.12) | copy-start | bytes 172804
  43.6 101.8 %copy-start.4 = (f32[1,32,450]{2,1,0:T(8,128)S(1)}, f32[1,32,450]{2,1,0:T(8,128)}, u32[]{:S(2)}) copy-start(f32[1,32,450]{2,1,0:T(8,128)} %param.13) | copy-start | bytes 172804
  129.2 144.9 %collective-permute-start.9 = (f32[64,3,16,450]{3,2,1,0:T(8,128)}, f32[64,3,16,450]{3,2,1,0:T(8,128)}, u32[]{:S(2)}, u32[]{:S(2)}) collective-permute-start(f32[64,3,16,450]{3,2,1,0:T(8,128)} %all_to_all.17), channel_id=1, source_target_pairs={{0,64},{64,0},{1,65},{65,1},{2,66},{66,2},{3,67},{67,3},{4,68},{68... | collective-permute-start | bytes 16588808 | tf_op jit(solution)/shard_map/ppermute | solution.py:10
  129.2 73.6 %collective-permute-start = (f32[16,1,450]{2,0,1:T(8,128)S(1)}, f32[16,1,450]{2,0,1:T(8,128)S(1)}, u32[]{:S(2)}, u32[]{:S(2)}) collective-permute-start(f32[16,1,450]{2,0,1:T(8,128)S(1)} %copy.122), channel_id=1, source_target_pairs={{8,0},{16,8},{24,16},{32,24},{40,32},{48,40},{56,48},{9,1},{17,9},... | collective-permute-start | bytes 86408 | tf_op jit(solution)/shard_map/ppermute | solution.py:23
  132.0 80.7 %collective-permute-start.1 = (f32[16,1,450]{2,1,0:T(1,128)S(1)}, f32[16,1,450]{2,1,0:T(1,128)}, u32[]{:S(2)}, u32[]{:S(2)}) collective-permute-start(f32[16,1,450]{2,1,0:T(1,128)S(1)} %get-tuple-element.13), channel_id=1, source_target_pairs={{0,8},{8,16},{16,24},{24,32},{32,40},{40,48},{48,56},{1,9},{9,17},... | collective-permute-start | bytes 86408 | tf_op jit(solution)/shard_map/ppermute | solution.py:20
  135.2 67.7 %collective-permute-start.2 = (f32[16,32,1]{2,1,0:T(8,128)S(1)}, f32[16,32,1]{2,1,0:T(8,128)S(1)}, u32[]{:S(2)}, u32[]{:S(2)}) collective-permute-start(f32[16,32,1]{2,1,0:T(8,128)S(1)} %get-tuple-element.14), channel_id=1, source_target_pairs={{1,0},{2,1},{3,2},{4,3},{5,4},{6,5},{7,6},{0,7},{9,8},{10,9},{11,1... | collective-permute-start | bytes 6152 | tf_op jit(solution)/shard_map/ppermute | solution.py:23
  138.7 15.2 %all-to-all-start = ((f32[64,1,3]{2,1,0:T(1,128)}), f32[64,1,3]{2,1,0:T(1,128)S(1)}, u32[]{:S(2)}, u32[]{:S(2)}) async-start(f32[64,1,3]{2,1,0:T(1,128)} %bitcast.15), calls=%async_computation | async-start | bytes 65536 | tf_op jit(solution)/shard_map/all_to_all | solution.py:36
  153.9 48.5 %collective-permute-start.8 = (f32[64,3]{1,0:T(8,128)S(1)}, f32[64,3]{1,0:T(8,128)S(1)}, u32[]{:S(2)}, u32[]{:S(2)}) collective-permute-start(f32[64,3]{1,0:T(8,128)S(1)} %bitcast.66), channel_id=1, source_target_pairs={{0,64},{64,0},{1,65},{65,1},{2,66},{66,2},{3,67},{67,3},{4,68},{68... | collective-permute-start | bytes 2312 | tf_op jit(solution)/shard_map/ppermute | solution.py:10
  202.4 10.3 %collective-permute-start.3 = (f32[16,32,1]{2,1,0:T(8,128)S(1)}, f32[16,32,1]{2,1,0:T(8,128)}, u32[]{:S(2)}, u32[]{:S(2)}) collective-permute-start(f32[16,32,1]{2,1,0:T(8,128)S(1)} %get-tuple-element.15), channel_id=1, source_target_pairs={{0,1},{1,2},{2,3},{3,4},{4,5},{5,6},{6,7},{7,0},{8,9},{9,10},{10,1... | collective-permute-start | bytes 6152 | tf_op jit(solution)/shard_map/ppermute | solution.py:20
  202.9 9.7 %copy-start.1 = (f32[16,32,1]{2,1,0:T(8,128)}, f32[16,32,1]{2,1,0:T(8,128)S(1)}, u32[]{:S(2)}) copy-start(f32[16,32,1]{2,1,0:T(8,128)S(1)} %collective-permute-done.2) | copy-start | bytes 6148
  214.5 79.9 %collective-permute-start.5 = (f32[16,1,450]{2,1,0:T(1,128)S(1)}, f32[16,1,450]{2,1,0:T(1,128)S(1)}, u32[]{:S(2)}, u32[]{:S(2)}) collective-permute-start(f32[16,1,450]{2,1,0:T(1,128)S(1)} %get-tuple-element.9), channel_id=1, source_target_pairs={{0,8},{8,16},{16,24},{24,32},{32,40},{40,48},{48,56},{1,9},{9,17},... | collective-permute-start | bytes 86408 | tf_op jit(solution)/shard_map/ppermute | solution.py:20
  216.9 57.1 %collective-permute-start.4 = (f32[16,1,450]{2,0,1:T(8,128)S(1)}, f32[16,1,450]{2,0,1:T(8,128)S(1)}, u32[]{:S(2)}, u32[]{:S(2)}) collective-permute-start(f32[16,1,450]{2,0,1:T(8,128)S(1)} %copy.123), channel_id=1, source_target_pairs={{8,0},{16,8},{24,16},{32,24},{40,32},{48,40},{56,48},{9,1},{17,9},... | collective-permute-start | bytes 86408 | tf_op jit(solution)/shard_map/ppermute | solution.py:23
  270.4 24.0 %collective-permute-start.6 = (f32[16,32,1]{2,1,0:T(8,128)}, f32[16,32,1]{2,1,0:T(8,128)}, u32[]{:S(2)}, u32[]{:S(2)}) collective-permute-start(f32[16,32,1]{2,1,0:T(8,128)} %get-tuple-element.10), channel_id=1, source_target_pairs={{1,0},{2,1},{3,2},{4,3},{5,4},{6,5},{7,6},{0,7},{9,8},{10,9},{11,1... | collective-permute-start | bytes 6152 | tf_op jit(solution)/shard_map/ppermute | solution.py:23
  271.9 22.5 %collective-permute-start.7 = (f32[16,32,1]{2,1,0:T(8,128)}, f32[16,32,1]{2,1,0:T(8,128)}, u32[]{:S(2)}, u32[]{:S(2)}) collective-permute-start(f32[16,32,1]{2,1,0:T(8,128)} %get-tuple-element.11), channel_id=1, source_target_pairs={{0,1},{1,2},{2,3},{3,4},{4,5},{5,6},{6,7},{7,0},{8,9},{9,10},{10,1... | collective-permute-start | bytes 6152 | tf_op jit(solution)/shard_map/ppermute | solution.py:20
where the time goes:
time: 300 us; the launch traced here: 298 us
  blocking collectives  175 us (58%)
  other arithmetic  30.6 us (10%)
  matrix products  27.6 us (9%)
  starting transfers between devices  25.1 us (8%)
  local copies, waits for them, and re-layouts  21.2 us (7%)
  waiting for transfers between devices  18 us (6%)
    all_gather x2, blocking collectives, one_sweep(): whole_row = lax.all_gather(field[:, -1, :], 'ty', axis=1, tiled=True)  89.8 us
    all_to_all x1, blocking collectives, route_blocks(): lax.all_to_all(buffer, ('tx', 'ty'), split_axis=0, concat_axis=0, tiled=T...  85.6 us
    dot_general x1, matrix products, body(): jnp.einsum('eij,lej->eli', entry_weight[0, 0], picked, preferred_element_...  27.6 us
    scatter-add x1, other arithmetic, body(): summed = jax.ops.segment_sum(arrived, row_ids, num_segments=rows + 1)  20.1 us
    ppermute x4, starting transfers between devices, extended(): lax.ppermute(lax.slice_in_dim(block, 0, width, axis=dim), axis, backward)  10.5 us
    ppermute x4, waiting for transfers between devices, extended(): lax.ppermute(lax.slice_in_dim(block, block.shape[dim] - width, None, axis...  9.68 us
    all_to_all x1, waiting for transfers between devices, route_blocks(): lax.all_to_all(labels, ('tx', 'ty'), split_axis=0, concat_axis=0, tiled=T...  8.31 us
    ppermute x4, starting transfers between devices, extended(): lax.ppermute(lax.slice_in_dim(block, block.shape[dim] - width, None, axis...  7.93 us
  transfers between devices with their start and end apart: 11, of which 2 were waited for; matrix products, arithmetic and copies ran while one was open for 10% of the time, Pallas kernels for 0%

commit v1 on v0

v1 whole, which is shorter than its diff:
```python
import functools

import jax
import jax.numpy as jnp
from jax import lax
from jax.experimental import pallas as pl
from jax.experimental.pallas import tpu as pltpu
from jax.sharding import PartitionSpec as P

TILE_AXES = ("tx", "ty")
QUARTERS = 4
LANES = 128
GROUP = 4
PARTS = 1
ROW_BLOCK = 256
VMEM_LIMIT = 40 * 1024 * 1024


def spans(cols):
    width = -(-cols // QUARTERS)
    return [(q * width, min(cols, (q + 1) * width)) for q in range(QUARTERS)]


def contribute_kernel(first, count, source, tile, dest, sent, weight, out):
    rows, levels, cols = sent.shape
    step = pl.program_id(0)
    lane = lax.broadcasted_iota(jnp.int32, (levels, LANES), 1)
    for g in range(GROUP):
        local = step * GROUP + g
        entry = first + local
        y = lax.dot_general(
            sent[source[entry]], weight[g], (((1,), (1,)), ((), ())), preferred_element_type=jnp.float32
        )
        tile_value = tile[entry].astype(jnp.float32)
        dest_value = dest[entry].astype(jnp.float32)
        tail = jnp.where(lane == LANES - 2, tile_value, 0.0)
        tail = jnp.where(lane == LANES - 1, dest_value, tail)
        for q, (low, high) in enumerate(spans(cols)):
            piece = jnp.concatenate([y[:, low:high], tail[:, high - low :]], axis=1)
            out[pl.ds(q * count + local, levels, stride=QUARTERS * count), :] = piece


def contribute(first, count, sent, weight, source, tile, dest):
    rows, levels, cols = sent.shape
    grid_spec = pltpu.PrefetchScalarGridSpec(
        num_scalar_prefetch=3,
        grid=(count // GROUP,),
        in_specs=[
            pl.BlockSpec((rows, levels, cols), lambda i, *_: (0, 0, 0)),
            pl.BlockSpec((GROUP, cols, cols), lambda i, *_: (first // GROUP + i, 0, 0)),
        ],
        out_specs=pl.BlockSpec((levels * QUARTERS * count, LANES), lambda i, *_: (0, 0)),
    )
    return pl.pallas_call(
        functools.partial(contribute_kernel, first, count),
        grid_spec=grid_spec,
        out_shape=jax.ShapeDtypeStruct((levels * QUARTERS * count, LANES), jnp.float32),
        compiler_params=pltpu.CompilerParams(vmem_limit_bytes=VMEM_LIMIT),
        cost_estimate=pl.CostEstimate(
            flops=2 * count * levels * cols * cols, bytes_accessed=2 * count * cols * cols, transcendentals=0
        ),
        name="contribute",
    )(source, tile, dest, sent, weight)


def gather_rows_kernel(tile_rows, values, out, halves, labels):
    block = pl.program_id(0)

    @pl.when(block == 0)
    def prepare():
        x = values[...]
        high = x.astype(jnp.bfloat16)
        low = (x - high.astype(jnp.float32)).astype(jnp.bfloat16)
        halves[:, :LANES] = high
        halves[:, LANES:] = low
        lane = lax.broadcasted_iota(jnp.int32, (8, LANES), 1)
        pick = jnp.where(lane == LANES - 2, float(tile_rows), jnp.where(lane == LANES - 1, 1.0, 0.0))
        labels[...] = lax.dot_general(
            pick.astype(jnp.bfloat16), high, (((1,), (1,)), ((), ())), preferred_element_type=jnp.float32
        ).astype(jnp.int32)

    count = values.shape[0]
    row = lax.broadcasted_iota(jnp.int32, (ROW_BLOCK, count), 0) + block * ROW_BLOCK
    onehot = jnp.where(row == labels[0:1, :], 1.0, 0.0).astype(jnp.bfloat16)
    sums = jnp.dot(onehot, halves[...], preferred_element_type=jnp.float32)
    out[...] = sums[:, :LANES] + sums[:, LANES:]


def gather_rows(values, tiles, tile_rows):
    count = values.shape[0]
    return pl.pallas_call(
        functools.partial(gather_rows_kernel, tile_rows),
        grid=(tiles * tile_rows // ROW_BLOCK,),
        in_specs=[pl.BlockSpec((count, LANES), lambda i: (0, 0))],
        out_specs=pl.BlockSpec((ROW_BLOCK, LANES), lambda i: (i, 0)),
        out_shape=jax.ShapeDtypeStruct((tiles * tile_rows, LANES), jnp.float32),
        scratch_shapes=[
            pltpu.VMEM((count, 2 * LANES), jnp.bfloat16),
            pltpu.VMEM((8, count), jnp.int32),
        ],
        compiler_params=pltpu.CompilerParams(vmem_limit_bytes=VMEM_LIMIT),
        name="gather_rows",
    )(values)


def finish_kernel(received, field, moved, rate, out):
    levels, rows, cols = field.shape
    for level in range(levels):
        parts = [
            received[level * QUARTERS + q][:, : high - low] for q, (low, high) in enumerate(spans(cols))
        ]
        whole = jnp.concatenate(parts, axis=1)
        out[level] = moved[level] + rate[...] * (whole - field[level])


def finish(received, field, moved, rate):
    return pl.pallas_call(
        finish_kernel,
        out_shape=jax.ShapeDtypeStruct(field.shape, jnp.float32),
        compiler_params=pltpu.CompilerParams(vmem_limit_bytes=VMEM_LIMIT),
        name="finish",
    )(received, field, moved, rate)


def shift(value, axis, forward, periodic):
    count = lax.axis_size(axis)
    pairs = [(i, i + 1) for i in range(count - 1)] + ([(count - 1, 0)] if periodic else [])
    if not forward:
        pairs = [(b, a) for a, b in pairs]
    return lax.ppermute(value, axis, pairs)


def sweep(f, c):
    mid = f[:, 1:-1, 1:-1]
    around = f[:, 2:, 1:-1] + f[:, :-2, 1:-1] + f[:, 1:-1, 2:] + f[:, 1:-1, :-2]
    return mid + c * (around - 4.0 * mid)


def mix(field, coef, ocean, fold_map):
    levels, rows, cols = field.shape
    stack = jnp.concatenate([field, coef[None]], axis=0)
    west = shift(stack[:, :, cols - 2 :], "ty", True, True)
    east = shift(stack[:, :, :2], "ty", False, True)
    wide = jnp.concatenate([west, stack, east], axis=2)
    south = shift(wide[:, rows - 2 :], "tx", True, False)
    north = shift(wide[:, :2], "tx", False, False)
    last = jnp.broadcast_to(field[None, :, rows - 1], (lax.axis_size("ty"), levels, cols))
    whole = lax.all_to_all(last, "ty", split_axis=0, concat_axis=0, tiled=True)
    whole = jnp.transpose(whole, (1, 0, 2)).reshape(levels, -1)
    folded = jnp.take(whole, fold_map, axis=1)
    fold_here = jnp.logical_and(ocean, lax.axis_index("tx") == lax.axis_size("tx") - 1)
    folded = jnp.pad(folded, ((0, 1), (2, 2)))
    north = jnp.concatenate([jnp.where(fold_here, folded, north[:, 0])[:, None], north[:, 1:]], axis=1)
    ext = jnp.concatenate([south, wide, north], axis=1)
    once = sweep(ext[:levels], ext[levels, 1:-1, 1:-1])
    return sweep(once, jnp.where(ocean, 0.0, coef))


def body(
    state,
    diffusion,
    exchange_rate,
    land_mask,
    fold_map,
    entry_tile,
    entry_source,
    entry_dest,
    entry_weight,
):
    field = state[0]
    levels, rows, cols = field.shape
    tiles = lax.axis_size("tx") * lax.axis_size("ty")
    entries = entry_source.shape[2]
    ocean = lax.axis_index("mp") == 1
    active = jnp.where(ocean, land_mask.astype(jnp.float32), 1.0)
    moved = mix(field, diffusion[0] * active, ocean, fold_map)

    sent = jnp.transpose(field.astype(jnp.bfloat16), (1, 0, 2))
    source, tile, dest = entry_source[0, 0], entry_tile[0, 0, :, 0], entry_dest[0, 0]
    count = entries // PARTS
    arrived = []
    for part in range(PARTS):
        pieces = contribute(part * count, count, sent, entry_weight[0, 0], source, tile, dest)
        pieces = pieces.reshape(tiles, count, LANES)
        arrived.append(
            lax.all_to_all(pieces, TILE_AXES, split_axis=0, concat_axis=0, tiled=True).reshape(-1, LANES)
        )
    summed = gather_rows(jnp.concatenate(arrived, axis=0), tiles, rows).reshape(tiles, rows, LANES)
    received = lax.all_to_all(summed, TILE_AXES, split_axis=0, concat_axis=0, tiled=True)
    received = lax.ppermute(received, "mp", [(0, 1), (1, 0)])
    result = finish(received, field, moved, exchange_rate[0] * active)
    return result[None]


def solution(mesh):
    in_specs = (
        P("mp", None, "tx", "ty"),
        P("mp", "tx", "ty"),
        P("mp", "tx", "ty"),
        P("tx", "ty"),
        P("ty"),
        P("mp", "tx", "ty", None),
        P("mp", "tx", "ty"),
        P("mp", "tx", "ty"),
        P("mp", "tx", "ty", None, None),
    )
    out_specs = P("mp", None, "tx", "ty")
    return jax.shard_map(body, mesh=mesh, in_specs=in_specs, out_specs=out_specs, check_vma=False)
```

time: 300 us -> 129 us (0.43)
  the two profiles are of different devices: /device:TPU:8 before, /device:TPU:9 now
where the time goes in v1:
time: 129 us; the launch traced here: 128 us
  starting transfers between devices  35 us (27%)
  waiting for transfers between devices  33.2 us (26%)
  local copies, waits for them, and re-layouts  26.8 us (21%)
  Pallas kernels  21.6 us (17%)
  other arithmetic  11.3 us (9%)
    all_to_all x1, waiting for transfers between devices, body(): lax.all_to_all(pieces, TILE_AXES, split_axis=0, concat_axis=0, tiled=True)  22.2 us
    unnamed x30, local copies, waits for them, and re-layouts  18.9 us
    pallas_call x1, Pallas kernels, contribute(): pl.pallas_call(functools.partial(contribute_kernel, first, count), grid_s...  15.3 us
    all_to_all x1, starting transfers between devices, body(): lax.all_to_all(pieces, TILE_AXES, split_axis=0, concat_axis=0, tiled=True)  11 us
    ppermute x4, waiting for transfers between devices, shift(): return lax.ppermute(value, axis, pairs)  11 us
    ppermute x4, starting transfers between devices, shift(): return lax.ppermute(value, axis, pairs)  10.2 us
    all_to_all x1, starting transfers between devices, body(): lax.all_to_all(summed, TILE_AXES, split_axis=0, concat_axis=0, tiled=True)  9.08 us
    pallas_call x1, Pallas kernels, gather_rows(): pl.pallas_call(functools.partial(gather_rows_kernel, tile_rows), grid=(ti...  5.03 us
  transfers between devices with their start and end apart: 8, of which 2 were waited for; matrix products, arithmetic and copies ran while one was open for 13% of the time, Pallas kernels for 4%

profile of v1, /device:TPU:9, one launch (start us, length us, event | category | flops | bytes accessed | tf_op | source)
XLA Modules:
  0.0 128.2 jit_solution(13107403599664381637)
XLA Ops:
  0.0 1.3 %convert_bitcast_fusion = bf16[32,16,450]{2,0,1:T(8,128)(2,1)S(1)} fusion(f32[1,16,32,450]{3,2,1,0:T(8,128)} %param.9), kind=kLoop, calls=%fused_computation.24 | loop fusion | flops 230400 | bytes 1382400 | tf_op jit(solution)/shard_map/transpose | solution.py:178
  1.6 16.7 %copy.34 = bf16[1,1,48,450,450]{4,3,2,1,0:T(8,128)(2,1)} copy(bf16[1,1,48,450,450]{4,2,3,1,0:T(8,128)(2,1)} %param.17) | data formatting | bytes 38880000 | tf_op args[8]
  18.3 15.3 %contribute.1 = f32[3072,128]{1,0:T(8,128)S(1)} custom-call(s32[48]{0:T(128)S(1)} %bitcast.48, s32[48]{0:T(128)S(1)} %bitcast.49, s32[48]{0:T(128)S(1)} %bitcast.50, bf16[32,16,450]{2,1,0:T(8,128)(2,1)S(1)} %copy.23.sent, bf16[48,450,450]{2,1,0:T(8,128)(2,1)} %bitcast.51), custom_call_target="tpu_custom_call" | custom-call | flops 311040000 | bytes 19440000 | tf_op jit(solution)/shard_map/contribute/pallas_call | solution.py:54
  33.6 1.2 copy-done.1
  34.8 11.0 %all-to-all-start = ((f32[64,48,128]{2,1,0:T(8,128)}), f32[64,48,128]{2,1,0:T(8,128)S(1)}, u32[]{:S(2)}, u32[]{:S(2)}) async-start(f32[64,48,128]{2,1,0:T(8,128)} %bitcast.46), calls=%async_computation | async-start | bytes 3145728 | tf_op jit(solution)/shard_map/all_to_all | solution.py:186
  45.9 22.2 %all-to-all-done = f32[64,48,128]{2,1,0:T(8,128)S(1)} async-done(((f32[64,48,128]{2,1,0:T(8,128)}), f32[64,48,128]{2,1,0:T(8,128)S(1)}, u32[]{:S(2)}, u32[]{:S(2)}) %all-to-all-start) | async-done | bytes 1572896 | tf_op jit(solution)/shard_map/all_to_all | solution.py:186
  68.8 4.0 %all-to-all-start.2 = ((f32[8,16,450]{2,1,0:T(8,128)}), f32[8,16,450]{2,1,0:T(8,128)}, u32[]{:S(2)}, u32[]{:S(2)}) async-start(f32[8,16,450]{2,1,0:T(8,128)} %broadcast_in_dim.41), calls=%async_computation.2 | async-start | bytes 524288 | tf_op jit(solution)/shard_map/all_to_all | solution.py:148
  73.6 0.9 pad_maximum_fusion.11
  74.5 5.0 %collective-permute-start.2 = (f32[17,32,2]{2,1,0:T(8,128)}, f32[17,32,2]{2,1,0:T(8,128)S(1)}, u32[]{:S(2)}, u32[]{:S(2)}) collective-permute-start(f32[17,32,2]{2,1,0:T(8,128)} %get-tuple-element.8), channel_id=1, source_target_pairs={{1,0},{2,1},{3,2},{4,3},{5,4},{6,5},{7,6},{0,7},{9,8},{10,9},{11,1... | collective-permute-start | bytes 13064 | tf_op jit(solution)/shard_map/ppermute | solution.py:130
  79.5 5.0 %gather_rows.1 = f32[2048,128]{1,0:T(8,128)S(1)} custom-call(f32[3072,128]{1,0:T(8,128)S(1)} %bitcast.45), custom_call_target="tpu_custom_call" | custom-call | tf_op jit(solution)/shard_map/gather_rows/pallas_call | solution.py:91
  84.5 1.0 copy-done.2
  85.5 9.1 %all-to-all-start.1 = ((f32[64,32,128]{2,1,0:T(8,128)}), f32[64,32,128]{2,1,0:T(8,128)}, u32[]{:S(2)}, u32[]{:S(2)}) async-start(f32[64,32,128]{2,1,0:T(8,128)} %bitcast.47), calls=%async_computation.1 | async-start | bytes 2097152 | tf_op jit(solution)/shard_map/all_to_all | solution.py:189
  96.0 3.1 %collective-permute-start.4 = (f32[17,2,454]{2,1,0:T(2,128)S(1)}, f32[17,2,454]{2,1,0:T(2,128)S(1)}, u32[]{:S(2)}, u32[]{:S(2)}) collective-permute-start(f32[17,2,454]{2,1,0:T(2,128)S(1)} %get-tuple-element.6), channel_id=1, source_target_pairs={{8,0},{16,8},{24,16},{32,24},{40,32},{48,40},{56,48},{9,1},{17,9},... | collective-permute-start | bytes 185240 | tf_op jit(solution)/shard_map/ppermute | solution.py:130
  99.1 2.2 %collective-permute-start.3 = (f32[17,2,454]{2,1,0:T(2,128)}, f32[17,2,454]{2,1,0:T(2,128)}, u32[]{:S(2)}, u32[]{:S(2)}) collective-permute-start(f32[17,2,454]{2,1,0:T(2,128)} %get-tuple-element.5), channel_id=1, source_target_pairs={{0,8},{8,16},{16,24},{24,32},{32,40},{40,48},{48,56},{1,9},{9,17},... | collective-permute-start | bytes 185240 | tf_op jit(solution)/shard_map/ppermute | solution.py:130
  101.3 11.0 %collective-permute-done.4 = f32[17,2,454]{2,1,0:T(2,128)S(1)} collective-permute-done((f32[17,2,454]{2,1,0:T(2,128)S(1)}, f32[17,2,454]{2,1,0:T(2,128)S(1)}, u32[]{:S(2)}, u32[]{:S(2)}) %collective-permute-start.4) | collective-permute-done | bytes 61776 | tf_op jit(solution)/shard_map/ppermute | solution.py:130
  112.9 1.1 copy.24
  114.9 1.5 %copy.25 = f32[16,3600]{0,1:T(8,128)S(1)} copy(f32[16,3600]{1,0:T(8,128)} %reshape.22) | data formatting | bytes 460800 | tf_op jit(solution)/shard_map/reshape | solution.py:149
  116.4 1.6 %gather_fusion = f32[450,16]{1,0:T(8,128)} fusion(f32[16,3600]{0,1:T(8,128)S(1)} %copy.25, s32[1024]{0:T(1024)S(1)} %pad_clamp_fusion), kind=kCustom, calls=%fused_computation | custom fusion | bytes 59400 | tf_op jit(solution)/shard_map/jit(_take)/gather | solution.py:150
  118.0 1.1 copy.26
  120.5 1.0 maximum_bitcast_fusion
  121.5 1.4 %pad_maximum_fusion = f32[17,35,454]{2,1,0:T(8,128)S(1)} fusion(f32[17,1,454]{2,1,0:T(1,128)S(1)} %copy.27, f32[17,32,2]{2,1,0:T(8,128)S(1)} %collective-permute-done.2, f32[1,32,450]{2,1,0:T(8,128)S(1)} %copy-done.7, f32[16,32,450]{2,1,0:T(8,128)S(1)} %bitcast.42, f32[17,32,2]{2,1,0:T(8,128)S(1)} %collective-permute-done.1, ...), kind=kLoop, calls=%fused_computation.2 | loop fusion | flops 1350650 | bytes 2161040 | tf_op jit(solution)/shard_map/concatenate | solution.py:154
  122.9 2.8 %fusion.2 = f32[16,34,452]{2,1,0:T(8,128)S(1)} fusion(f32[17,35,454]{2,1,0:T(8,128)S(1)} %pad_maximum_fusion, f32[17,2,454]{2,1,0:T(2,128)} %collective-permute-done.3, f32[17,32,2]{2,1,0:T(8,128)S(1)} %collective-permute-done.2, f32[17,32,2]{2,1,0:T(8,128)S(1)} %collective-permute-done.1, f32[1,32,450]{2,1,0:T(8,128)S(1)} %copy-done.7, ...), kind=kLoop, calls=%fused_computation.6 | loop fusion | flops 3934208 | bytes 5107072 | tf_op jit(solution)/shard_map/add | solution.py:136
  125.7 1.2 fusion.6.moved
  126.9 1.2 finish.1
  (48 shorter events, 6.1 us)
Async XLA Ops:
  1.6 16.7 %copy-start.3 = (s32[1,1,48]{2,1,0:T(1,128)S(1)}, s32[1,1,48]{2,1,0:T(1,128)}, u32[]{:S(2)}) copy-start(s32[1,1,48]{2,1,0:T(1,128)} %param.15) | copy-start | bytes 580
  1.6 16.7 %copy-start.4 = (s32[1,1,48,1]{2,3,1,0:T(1,128)S(1)}, s32[1,1,48,1]{2,3,1,0:T(1,128)}, u32[]{:S(2)}) copy-start(s32[1,1,48,1]{2,3,1,0:T(1,128)} %param.14) | copy-start | bytes 580
  1.6 16.7 %copy-start.5 = (s32[1,1,48]{2,1,0:T(1,128)S(1)}, s32[1,1,48]{2,1,0:T(1,128)}, u32[]{:S(2)}) copy-start(s32[1,1,48]{2,1,0:T(1,128)} %param.16) | copy-start | bytes 580
  33.6 1.2 copy-start.1
  34.8 11.0 %copy-start = (f32[1,16,32,450]{3,2,1,0:T(8,128)S(1)}, f32[1,16,32,450]{3,2,1,0:T(8,128)}, u32[]{:S(2)}) copy-start(f32[1,16,32,450]{3,2,1,0:T(8,128)} %param.9) | copy-start | bytes 2764804
  34.8 38.1 %copy-start.10 = (s32[32,450]{1,0:T(8,128)S(1)}, s32[32,450]{1,0:T(8,128)}, u32[]{:S(2)}) copy-start(s32[32,450]{1,0:T(8,128)} %param.12) | copy-start | bytes 172804
  34.8 38.1 %copy-start.11 = (f32[1,32,450]{2,1,0:T(8,128)S(1)}, f32[1,32,450]{2,1,0:T(8,128)}, u32[]{:S(2)}) copy-start(f32[1,32,450]{2,1,0:T(8,128)} %param.10) | copy-start | bytes 172804
  34.8 38.1 %copy-start.12 = (f32[1,32,450]{2,1,0:T(8,128)S(1)}, f32[1,32,450]{2,1,0:T(8,128)}, u32[]{:S(2)}) copy-start(f32[1,32,450]{2,1,0:T(8,128)} %param.11) | copy-start | bytes 172804
  34.8 33.3 %all-to-all-start = ((f32[64,48,128]{2,1,0:T(8,128)}), f32[64,48,128]{2,1,0:T(8,128)S(1)}, u32[]{:S(2)}, u32[]{:S(2)}) async-start(f32[64,48,128]{2,1,0:T(8,128)} %bitcast.46), calls=%async_computation | async-start | bytes 3145728 | tf_op jit(solution)/shard_map/all_to_all | solution.py:186
  68.8 16.6 %all-to-all-start.2 = ((f32[8,16,450]{2,1,0:T(8,128)}), f32[8,16,450]{2,1,0:T(8,128)}, u32[]{:S(2)}, u32[]{:S(2)}) async-start(f32[8,16,450]{2,1,0:T(8,128)} %broadcast_in_dim.41), calls=%async_computation.2 | async-start | bytes 524288 | tf_op jit(solution)/shard_map/all_to_all | solution.py:148
  73.6 21.6 %copy-start.6 = (f32[1,32,450]{2,1,0:T(8,128)}, f32[1,32,450]{2,1,0:T(8,128)S(1)}, u32[]{:S(2)}) copy-start(f32[1,32,450]{2,1,0:T(8,128)S(1)} %get-tuple-element.10) | copy-start | bytes 172804
  74.5 20.6 %collective-permute-start.2 = (f32[17,32,2]{2,1,0:T(8,128)}, f32[17,32,2]{2,1,0:T(8,128)S(1)}, u32[]{:S(2)}, u32[]{:S(2)}) collective-permute-start(f32[17,32,2]{2,1,0:T(8,128)} %get-tuple-element.8), channel_id=1, source_target_pairs={{1,0},{2,1},{3,2},{4,3},{5,4},{6,5},{7,6},{0,7},{9,8},{10,9},{11,1... | collective-permute-start | bytes 13064 | tf_op jit(solution)/shard_map/ppermute | solution.py:130
  79.5 15.7 %collective-permute-start.1 = (f32[17,32,2]{2,1,0:T(8,128)}, f32[17,32,2]{2,1,0:T(8,128)S(1)}, u32[]{:S(2)}, u32[]{:S(2)}) collective-permute-start(f32[17,32,2]{2,1,0:T(8,128)} %get-tuple-element.7), channel_id=1, source_target_pairs={{0,1},{1,2},{2,3},{3,4},{4,5},{5,6},{6,7},{7,0},{8,9},{9,10},{10,1... | collective-permute-start | bytes 13064 | tf_op jit(solution)/shard_map/ppermute | solution.py:130
  84.5 1.0 copy-start.2
  85.5 9.1 %copy-start.13 = (s32[450]{0:T(512)S(1)}, s32[450]{0:T(512)}, u32[]{:S(2)}) copy-start(s32[450]{0:T(512)} %param.13) | copy-start | bytes 5404
  85.5 34.2 %all-to-all-start.1 = ((f32[64,32,128]{2,1,0:T(8,128)}), f32[64,32,128]{2,1,0:T(8,128)}, u32[]{:S(2)}, u32[]{:S(2)}) async-start(f32[64,32,128]{2,1,0:T(8,128)} %bitcast.47), calls=%async_computation.1 | async-start | bytes 2097152 | tf_op jit(solution)/shard_map/all_to_all | solution.py:189
  96.0 16.3 %collective-permute-start.4 = (f32[17,2,454]{2,1,0:T(2,128)S(1)}, f32[17,2,454]{2,1,0:T(2,128)S(1)}, u32[]{:S(2)}, u32[]{:S(2)}) collective-permute-start(f32[17,2,454]{2,1,0:T(2,128)S(1)} %get-tuple-element.6), channel_id=1, source_target_pairs={{8,0},{16,8},{24,16},{32,24},{40,32},{48,40},{56,48},{9,1},{17,9},... | collective-permute-start | bytes 185240 | tf_op jit(solution)/shard_map/ppermute | solution.py:130
  99.1 21.4 %collective-permute-start.3 = (f32[17,2,454]{2,1,0:T(2,128)}, f32[17,2,454]{2,1,0:T(2,128)}, u32[]{:S(2)}, u32[]{:S(2)}) collective-permute-start(f32[17,2,454]{2,1,0:T(2,128)} %get-tuple-element.5), channel_id=1, source_target_pairs={{0,8},{8,16},{16,24},{24,32},{32,40},{40,48},{48,56},{1,9},{9,17},... | collective-permute-start | bytes 185240 | tf_op jit(solution)/shard_map/ppermute | solution.py:130
  118.0 3.4 %copy-start.7 = (f32[1,32,450]{2,1,0:T(8,128)S(1)}, f32[1,32,450]{2,1,0:T(8,128)}, u32[]{:S(2)}) copy-start(f32[1,32,450]{2,1,0:T(8,128)} %copy-done.6) | copy-start | bytes 172804
  119.7 7.2 %collective-permute-start = (f32[64,32,128]{2,1,0:T(8,128)}, f32[64,32,128]{2,1,0:T(8,128)S(1)}, u32[]{:S(2)}, u32[]{:S(2)}) collective-permute-start(f32[64,32,128]{2,1,0:T(8,128)} %all-to-all-done.1), channel_id=1, source_target_pairs={{0,64},{64,0},{1,65},{65,1},{2,66},{66,2},{3,67},{67,3},{4,68},{68... | collective-permute-start | bytes 3145736 | tf_op jit(solution)/shard_map/ppermute | solution.py:190
  121.4 1.5 %copy-start.9 = (f32[17,1,454]{2,1,0:T(1,128)S(1)}, f32[17,1,454]{2,1,0:T(1,128)}, u32[]{:S(2)}) copy-start(f32[17,1,454]{2,1,0:T(1,128)} %get-tuple-element.11) | copy-start | bytes 92620
  122.9 2.8 %copy-start.8 = (f32[32,450]{1,0:T(8,128)S(1)}, f32[32,450]{1,0:T(8,128)}, u32[]{:S(2)}) copy-start(f32[32,450]{1,0:T(8,128)} %get-tuple-element.9) | copy-start | bytes 172804

commit v2 on v1

--- a/solution.py
+++ b/solution.py
@@ -10,57 +10,113 @@
 TILE_AXES = ("tx", "ty")
 QUARTERS = 4
 LANES = 128
-GROUP = 4
-PARTS = 1
+PACK = 16
+WIDTH = 120
+BLOCK = 40
 ROW_BLOCK = 256
 VMEM_LIMIT = 40 * 1024 * 1024
 
 
 def spans(cols):
-    width = -(-cols // QUARTERS)
-    return [(q * width, min(cols, (q + 1) * width)) for q in range(QUARTERS)]
-
-
-def contribute_kernel(first, count, source, tile, dest, sent, weight, out):
-    rows, levels, cols = sent.shape
+    return [(q * WIDTH, min(cols, (q + 1) * WIDTH)) for q in range(QUARTERS)]
+
+
+def contribute_kernel(cols, source, tile, dest, state, weight, out, loose, picks, product, turned):
+    levels, rows, _ = state.shape
+    entries = weight.shape[1]
     step = pl.program_id(0)
-    lane = lax.broadcasted_iota(jnp.int32, (levels, LANES), 1)
-    for g in range(GROUP):
-        local = step * GROUP + g
-        entry = first + local
-        y = lax.dot_general(
-            sent[source[entry]], weight[g], (((1,), (1,)), ((), ())), preferred_element_type=jnp.float32
-        )
-        tile_value = tile[entry].astype(jnp.float32)
-        dest_value = dest[entry].astype(jnp.float32)
-        tail = jnp.where(lane == LANES - 2, tile_value, 0.0)
-        tail = jnp.where(lane == LANES - 1, dest_value, tail)
-        for q, (low, high) in enumerate(spans(cols)):
-            piece = jnp.concatenate([y[:, low:high], tail[:, high - low :]], axis=1)
-            out[pl.ds(q * count + local, levels, stride=QUARTERS * count), :] = piece
-
-
-def contribute(first, count, sent, weight, source, tile, dest):
-    rows, levels, cols = sent.shape
+    steps = WIDTH // BLOCK
+    groups = entries // PACK
+    lane = lax.broadcasted_iota(jnp.int32, (1, LANES), 1)
+
+    @pl.when(step == 0)
+    def prepare():
+        place = lax.broadcasted_iota(jnp.int32, (entries, rows), 0)
+        wanted = jnp.zeros((entries, rows), jnp.int32)
+        for entry in range(entries):
+            wanted = jnp.where(place == entry, source[entry], wanted)
+        onehot = jnp.where(wanted == lax.broadcasted_iota(jnp.int32, (entries, rows), 1), 1.0, 0.0)
+        onehot = onehot.astype(jnp.bfloat16)
+        for level in range(levels):
+            picked = jnp.dot(
+                onehot, state[level].astype(jnp.bfloat16), preferred_element_type=jnp.float32
+            )
+            for half in range(2 * groups):
+                loose[half, level * 8 : level * 8 + 8, :] = picked[half * 8 : half * 8 + 8]
+        for group in range(groups):
+            for half in range(2):
+                picks[group, half * LANES : (half + 1) * LANES, :] = loose[2 * group + half].astype(
+                    jnp.bfloat16
+                )
+        below = lax.broadcasted_iota(jnp.int32, (8, LANES), 0)
+        for half in range(2 * groups):
+            tiles = jnp.zeros((8, LANES), jnp.int32)
+            dests = jnp.zeros((8, LANES), jnp.int32)
+            for e in range(8):
+                here = lax.broadcasted_iota(jnp.int32, (8, LANES), 1) % 8 == e
+                tiles = jnp.where(here, tile[half * 8 + e], tiles)
+                dests = jnp.where(here, dest[half * 8 + e], dests)
+            tail = jnp.where(below == 6, tiles, jnp.where(below == 7, dests, 0))
+            turned[WIDTH:LANES, half * LANES : (half + 1) * LANES] = tail.astype(jnp.float32)
+
+    base = pl.multiple_of((step % steps) * BLOCK, 8)
+    column = lax.broadcasted_iota(jnp.int32, (BLOCK, LANES), 0) + step * BLOCK
+    for group in range(groups):
+        streamed = weight[:, group * PACK : (group + 1) * PACK, :].reshape(BLOCK * PACK, cols)
+        whole = lax.dot_general(
+            streamed, picks[group], (((1,), (1,)), ((), ())), preferred_element_type=jnp.float32
+        ).reshape(BLOCK, PACK, 2 * LANES)
+        for half in range(2):
+            slot = 2 * group + half
+            own = whole[:, half * 8 : half * 8 + 8, half * LANES : (half + 1) * LANES]
+            product[slot] = own.reshape(BLOCK * 8, LANES)
+            y = jnp.zeros((BLOCK, LANES), jnp.float32)
+            for e in range(8):
+                y = jnp.where(lane % 8 == e, product[slot, pl.ds(e, BLOCK, stride=8), :], y)
+            y = jnp.where(column < cols, y, 0.0)
+            turned[pl.ds(base, BLOCK), slot * LANES : (slot + 1) * LANES] = y
+
+    @pl.when(step % steps == steps - 1)
+    def turn():
+        quarter = step // steps
+        for slot in range(2 * groups):
+            block = turned[:, slot * LANES : (slot + 1) * LANES].T
+            for level in range(levels):
+                start = pl.multiple_of((level * QUARTERS + quarter) * entries + slot * 8, 8)
+                out[pl.ds(start, 8), :] = block[level * 8 : level * 8 + 8]
+
+
+def contribute(state, weight, source, tile, dest):
+    levels, rows, cols = state.shape
+    entries = weight.shape[1]
+    groups = entries // PACK
     grid_spec = pltpu.PrefetchScalarGridSpec(
         num_scalar_prefetch=3,
-        grid=(count // GROUP,),
+        grid=(QUARTERS * WIDTH // BLOCK,),
         in_specs=[
-            pl.BlockSpec((rows, levels, cols), lambda i, *_: (0, 0, 0)),
-            pl.BlockSpec((GROUP, cols, cols), lambda i, *_: (first // GROUP + i, 0, 0)),
+            pl.BlockSpec((levels, rows, cols), lambda i, *_: (0, 0, 0)),
+            pl.BlockSpec((BLOCK, entries, cols), lambda i, *_: (i, 0, 0)),
         ],
-        out_specs=pl.BlockSpec((levels * QUARTERS * count, LANES), lambda i, *_: (0, 0)),
+        out_specs=pl.BlockSpec((levels * QUARTERS * entries, LANES), lambda i, *_: (0, 0)),
+        scratch_shapes=[
+            pltpu.VMEM((2 * groups, LANES, cols), jnp.float32),
+            pltpu.VMEM((groups, 2 * LANES, cols), jnp.bfloat16),
+            pltpu.VMEM((2 * groups, BLOCK * 8, LANES), jnp.float32),
+            pltpu.VMEM((LANES, 2 * groups * LANES), jnp.float32),
+        ],
     )
     return pl.pallas_call(
-        functools.partial(contribute_kernel, first, count),
+        functools.partial(contribute_kernel, cols),
         grid_spec=grid_spec,
-        out_shape=jax.ShapeDtypeStruct((levels * QUARTERS * count, LANES), jnp.float32),
+        out_shape=jax.ShapeDtypeStruct((levels * QUARTERS * entries, LANES), jnp.float32),
         compiler_params=pltpu.CompilerParams(vmem_limit_bytes=VMEM_LIMIT),
         cost_estimate=pl.CostEstimate(
-            flops=2 * count * levels * cols * cols, bytes_accessed=2 * count * cols * cols, transcendentals=0
+            flops=2 * entries * levels * cols * cols,
+            bytes_accessed=2 * entries * cols * cols,
+            transcendentals=0,
         ),
         name="contribute",
-    )(source, tile, dest, sent, weight)
+    )(source, tile, dest, state, weight)
 
 
 def gather_rows_kernel(tile_rows, values, out, halves, labels):
@@ -175,17 +231,12 @@
     active = jnp.where(ocean, land_mask.astype(jnp.float32), 1.0)
     moved = mix(field, diffusion[0] * active, ocean, fold_map)
 
-    sent = jnp.transpose(field.astype(jnp.bfloat16), (1, 0, 2))
     source, tile, dest = entry_source[0, 0], entry_tile[0, 0, :, 0], entry_dest[0, 0]
-    count = entries // PARTS
-    arrived = []
-    for part in range(PARTS):
-        pieces = contribute(part * count, count, sent, entry_weight[0, 0], source, tile, dest)
-        pieces = pieces.reshape(tiles, count, LANES)
-        arrived.append(
-            lax.all_to_all(pieces, TILE_AXES, split_axis=0, concat_axis=0, tiled=True).reshape(-1, LANES)
-        )
-    summed = gather_rows(jnp.concatenate(arrived, axis=0), tiles, rows).reshape(tiles, rows, LANES)
+    weight = jnp.transpose(entry_weight[0, 0], (1, 0, 2))
+    pieces = contribute(field, weight, source, tile, dest).reshape(tiles, entries, LANES)
+    arrived = lax.all_to_all(pieces, TILE_AXES, split_axis=0, concat_axis=0, tiled=True)
+    arrived, moved = lax.optimization_barrier((arrived, moved))
+    summed = gather_rows(arrived.reshape(-1, LANES), tiles, rows).reshape(tiles, rows, LANES)
     received = lax.all_to_all(summed, TILE_AXES, split_axis=0, concat_axis=0, tiled=True)
     received = lax.ppermute(received, "mp", [(0, 1), (1, 0)])
     result = finish(received, field, moved, exchange_rate[0] * active)

time: 129 us -> 114 us (0.88)
  the two profiles are of different devices: /device:TPU:9 before, /device:TPU:1 now
where the time goes in v2:
time: 114 us; the launch traced here: 113 us
  starting transfers between devices  29.2 us (26%)
  Pallas kernels  22.6 us (20%)
  blocking collectives  21.5 us (19%)
  waiting for transfers between devices  15.5 us (14%)
  other arithmetic  12.4 us (11%)
  local copies, waits for them, and re-layouts  11.5 us (10%)
    all_to_all x1, blocking collectives, body(): lax.all_to_all(summed, TILE_AXES, split_axis=0, concat_axis=0, tiled=True)  21.5 us
    pallas_call x1, Pallas kernels, contribute(): pl.pallas_call(functools.partial(contribute_kernel, cols), grid_spec=grid...  16.3 us
    ppermute x4, starting transfers between devices, shift(): return lax.ppermute(value, axis, pairs)  12.6 us
    ppermute x4, waiting for transfers between devices, shift(): return lax.ppermute(value, axis, pairs)  9.84 us
    all_to_all x1, starting transfers between devices, body(): lax.all_to_all(pieces, TILE_AXES, split_axis=0, concat_axis=0, tiled=True)  7.55 us
    pallas_call x1, Pallas kernels, gather_rows(): pl.pallas_call(functools.partial(gather_rows_kernel, tile_rows), grid=(ti...  5.02 us
    add x2, other arithmetic, sweep(): return mid + c * (around - 4.0 * mid)  4.94 us
    ppermute x1, starting transfers between devices, body(): received = lax.ppermute(received, 'mp', [(0, 1), (1, 0)])  4.56 us
  transfers between devices with their start and end apart: 7, of which 4 were waited for; matrix products, arithmetic and copies ran while one was open for 17% of the time, Pallas kernels for 14%

profile of v2, /device:TPU:1, one launch (start us, length us, event | category | flops | bytes accessed | tf_op | source)
XLA Modules:
  0.0 113.0 jit_solution(16452928047885898275)
XLA Ops:
  0.0 1.6 %broadcast_select_fusion = (f32[32,450]{1,0:T(8,128)}, f32[1,32,450]{2,1,0:T(8,128)S(1)}, f32[32,450]{1,0:T(8,128)S(1)}) fusion(pred[]{:T(512)S(6)} %eq.6, s32[32,450]{1,0:T(8,128)} %param.12, f32[1,32,450]{2,1,0:T(8,128)} %param.10, f32[1,32,450]{2,1,0:T(8,128)} %param.11), kind=kLoop, calls=%fused_computation.37 | loop fusion | flops 72000 | bytes 345601 | tf_op jit(solution)/shard_map/jit(_where)/select_n | solution.py:212
  1.6 1.2 %pad_maximum_fusion.11 = (f32[17,32,2]{2,1,0:T(8,128)S(1)}, f32[17,32,2]{2,1,0:T(8,128)S(1)}) fusion(f32[1,32,450]{2,1,0:T(8,128)S(1)} %get-tuple-element.14, f32[16,32,450]{2,1,0:T(8,128)} %bitcast.35), kind=kLoop, calls=%fused_computation.24 | loop fusion | flops 2176 | bytes 987904 | tf_op jit(solution)/shard_map/slice | solution.py:198
  2.8 4.5 %collective-permute-start = (f32[17,32,2]{2,1,0:T(8,128)S(1)}, f32[17,32,2]{2,1,0:T(8,128)S(1)}, u32[]{:S(2)}, u32[]{:S(2)}) collective-permute-start(f32[17,32,2]{2,1,0:T(8,128)S(1)} %get-tuple-element.11), channel_id=1, source_target_pairs={{0,1},{1,2},{2,3},{3,4},{4,5},{5,6},{6,7},{7,0},{8,9},{9,10},{10,1... | collective-permute-start | bytes 13064 | tf_op jit(solution)/shard_map/ppermute | solution.py:186
  7.3 2.3 %collective-permute-start.1 = (f32[17,32,2]{2,1,0:T(8,128)S(1)}, f32[17,32,2]{2,1,0:T(8,128)S(1)}, u32[]{:S(2)}, u32[]{:S(2)}) collective-permute-start(f32[17,32,2]{2,1,0:T(8,128)S(1)} %get-tuple-element.12), channel_id=1, source_target_pairs={{1,0},{2,1},{3,2},{4,3},{5,4},{6,5},{7,6},{0,7},{9,8},{10,9},{11,1... | collective-permute-start | bytes 13064 | tf_op jit(solution)/shard_map/ppermute | solution.py:186
  10.4 4.4 %all-to-all-start.1 = ((f32[8,16,450]{2,1,0:T(8,128)}), f32[8,16,450]{2,1,0:T(8,128)S(1)}, u32[]{:S(2)}, u32[]{:S(2)}) async-start(f32[8,16,450]{2,1,0:T(8,128)} %broadcast_in_dim.41), calls=%async_computation.1 | async-start | bytes 524288 | tf_op jit(solution)/shard_map/all_to_all | solution.py:204
  14.9 5.0 %collective-permute-done = f32[17,32,2]{2,1,0:T(8,128)S(1)} collective-permute-done((f32[17,32,2]{2,1,0:T(8,128)S(1)}, f32[17,32,2]{2,1,0:T(8,128)S(1)}, u32[]{:S(2)}, u32[]{:S(2)}) %collective-permute-start) | collective-permute-done | bytes 4384 | tf_op jit(solution)/shard_map/ppermute | solution.py:186
  19.9 4.8 %collective-permute-done.1 = f32[17,32,2]{2,1,0:T(8,128)S(1)} collective-permute-done((f32[17,32,2]{2,1,0:T(8,128)S(1)}, f32[17,32,2]{2,1,0:T(8,128)S(1)}, u32[]{:S(2)}, u32[]{:S(2)}) %collective-permute-start.1) | collective-permute-done | bytes 4384 | tf_op jit(solution)/shard_map/ppermute | solution.py:186
  25.6 1.3 %collective-permute-start.3 = (f32[17,2,454]{2,1,0:T(2,128)S(1)}, f32[17,2,454]{2,1,0:T(2,128)S(1)}, u32[]{:S(2)}, u32[]{:S(2)}) collective-permute-start(f32[17,2,454]{2,1,0:T(2,128)S(1)} %get-tuple-element.10), channel_id=1, source_target_pairs={{8,0},{16,8},{24,16},{32,24},{40,32},{48,40},{56,48},{9,1},{17,9},... | collective-permute-start | bytes 185240 | tf_op jit(solution)/shard_map/ppermute | solution.py:186
  26.9 16.3 %contribute.1 = f32[3072,128]{1,0:T(8,128)S(1)} custom-call(s32[48]{0:T(128)S(1)} %bitcast.46, s32[48]{0:T(128)S(1)} %bitcast.47, s32[48]{0:T(128)S(1)} %bitcast.48, f32[16,32,450]{2,1,0:T(8,128)S(1)} %bitcast.38, bf16[450,48,450]{2,1,0:T(8,128)(2,1)} %bitcast.49), custom_call_target="tpu_custom_call" | custom-call | flops 311040000 | bytes 19440000 | tf_op jit(solution)/shard_map/contribute/pallas_call | solution.py:108
  43.2 1.1 %copy-done.1 = f32[3072,128]{1,0:T(8,128)} copy-done((f32[3072,128]{1,0:T(8,128)}, f32[3072,128]{1,0:T(8,128)S(1)}, u32[]{:S(2)}) %copy-start.1) | copy-done | bytes 1572888
  44.4 4.6 %collective-permute-start.2 = (f32[17,2,454]{2,1,0:T(2,128)}, f32[17,2,454]{2,1,0:T(2,128)}, u32[]{:S(2)}, u32[]{:S(2)}) collective-permute-start(f32[17,2,454]{2,1,0:T(2,128)} %get-tuple-element.9), channel_id=1, source_target_pairs={{0,8},{8,16},{16,24},{24,32},{32,40},{40,48},{48,56},{1,9},{9,17},... | collective-permute-start | bytes 185240 | tf_op jit(solution)/shard_map/ppermute | solution.py:186
  49.7 7.6 %all-to-all-start = ((f32[64,48,128]{2,1,0:T(8,128)}), f32[64,48,128]{2,1,0:T(8,128)S(1)}, u32[]{:S(2)}, u32[]{:S(2)}) async-start(f32[64,48,128]{2,1,0:T(8,128)} %bitcast.44), calls=%async_computation | async-start | bytes 3145728 | tf_op jit(solution)/shard_map/all_to_all | solution.py:237
  57.9 1.8 %copy.18 = f32[16,8,450]{2,1,0:T(8,128)} copy(f32[16,8,450]{2,0,1:T(8,128)} %bitcast.50) | data formatting | bytes 460800 | tf_op jit(solution)/shard_map/transpose | solution.py:205
  60.9 1.8 %copy.19 = f32[16,3600]{0,1:T(8,128)} copy(f32[16,3600]{1,0:T(8,128)S(1)} %reshape.20) | data formatting | bytes 460800 | tf_op jit(solution)/shard_map/reshape | solution.py:205
  62.7 2.7 %gather_fusion = f32[450,16]{1,0:T(8,128)S(1)} fusion(f32[16,3600]{0,1:T(8,128)} %copy.19, s32[1024]{0:T(1024)S(1)} %pad_clamp_fusion), kind=kCustom, calls=%fused_computation | custom fusion | bytes 59400 | tf_op jit(solution)/shard_map/jit(_take)/gather | solution.py:206
  68.5 1.4 %pad_maximum_fusion = f32[17,35,454]{2,1,0:T(8,128)S(1)} fusion(f32[17,1,454]{2,1,0:T(1,128)S(1)} %copy.21, f32[17,32,2]{2,1,0:T(8,128)S(1)} %collective-permute-done.1, f32[1,32,450]{2,1,0:T(8,128)S(1)} %get-tuple-element.14, f32[16,32,450]{2,1,0:T(8,128)S(1)} %bitcast.40, f32[17,32,2]{2,1,0:T(8,128)S(1)} %collective-permute-done, ...), kind=kLoop, calls=%fused_computation.1 | loop fusion | flops 1350650 | bytes 2161040 | tf_op jit(solution)/shard_map/concatenate | solution.py:210
  70.0 2.8 %fusion.2 = f32[16,34,452]{2,1,0:T(8,128)S(1)} fusion(f32[17,35,454]{2,1,0:T(8,128)S(1)} %pad_maximum_fusion, f32[17,2,454]{2,1,0:T(2,128)} %collective-permute-done.2, f32[17,32,2]{2,1,0:T(8,128)S(1)} %collective-permute-done.1, f32[17,32,2]{2,1,0:T(8,128)S(1)} %collective-permute-done, f32[1,32,450]{2,1,0:T(8,128)S(1)} %get-tuple-element.14, ...), kind=kLoop, calls=%fused_computation.5 | loop fusion | flops 3934208 | bytes 5107072 | tf_op jit(solution)/shard_map/add | solution.py:192
  72.8 2.1 %fusion.6.moved = f32[16,32,450]{2,1,0:T(8,128)} fusion(f32[16,34,452]{2,1,0:T(8,128)S(1)} %fusion.2, f32[32,450]{1,0:T(8,128)S(1)} %copy-done.7), kind=kLoop, calls=%fused_computation.20 | loop fusion | flops 1612800 | bytes 5587200 | tf_op jit(solution)/shard_map/add | solution.py:192
  75.0 3.3 %all-to-all-done = f32[64,48,128]{2,1,0:T(8,128)S(1)} async-done(((f32[64,48,128]{2,1,0:T(8,128)}), f32[64,48,128]{2,1,0:T(8,128)S(1)}, u32[]{:S(2)}, u32[]{:S(2)}) %all-to-all-start) | async-done | bytes 1572896 | tf_op jit(solution)/shard_map/all_to_all | solution.py:237
  78.3 5.0 %gather_rows.1 = f32[2048,128]{1,0:T(8,128)S(1)} custom-call(f32[3072,128]{1,0:T(8,128)S(1)} %bitcast.43), custom_call_target="tpu_custom_call" | custom-call | tf_op jit(solution)/shard_map/gather_rows/pallas_call | solution.py:147
  83.3 21.5 %all_to_all.15 = f32[64,32,128]{2,1,0:T(8,128)S(1)} all-to-all(f32[64,32,128]{2,1,0:T(8,128)S(1)} %bitcast.45), channel_id=1, replica_groups=mesh['mp'=2,'tx'=8,'ty'=8] {'tx','ty'}, dimensions={0} | all-to-all | bytes 2097152 | tf_op jit(solution)/shard_map/all_to_all | solution.py:240
  104.9 4.6 %collective-permute-start.4 = (f32[64,32,128]{2,1,0:T(8,128)S(1)}, f32[64,32,128]{2,1,0:T(8,128)S(1)}, u32[]{:S(2)}, u32[]{:S(2)}) collective-permute-start(f32[64,32,128]{2,1,0:T(8,128)S(1)} %all_to_all.15), channel_id=1, source_target_pairs={{0,64},{64,0},{1,65},{65,1},{2,66},{66,2},{3,67},{67,3},{4,68},{68... | collective-permute-start | bytes 3145736 | tf_op jit(solution)/shard_map/ppermute | solution.py:241
  109.4 2.3 %collective-permute-done.4.received = f32[64,32,128]{2,1,0:T(8,128)S(1)} collective-permute-done((f32[64,32,128]{2,1,0:T(8,128)S(1)}, f32[64,32,128]{2,1,0:T(8,128)S(1)}, u32[]{:S(2)}, u32[]{:S(2)}) %collective-permute-start.4) | collective-permute-done | bytes 1048608 | tf_op jit(solution)/shard_map/ppermute | solution.py:241
  111.7 1.2 %finish.1 = f32[16,32,450]{2,1,0:T(8,128)} custom-call(f32[64,32,128]{2,1,0:T(8,128)S(1)} %collective-permute-done.4.received, f32[16,32,450]{2,1,0:T(8,128)S(1)} %bitcast.42, f32[16,32,450]{2,1,0:T(8,128)S(1)} %copy-done.2, f32[32,450]{1,0:T(8,128)S(1)} %get-tuple-element.17.rate), custom_call_target="tpu_custom_call" | custom-call | tf_op jit(solution)/shard_map/finish/pallas_call | solution.py:173
  (36 shorter events, 7.4 us)
Async XLA Ops:
  0.0 9.6 %copy-start = (f32[1,16,32,450]{3,2,1,0:T(8,128)S(1)}, f32[1,16,32,450]{3,2,1,0:T(8,128)}, u32[]{:S(2)}) copy-start(f32[1,16,32,450]{3,2,1,0:T(8,128)} %param.9) | copy-start | bytes 2764804
  1.6 13.2 %copy-start.9 = (s32[450]{0:T(512)S(1)}, s32[450]{0:T(512)}, u32[]{:S(2)}) copy-start(s32[450]{0:T(512)} %param.13) | copy-start | bytes 5404
  2.8 17.1 %collective-permute-start = (f32[17,32,2]{2,1,0:T(8,128)S(1)}, f32[17,32,2]{2,1,0:T(8,128)S(1)}, u32[]{:S(2)}, u32[]{:S(2)}) collective-permute-start(f32[17,32,2]{2,1,0:T(8,128)S(1)} %get-tuple-element.11), channel_id=1, source_target_pairs={{0,1},{1,2},{2,3},{3,4},{4,5},{5,6},{6,7},{7,0},{8,9},{9,10},{10,1... | collective-permute-start | bytes 13064 | tf_op jit(solution)/shard_map/ppermute | solution.py:186
  7.3 17.4 %collective-permute-start.1 = (f32[17,32,2]{2,1,0:T(8,128)S(1)}, f32[17,32,2]{2,1,0:T(8,128)S(1)}, u32[]{:S(2)}, u32[]{:S(2)}) collective-permute-start(f32[17,32,2]{2,1,0:T(8,128)S(1)} %get-tuple-element.12), channel_id=1, source_target_pairs={{1,0},{2,1},{3,2},{4,3},{5,4},{6,5},{7,6},{0,7},{9,8},{10,9},{11,1... | collective-permute-start | bytes 13064 | tf_op jit(solution)/shard_map/ppermute | solution.py:186
  9.6 17.2 %copy-start.3 = (s32[1,1,48]{2,1,0:T(1,128)S(1)}, s32[1,1,48]{2,1,0:T(1,128)}, u32[]{:S(2)}) copy-start(s32[1,1,48]{2,1,0:T(1,128)} %param.15) | copy-start | bytes 580
  9.6 17.2 %copy-start.4 = (s32[1,1,48,1]{2,3,1,0:T(1,128)S(1)}, s32[1,1,48,1]{2,3,1,0:T(1,128)}, u32[]{:S(2)}) copy-start(s32[1,1,48,1]{2,3,1,0:T(1,128)} %param.14) | copy-start | bytes 580
  9.7 17.2 %copy-start.5 = (s32[1,1,48]{2,1,0:T(1,128)S(1)}, s32[1,1,48]{2,1,0:T(1,128)}, u32[]{:S(2)}) copy-start(s32[1,1,48]{2,1,0:T(1,128)} %param.16) | copy-start | bytes 580
  10.4 38.6 %all-to-all-start.1 = ((f32[8,16,450]{2,1,0:T(8,128)}), f32[8,16,450]{2,1,0:T(8,128)S(1)}, u32[]{:S(2)}, u32[]{:S(2)}) async-start(f32[8,16,450]{2,1,0:T(8,128)} %broadcast_in_dim.41), calls=%async_computation.1 | async-start | bytes 524288 | tf_op jit(solution)/shard_map/all_to_all | solution.py:204
  25.6 31.7 %collective-permute-start.3 = (f32[17,2,454]{2,1,0:T(2,128)S(1)}, f32[17,2,454]{2,1,0:T(2,128)S(1)}, u32[]{:S(2)}, u32[]{:S(2)}) collective-permute-start(f32[17,2,454]{2,1,0:T(2,128)S(1)} %get-tuple-element.10), channel_id=1, source_target_pairs={{8,0},{16,8},{24,16},{32,24},{40,32},{48,40},{56,48},{9,1},{17,9},... | collective-permute-start | bytes 185240 | tf_op jit(solution)/shard_map/ppermute | solution.py:186
  43.2 1.1 %copy-start.1 = (f32[3072,128]{1,0:T(8,128)}, f32[3072,128]{1,0:T(8,128)S(1)}, u32[]{:S(2)}) copy-start(f32[3072,128]{1,0:T(8,128)S(1)} %contribute.1) | copy-start | bytes 4718596
  44.4 23.4 %collective-permute-start.2 = (f32[17,2,454]{2,1,0:T(2,128)}, f32[17,2,454]{2,1,0:T(2,128)}, u32[]{:S(2)}, u32[]{:S(2)}) collective-permute-start(f32[17,2,454]{2,1,0:T(2,128)} %get-tuple-element.9), channel_id=1, source_target_pairs={{0,8},{8,16},{16,24},{24,32},{32,40},{40,48},{48,56},{1,9},{9,17},... | collective-permute-start | bytes 185240 | tf_op jit(solution)/shard_map/ppermute | solution.py:186
  49.0 0.7 copy-start.6
  49.7 28.6 %all-to-all-start = ((f32[64,48,128]{2,1,0:T(8,128)}), f32[64,48,128]{2,1,0:T(8,128)S(1)}, u32[]{:S(2)}, u32[]{:S(2)}) async-start(f32[64,48,128]{2,1,0:T(8,128)} %bitcast.44), calls=%async_computation | async-start | bytes 3145728 | tf_op jit(solution)/shard_map/all_to_all | solution.py:237
  68.5 1.5 %copy-start.8 = (f32[17,1,454]{2,1,0:T(1,128)S(1)}, f32[17,1,454]{2,1,0:T(1,128)}, u32[]{:S(2)}) copy-start(f32[17,1,454]{2,1,0:T(1,128)} %get-tuple-element.15) | copy-start | bytes 92620
  70.0 2.8 %copy-start.7 = (f32[32,450]{1,0:T(8,128)S(1)}, f32[32,450]{1,0:T(8,128)}, u32[]{:S(2)}) copy-start(f32[32,450]{1,0:T(8,128)} %get-tuple-element.13) | copy-start | bytes 172804
  83.3 28.4 %copy-start.2 = (f32[16,32,450]{2,1,0:T(8,128)S(1)}, f32[16,32,450]{2,1,0:T(8,128)}, u32[]{:S(2)}) copy-start(f32[16,32,450]{2,1,0:T(8,128)} %fusion.6.moved) | copy-start | bytes 2764804
  104.9 6.8 %collective-permute-start.4 = (f32[64,32,128]{2,1,0:T(8,128)S(1)}, f32[64,32,128]{2,1,0:T(8,128)S(1)}, u32[]{:S(2)}, u32[]{:S(2)}) collective-permute-start(f32[64,32,128]{2,1,0:T(8,128)S(1)} %all_to_all.15), channel_id=1, source_target_pairs={{0,64},{64,0},{1,65},{65,1},{2,66},{66,2},{3,67},{67,3},{4,68},{68... | collective-permute-start | bytes 3145736 | tf_op jit(solution)/shard_map/ppermute | solution.py:241

commit v3 on v1

v3 whole, which is shorter than its diff:
```python
import functools

import jax
import jax.numpy as jnp
from jax import lax
from jax.experimental import pallas as pl
from jax.experimental.pallas import tpu as pltpu
from jax.sharding import PartitionSpec as P

TILE_AXES = ("tx", "ty")
QUARTERS = 4
LANES = 128
PACK = 16
WIDTH = 120
BLOCK = 30
FETCHES = (0, 30, 90, 150, 240, 330)
ROW_BLOCK = 1024
VMEM_LIMIT = 40 * 1024 * 1024


def spans(cols):
    return [(q * WIDTH, min(cols, (q + 1) * WIDTH)) for q in range(QUARTERS)]


def contribute_kernel(
    source, tile, dest, state, weight, out, field, blocks, loose, picks, product, turned, ready, sems, sent
):
    levels, rows, cols = state.shape
    entries = weight.shape[1]
    per_quarter = WIDTH // BLOCK
    groups = entries // PACK
    steps = -(-cols // BLOCK)
    lane = lax.broadcasted_iota(jnp.int32, (1, LANES), 1)

    fetch_state = pltpu.make_async_copy(state, field, sent.at[QUARTERS])
    fetch_state.start()
    fetches = {}
    for number, (low, high) in enumerate(zip(FETCHES, FETCHES[1:] + (cols,))):
        span = pl.ds(low, high - low)
        fetches[low] = pltpu.make_async_copy(weight.at[span], blocks.at[span], sems.at[number])
        fetches[low].start()

    place = lax.broadcasted_iota(jnp.int32, (entries, rows), 0)
    wanted = jnp.zeros((entries, rows), jnp.int32)
    for entry in range(entries):
        wanted = jnp.where(place == entry, source[entry], wanted)
    onehot = jnp.where(wanted == lax.broadcasted_iota(jnp.int32, (entries, rows), 1), 1.0, 0.0)
    onehot = onehot.astype(jnp.bfloat16)
    below = lax.broadcasted_iota(jnp.int32, (8, LANES), 0)
    here = lax.broadcasted_iota(jnp.int32, (8, LANES), 1) % 8
    for slot in range(2 * groups):
        tiles = jnp.zeros((8, LANES), jnp.int32)
        dests = jnp.zeros((8, LANES), jnp.int32)
        for e in range(8):
            tiles = jnp.where(here == e, tile[slot * 8 + e], tiles)
            dests = jnp.where(here == e, dest[slot * 8 + e], dests)
        tail = jnp.where(below == 6, tiles, jnp.where(below == 7, dests, 0))
        turned[WIDTH:LANES, slot * LANES : (slot + 1) * LANES] = tail.astype(jnp.float32)
    fetch_state.wait()
    for level in range(levels):
        picked = jnp.dot(onehot, field[level].astype(jnp.bfloat16), preferred_element_type=jnp.float32)
        for slot in range(2 * groups):
            loose[slot, level * 8 : level * 8 + 8, :] = picked[slot * 8 : slot * 8 + 8]
    for group in range(groups):
        for half in range(2):
            picks[group, half * LANES : (half + 1) * LANES, :] = loose[2 * group + half].astype(jnp.bfloat16)

    sends = []
    for step in range(steps):
        if step * BLOCK in fetches:
            fetches[step * BLOCK].wait()
        base = (step % per_quarter) * BLOCK
        for group in range(groups):
            streamed = blocks[step * BLOCK : (step + 1) * BLOCK, group * PACK : (group + 1) * PACK, :]
            whole = lax.dot_general(
                streamed.reshape(BLOCK * PACK, cols),
                picks[group],
                (((1,), (1,)), ((), ())),
                preferred_element_type=jnp.float32,
            ).reshape(BLOCK, PACK, 2 * LANES)
            for half in range(2):
                slot = 2 * group + half
                own = whole[:, half * 8 : half * 8 + 8, half * LANES : (half + 1) * LANES]
                product[slot] = own.reshape(BLOCK * 8, LANES)
                y = jnp.zeros((BLOCK, LANES), jnp.float32)
                for e in range(8):
                    y = jnp.where(lane % 8 == e, product[slot, pl.ds(e, BLOCK, stride=8), :], y)
                if (step + 1) * BLOCK > cols:
                    column = lax.broadcasted_iota(jnp.int32, (BLOCK, LANES), 0) + step * BLOCK
                    y = jnp.where(column < cols, y, 0.0)
                turned[base : base + BLOCK, slot * LANES : (slot + 1) * LANES] = y
        if step % per_quarter == per_quarter - 1 or step == steps - 1:
            quarter = step // per_quarter
            for slot in range(2 * groups):
                block = turned[:, slot * LANES : (slot + 1) * LANES].T
                for level in range(levels):
                    ready[quarter, level, slot * 8 : slot * 8 + 8, :] = block[level * 8 : level * 8 + 8]
            sends.append(pltpu.make_async_copy(ready.at[quarter], out.at[:, quarter], sent.at[quarter]))
            sends[-1].start()
    for send in sends:
        send.wait()


def contribute(state, weight, source, tile, dest):
    levels, rows, cols = state.shape
    entries = weight.shape[1]
    groups = entries // PACK
    steps = -(-cols // BLOCK)
    scalars = pl.BlockSpec(memory_space=pltpu.SMEM)
    away = pl.BlockSpec(memory_space=pltpu.HBM)
    return pl.pallas_call(
        contribute_kernel,
        in_specs=[scalars, scalars, scalars, away, away],
        out_specs=away,
        scratch_shapes=[
            pltpu.VMEM((levels, rows, cols), jnp.float32),
            pltpu.VMEM((steps * BLOCK, entries, cols), jnp.bfloat16),
            pltpu.VMEM((2 * groups, LANES, cols), jnp.float32),
            pltpu.VMEM((groups, 2 * LANES, cols), jnp.bfloat16),
            pltpu.VMEM((2 * groups, BLOCK * 8, LANES), jnp.float32),
            pltpu.VMEM((LANES, 2 * groups * LANES), jnp.float32),
            pltpu.VMEM((QUARTERS, levels, entries, LANES), jnp.float32),
            pltpu.SemaphoreType.DMA((len(FETCHES),)),
            pltpu.SemaphoreType.DMA((QUARTERS + 1,)),
        ],
        out_shape=jax.ShapeDtypeStruct((levels, QUARTERS, entries, LANES), jnp.float32),
        compiler_params=pltpu.CompilerParams(vmem_limit_bytes=VMEM_LIMIT),
        cost_estimate=pl.CostEstimate(
            flops=2 * entries * levels * cols * cols,
            bytes_accessed=2 * entries * cols * cols,
            transcendentals=0,
        ),
        name="contribute",
    )(source, tile, dest, state, weight)


def gather_rows_kernel(tile_rows, values, out, halves, labels):
    block = pl.program_id(0)

    @pl.when(block == 0)
    def prepare():
        x = values[...]
        high = x.astype(jnp.bfloat16)
        low = (x - high.astype(jnp.float32)).astype(jnp.bfloat16)
        halves[:, :LANES] = high
        halves[:, LANES:] = low
        lane = lax.broadcasted_iota(jnp.int32, (8, LANES), 1)
        pick = jnp.where(lane == LANES - 2, float(tile_rows), jnp.where(lane == LANES - 1, 1.0, 0.0))
        labels[...] = lax.dot_general(
            pick.astype(jnp.bfloat16), high, (((1,), (1,)), ((), ())), preferred_element_type=jnp.float32
        ).astype(jnp.int32)

    count = values.shape[0]
    row = lax.broadcasted_iota(jnp.int32, (ROW_BLOCK, count), 0) + block * ROW_BLOCK
    onehot = jnp.where(row == labels[0:1, :], 1.0, 0.0).astype(jnp.bfloat16)
    sums = jnp.dot(onehot, halves[...], preferred_element_type=jnp.float32)
    out[...] = sums[:, :LANES] + sums[:, LANES:]


def gather_rows(values, tiles, tile_rows):
    count = values.shape[0]
    return pl.pallas_call(
        functools.partial(gather_rows_kernel, tile_rows),
        grid=(tiles * tile_rows // ROW_BLOCK,),
        in_specs=[pl.BlockSpec((count, LANES), lambda i: (0, 0))],
        out_specs=pl.BlockSpec((ROW_BLOCK, LANES), lambda i: (i, 0)),
        out_shape=jax.ShapeDtypeStruct((tiles * tile_rows, LANES), jnp.float32),
        scratch_shapes=[
            pltpu.VMEM((count, 2 * LANES), jnp.bfloat16),
            pltpu.VMEM((8, count), jnp.int32),
        ],
        compiler_params=pltpu.CompilerParams(vmem_limit_bytes=VMEM_LIMIT),
        name="gather_rows",
    )(values)


def coefficient(flags, diffusion, mask):
    return diffusion * jnp.where(flags[0] == 1, mask.astype(jnp.float32), 1.0)


def edges_kernel(first, last, bottom, diffusion, low, high):
    levels, rows, _ = first.shape
    cols = diffusion.shape[1]
    end = (cols - 2) % LANES
    starts = [first[level][:, :2] for level in range(levels)] + [diffusion[:, :2]]
    ends = [last[level][:, end : end + 2] for level in range(levels)] + [diffusion[:, cols - 2 :]]
    edge = jnp.concatenate([bottom[level, 7:8, :] for level in range(levels)], axis=0)
    for out, pairs in ((low, starts), (high, ends)):
        message = jnp.concatenate(pairs, axis=1)
        out[:levels, :cols] = edge
        for part in range(rows // 8):
            start = part * LANES
            out[levels:, start : start + message.shape[1]] = message[part * 8 : part * 8 + 8]


def edges(field, diffusion):
    levels, rows, cols = field.shape
    out = jax.ShapeDtypeStruct((levels + 8, rows // 8 * LANES), jnp.float32)
    message = pl.BlockSpec(out.shape, lambda i: (0, 0))
    return pl.pallas_call(
        edges_kernel,
        grid=(1,),
        in_specs=[
            pl.BlockSpec((levels, rows, LANES), lambda i: (0, 0, 0)),
            pl.BlockSpec((levels, rows, LANES), lambda i: (0, 0, (cols - 2) // LANES)),
            pl.BlockSpec((levels, 8, cols), lambda i: (0, rows // 8 - 1, 0)),
            pl.BlockSpec((rows, cols), lambda i: (0, 0)),
        ],
        out_specs=[message, message],
        out_shape=[out, out],
        name="edges",
    )(field, field, field, diffusion)


def columns(message, rows):
    tall = message.shape[0]
    parts = [message[tall - 8 :, part * LANES : (part + 1) * LANES] for part in range(rows // 8)]
    return jnp.concatenate(parts, axis=0)


def rims_kernel(first, last, diffusion, west, east, low, high, three):
    levels, _, cols = first.shape
    rows = diffusion.shape[0]
    left, right = columns(west, rows), columns(east, rows)
    low[...] = jnp.zeros(low.shape, jnp.float32)
    high[...] = jnp.zeros(high.shape, jnp.float32)
    for out, block, start in ((low, first, 0), (high, last, rows - 2)):
        for level in range(levels + 1):
            place = pl.ds(2 * level, 2)
            if level < levels:
                out[place, LANES : LANES + cols] = block[level, start % 8 : start % 8 + 2, :]
            else:
                out[place, LANES : LANES + cols] = diffusion[start : start + 2, :]
            out[place, LANES - 2 : LANES] = left[start : start + 2, 2 * level : 2 * level + 2]
            out[place, LANES + cols : LANES + cols + 2] = right[start : start + 2, 2 * level : 2 * level + 2]
    three[0] = west[:levels, :cols]
    three[1] = jnp.concatenate([last[level, 7:8, :] for level in range(levels)], axis=0)
    three[2] = east[:levels, :cols]


def rims(field, diffusion, west, east):
    levels, rows, cols = field.shape
    wide = LANES * (2 + -(-cols // LANES))
    rim = jax.ShapeDtypeStruct((2 * levels + 2, wide), jnp.float32)
    three = jax.ShapeDtypeStruct((3, levels, cols), jnp.float32)
    whole = lambda shape: pl.BlockSpec(shape, lambda i: (0,) * len(shape))
    return pl.pallas_call(
        rims_kernel,
        grid=(1,),
        in_specs=[
            pl.BlockSpec((levels, 8, cols), lambda i: (0, 0, 0)),
            pl.BlockSpec((levels, 8, cols), lambda i: (0, rows // 8 - 1, 0)),
            whole((rows, cols)),
            whole(west.shape),
            whole(east.shape),
        ],
        out_specs=[whole(rim.shape), whole(rim.shape), whole(three.shape)],
        out_shape=[rim, rim, three],
        name="rims",
    )(field, field, diffusion, west, east)


def mix_kernel(
    flags, field, diffusion, rate, mask, west, east, south, north, near, behind, ahead, fold_map, out, ext, coefs, folded, sides
):
    part, rows, cols = field.shape
    levels = near.shape[1]
    step = pl.program_id(0)
    own_rows, own_lanes = slice(8, 8 + rows), slice(LANES, LANES + cols)
    active = coefficient(flags, 1.0, mask[...])

    @pl.when(step == 0)
    def prepare():
        ext[...] = jnp.zeros(ext.shape, jnp.float32)
        coefs[...] = jnp.zeros(coefs.shape, jnp.float32)
        coefs[own_rows, own_lanes] = diffusion[...] * active
        sides[0] = columns(west, rows)
        sides[1] = columns(east, rows)
        coefs[own_rows, LANES - 2 : LANES] = sides[0, :, 2 * levels : 2 * levels + 2]
        coefs[own_rows, LANES + cols : LANES + cols + 2] = sides[1, :, 2 * levels : 2 * levels + 2]
        coefs[6:8, :] = south[2 * levels : 2 * levels + 2, :]
        coefs[8 + rows : 10 + rows, :] = north[2 * levels : 2 * levels + 2, :]

    @pl.when(jnp.logical_and(step == 0, flags[1] == 1))
    def fold():
        total = jnp.zeros((3 * levels, cols), jnp.float32)
        place = lax.broadcasted_iota(jnp.int32, (cols, cols), 0)
        held = [behind[1], behind[2], near[0], near[1], near[2], ahead[0], ahead[1], ahead[2]]
        for number, whole in enumerate(held):
            copy = (flags[2] + number + 5) % 8
            high = whole.astype(jnp.bfloat16).astype(jnp.float32)
            rest = whole - high
            middle = rest.astype(jnp.bfloat16).astype(jnp.float32)
            parts = jnp.concatenate([high, middle, rest - middle], axis=0).astype(jnp.bfloat16)
            onehot = jnp.where(place + copy * cols == fold_map[...], 1.0, 0.0).astype(jnp.bfloat16)
            total = total + jnp.dot(parts, onehot, preferred_element_type=jnp.float32)
        folded[...] = total[:levels] + total[levels : 2 * levels] + total[2 * levels :]

    tall, wide = ext.shape[1:]
    again = jnp.where(flags[0] == 1, 0.0, 1.0)

    def sweep(f, c):
        around = pltpu.roll(f, 1, 0) + pltpu.roll(f, tall - 1, 0)
        around = around + pltpu.roll(f, 1, 1) + pltpu.roll(f, wide - 1, 1)
        return f + c * (around - 4.0 * f)

    for local in range(part):
        ext[local, own_rows, own_lanes] = field[local]

    for number in range(levels // part):

        @pl.when(step == number)
        def outside():
            for local in range(part):
                level = number * part + local
                pair = slice(2 * level, 2 * level + 2)
                ext[local, own_rows, LANES - 2 : LANES] = sides[0, :, pair]
                ext[local, own_rows, LANES + cols : LANES + cols + 2] = sides[1, :, pair]
                ext[local, 6:8, :] = south[pair, :]
                ext[local, 8 + rows : 10 + rows, :] = north[pair, :]

        @pl.when(jnp.logical_and(step == number, flags[1] == 1))
        def folded_rows():
            for local in range(part):
                level = number * part + local
                ext[local, 8 + rows : 9 + rows, own_lanes] = folded[level : level + 1, :]

    for local in range(part):
        once = sweep(ext[local], coefs[...])
        twice = sweep(once, coefs[...] * again)
        out[local] = twice[own_rows, own_lanes] - rate[...] * active * field[local]


def mix(flags, field, diffusion, rate, mask, west, east, south, north, near, behind, ahead, fold_map):
    levels, rows, cols = field.shape
    part = 4
    wide = south.shape[1]
    whole = lambda shape: pl.BlockSpec(shape, lambda i: (0,) * len(shape))
    block = pl.BlockSpec((part, rows, cols), lambda i: (i, 0, 0))
    return pl.pallas_call(
        mix_kernel,
        grid=(levels // part,),
        in_specs=[
            pl.BlockSpec(memory_space=pltpu.SMEM),
            block,
            whole((rows, cols)),
            whole((rows, cols)),
            whole((rows, cols)),
            whole(west.shape),
            whole(east.shape),
            whole(south.shape),
            whole(north.shape),
            whole(near.shape),
            whole(behind.shape),
            whole(ahead.shape),
            whole((1, cols)),
        ],
        out_specs=block,
        scratch_shapes=[
            pltpu.VMEM((part, rows + 16, wide), jnp.float32),
            pltpu.VMEM((rows + 16, wide), jnp.float32),
            pltpu.VMEM((levels, cols), jnp.float32),
            pltpu.VMEM((2, rows, LANES), jnp.float32),
        ],
        out_shape=jax.ShapeDtypeStruct(field.shape, jnp.float32),
        name="mix",
    )(flags, field, diffusion, rate, mask, west, east, south, north, near, behind, ahead, fold_map[None])


def finish_kernel(flags, received, base, rate, mask, out, inner, outer, fetched, stored):
    levels, rows, cols = base.shape
    parts = fetched.shape[0]
    part = levels // parts
    fetches = []
    for number in range(parts):
        span = pl.ds(number * part, part)
        fetches.append(pltpu.make_async_copy(base.at[span], inner.at[span], fetched.at[number]))
        fetches[-1].start()
    pull = coefficient(flags, rate[...], mask[...])
    stores = []
    for number in range(parts):
        fetches[number].wait()
        for level in range(number * part, (number + 1) * part):
            pieces = [received[level * QUARTERS + q][:, : high - low] for q, (low, high) in enumerate(spans(cols))]
            outer[level] = inner[level] + pull * jnp.concatenate(pieces, axis=1)
        span = pl.ds(number * part, part)
        stores.append(pltpu.make_async_copy(outer.at[span], out.at[span], stored.at[number]))
        stores[-1].start()
    for store in stores:
        store.wait()


def finish(flags, received, base, rate, mask):
    parts = 4
    inside = pl.BlockSpec(memory_space=pltpu.VMEM)
    away = pl.BlockSpec(memory_space=pltpu.HBM)
    return pl.pallas_call(
        finish_kernel,
        in_specs=[pl.BlockSpec(memory_space=pltpu.SMEM), inside, away, inside, inside],
        out_specs=away,
        out_shape=jax.ShapeDtypeStruct(base.shape, jnp.float32),
        scratch_shapes=[
            pltpu.VMEM(base.shape, jnp.float32),
            pltpu.VMEM(base.shape, jnp.float32),
            pltpu.SemaphoreType.DMA((parts,)),
            pltpu.SemaphoreType.DMA((parts,)),
        ],
        compiler_params=pltpu.CompilerParams(vmem_limit_bytes=VMEM_LIMIT),
        name="finish",
    )(flags, received, base, rate, mask)


def shift(value, axis, forward, periodic):
    count = lax.axis_size(axis)
    pairs = [(i, i + 1) for i in range(count - 1)] + ([(count - 1, 0)] if periodic else [])
    if not forward:
        pairs = [(b, a) for a, b in pairs]
    return lax.ppermute(value, axis, pairs)


def across(value, distance):
    count = lax.axis_size("ty")
    start = 2 * lax.axis_size("tx") * count - count
    pairs = [(start + i, start + (i + distance) % count) for i in range(count)]
    return lax.ppermute(value, ("mp", "tx", "ty"), pairs)


def spread(value, axes):
    return lax.all_to_all(value, axes, split_axis=0, concat_axis=0, tiled=True)


def body(
    state,
    diffusion,
    exchange_rate,
    land_mask,
    fold_map,
    entry_tile,
    entry_source,
    entry_dest,
    entry_weight,
):
    field = state[0]
    levels, rows, cols = field.shape
    tiles = lax.axis_size("tx") * lax.axis_size("ty")
    entries = entry_source.shape[2]
    ocean = lax.axis_index("mp") == 1
    fold_here = jnp.logical_and(ocean, lax.axis_index("tx") == lax.axis_size("tx") - 1)
    flags = jnp.stack([ocean, fold_here, lax.axis_index("ty")]).astype(jnp.int32)
    low, high = edges(field, diffusion[0])
    west = shift(high, "ty", True, True)
    east = shift(low, "ty", False, True)

    source, tile, dest = entry_source[0, 0], entry_tile[0, 0, :, 0], entry_dest[0, 0]
    weight = jnp.transpose(entry_weight[0, 0], (1, 0, 2))
    pieces = contribute(field, weight, source, tile, dest)
    pieces, west, east = lax.optimization_barrier((pieces, west, east))
    arrived = spread(pieces.reshape(tiles, entries, LANES), TILE_AXES)

    low, high, near = rims(field, diffusion[0], west, east)
    south = shift(high, "tx", True, False)
    north = shift(low, "tx", False, False)
    behind = across(near, 3)
    ahead = across(near, -3)
    summed = gather_rows(arrived.reshape(-1, LANES), tiles, rows).reshape(tiles, rows, LANES)
    summed, south, north, behind, ahead = lax.optimization_barrier((summed, south, north, behind, ahead))
    base = mix(
        flags,
        field,
        diffusion[0],
        exchange_rate[0],
        land_mask,
        west,
        east,
        south,
        north,
        near,
        behind,
        ahead,
        fold_map,
    )
    received, base = lax.optimization_barrier((spread(summed, TILE_AXES), base))
    received = lax.ppermute(received, "mp", [(0, 1), (1, 0)])
    return finish(flags, received, base, exchange_rate[0], land_mask)[None]


def solution(mesh):
    in_specs = (
        P("mp", None, "tx", "ty"),
        P("mp", "tx", "ty"),
        P("mp", "tx", "ty"),
        P("tx", "ty"),
        P("ty"),
        P("mp", "tx", "ty", None),
        P("mp", "tx", "ty"),
        P("mp", "tx", "ty"),
        P("mp", "tx", "ty", None, None),
    )
    out_specs = P("mp", None, "tx", "ty")
    return jax.shard_map(body, mesh=mesh, in_specs=in_specs, out_specs=out_specs, check_vma=False)
```

time: 129 us -> 90.2 us (0.70)
  the two profiles are of different devices: /device:TPU:9 before, /device:TPU:1 now
where the time goes in v3:
time: 90.2 us; the launch traced here: 89.7 us
  starting transfers between devices  31.2 us (35%)
  waiting for transfers between devices  28.2 us (31%)
  Pallas kernels  27.7 us (31%)
  local copies, waits for them, and re-layouts  1.87 us (2%)
    all_to_all x2, waiting for transfers between devices, spread(): return lax.all_to_all(value, axes, split_axis=0, concat_axis=0, tiled=True)  25.9 us
    all_to_all x2, starting transfers between devices, spread(): return lax.all_to_all(value, axes, split_axis=0, concat_axis=0, tiled=True)  16.1 us
    pallas_call x1, Pallas kernels, contribute(): pl.pallas_call(contribute_kernel, in_specs=[scalars, scalars, scalars, aw...  11.1 us
    ppermute x4, starting transfers between devices, shift(): return lax.ppermute(value, axis, pairs)  10.8 us
    pallas_call x1, Pallas kernels, mix(): pl.pallas_call(mix_kernel, grid=(levels // part,), in_specs=[pl.BlockSpec...  5.93 us
    pallas_call x1, Pallas kernels, gather_rows(): pl.pallas_call(functools.partial(gather_rows_kernel, tile_rows), grid=(ti...  4.76 us
    ppermute x1, starting transfers between devices, body(): received = lax.ppermute(received, 'mp', [(0, 1), (1, 0)])  2.85 us
    ppermute x1, waiting for transfers between devices, body(): received = lax.ppermute(received, 'mp', [(0, 1), (1, 0)])  2.29 us
  transfers between devices with their start and end apart: 9, of which 3 were waited for; matrix products, arithmetic and copies ran while one was open for 1% of the time, Pallas kernels for 26%

profile of v3, /device:TPU:1, one launch (start us, length us, event | category | flops | bytes accessed | tf_op | source)
XLA Modules:
  0.0 89.7 jit_solution(5004364938646265880)
XLA Ops:
  0.0 2.0 %edges.1 = (f32[24,512]{1,0:T(8,128)}, f32[24,512]{1,0:T(8,128)}) custom-call(f32[16,32,450]{2,1,0:T(8,128)} %bitcast.17, f32[16,32,450]{2,1,0:T(8,128)} %bitcast.18, f32[16,32,450]{2,1,0:T(8,128)} %bitcast.19, f32[32,450]{1,0:T(8,128)} %bitcast.31), custom_call_target="tpu_custom_call" | custom-call | tf_op jit(solution)/shard_map/edges/pallas_call | solution.py:200
  2.0 4.4 %collective-permute-start = (f32[24,512]{1,0:T(8,128)}, f32[24,512]{1,0:T(8,128)S(1)}, u32[]{:S(2)}, u32[]{:S(2)}) collective-permute-start(f32[24,512]{1,0:T(8,128)} %get-tuple-element.20), channel_id=1, source_target_pairs={{0,1},{1,2},{2,3},{3,4},{4,5},{5,6},{6,7},{7,0},{8,9},{9,10},{10,1... | collective-permute-start | bytes 147464 | tf_op jit(solution)/shard_map/ppermute | solution.py:418
  6.5 2.2 %collective-permute-start.1 = (f32[24,512]{1,0:T(8,128)}, f32[24,512]{1,0:T(8,128)S(1)}, u32[]{:S(2)}, u32[]{:S(2)}) collective-permute-start(f32[24,512]{1,0:T(8,128)} %get-tuple-element.21), channel_id=1, source_target_pairs={{1,0},{2,1},{3,2},{4,3},{5,4},{6,5},{7,6},{0,7},{9,8},{10,9},{11,1... | collective-permute-start | bytes 147464 | tf_op jit(solution)/shard_map/ppermute | solution.py:418
  8.7 11.1 %contribute.1 = f32[16,4,48,128]{3,2,1,0:T(8,128)} custom-call(s32[48]{0:T(128)S(1)} %bitcast.27, s32[48]{0:T(128)S(1)} %bitcast.28, s32[48]{0:T(128)S(1)} %bitcast.29, f32[16,32,450]{2,1,0:T(8,128)S(1)} %bitcast.23, bf16[450,48,450]{2,1,0:T(8,128)(2,1)} %bitcast.30), custom_call_target="tpu_custom_call" | custom-call | flops 311040000 | bytes 19440000 | tf_op jit(solution)/shard_map/contribute/pallas_call | solution.py:111
  19.9 0.6 copy-done.8
  20.5 0.0 copy-done.9
  20.5 8.3 %all-to-all-start = ((f32[64,48,128]{2,1,0:T(8,128)}), f32[64,48,128]{2,1,0:T(8,128)S(1)}, u32[]{:S(2)}, u32[]{:S(2)}) async-start(f32[64,48,128]{2,1,0:T(8,128)} %bitcast.10), calls=%async_computation | async-start | bytes 3145728 | tf_op jit(solution)/shard_map/all_to_all | solution.py:429
  28.8 1.9 %rims.1 = (f32[34,768]{1,0:T(8,128)}, f32[34,768]{1,0:T(8,128)}, f32[3,16,450]{2,1,0:T(8,128)}) custom-call(f32[16,32,450]{2,1,0:T(8,128)} %bitcast.20, f32[16,32,450]{2,1,0:T(8,128)} %bitcast.21, f32[32,450]{1,0:T(8,128)} %bitcast.32, f32[24,512]{1,0:T(8,128)} %copy-done.8, f32[24,512]{1,0:T(8,128)} %copy-done.9), custom_call_target="tpu_custom_call" | custom-call | tf_op jit(solution)/shard_map/rims/pallas_call | solution.py:247
  30.7 2.9 %collective-permute-start.2 = (f32[34,768]{1,0:T(8,128)}, f32[34,768]{1,0:T(8,128)S(1)}, u32[]{:S(2)}, u32[]{:S(2)}) collective-permute-start(f32[34,768]{1,0:T(8,128)} %get-tuple-element.25), channel_id=1, source_target_pairs={{0,8},{8,16},{16,24},{24,32},{32,40},{40,48},{48,56},{1,9},{9,17},... | collective-permute-start | bytes 313352 | tf_op jit(solution)/shard_map/ppermute | solution.py:418
  33.6 1.3 %collective-permute-start.3 = (f32[34,768]{1,0:T(8,128)}, f32[34,768]{1,0:T(8,128)S(1)}, u32[]{:S(2)}, u32[]{:S(2)}) collective-permute-start(f32[34,768]{1,0:T(8,128)} %get-tuple-element.26), channel_id=1, source_target_pairs={{8,0},{16,8},{24,16},{32,24},{40,32},{48,40},{56,48},{9,1},{17,9},... | collective-permute-start | bytes 313352 | tf_op jit(solution)/shard_map/ppermute | solution.py:418
  34.9 0.7 collective-permute-start.5
  35.6 0.7 collective-permute-start.4
  36.3 15.6 %all-to-all-done = f32[64,48,128]{2,1,0:T(8,128)S(1)} async-done(((f32[64,48,128]{2,1,0:T(8,128)}), f32[64,48,128]{2,1,0:T(8,128)S(1)}, u32[]{:S(2)}, u32[]{:S(2)}) %all-to-all-start) | async-done | bytes 1572896 | tf_op jit(solution)/shard_map/all_to_all | solution.py:429
  51.9 4.8 %gather_rows.1 = f32[2048,128]{1,0:T(8,128)} custom-call(f32[3072,128]{1,0:T(8,128)S(1)} %bitcast.24), custom_call_target="tpu_custom_call" | custom-call | tf_op jit(solution)/shard_map/gather_rows/pallas_call | solution.py:162
  56.7 7.8 %all-to-all-start.1 = ((f32[64,32,128]{2,1,0:T(8,128)}), f32[64,32,128]{2,1,0:T(8,128)S(1)}, u32[]{:S(2)}, u32[]{:S(2)}) async-start(f32[64,32,128]{2,1,0:T(8,128)} %bitcast.12), calls=%async_computation.1 | async-start | bytes 2097152 | tf_op jit(solution)/shard_map/all_to_all | solution.py:429
  64.5 0.0 copy-start.2
  64.6 0.0 copy-start.3
  64.6 0.7 pad_add_fusion.flags
  65.3 5.9 %mix.1.base = f32[16,32,450]{2,1,0:T(8,128)} custom-call(s32[3]{0:T(128)} %pad_add_fusion.flags, f32[16,32,450]{2,1,0:T(8,128)} %bitcast.22, f32[32,450]{1,0:T(8,128)} %bitcast.33, f32[32,450]{1,0:T(8,128)} %bitcast.25, s32[32,450]{1,0:T(8,128)} %mask.3, f32[24,512]{1,0:T(8,128)} %copy-done.8, f32[24,512]{1,0:T(8,128)} %copy-done.9, f32[34,768]{1,0:T(8,128)} %copy-done.10, ...), custom_call_target="tpu_custom_call" | custom-call | tf_op jit(solution)/shard_map/mix/pallas_call | solution.py:340
  71.2 10.3 %all-to-all-done.1 = f32[64,32,128]{2,1,0:T(8,128)S(1)} async-done(((f32[64,32,128]{2,1,0:T(8,128)}), f32[64,32,128]{2,1,0:T(8,128)S(1)}, u32[]{:S(2)}, u32[]{:S(2)}) %all-to-all-start.1) | async-done | bytes 1048608 | tf_op jit(solution)/shard_map/all_to_all | solution.py:429
  81.5 2.9 %collective-permute-start.6 = (f32[64,32,128]{2,1,0:T(8,128)S(1)}, f32[64,32,128]{2,1,0:T(8,128)S(1)}, u32[]{:S(2)}, u32[]{:S(2)}) collective-permute-start(f32[64,32,128]{2,1,0:T(8,128)S(1)} %all-to-all-done.1), channel_id=1, source_target_pairs={{0,64},{64,0},{1,65},{65,1},{2,66},{66,2},{3,67},{67,3},{4,68},{68... | collective-permute-start | bytes 3145736 | tf_op jit(solution)/shard_map/ppermute | solution.py:483
  84.3 2.3 %collective-permute-done.6.received = f32[64,32,128]{2,1,0:T(8,128)S(1)} collective-permute-done((f32[64,32,128]{2,1,0:T(8,128)S(1)}, f32[64,32,128]{2,1,0:T(8,128)S(1)}, u32[]{:S(2)}, u32[]{:S(2)}) %collective-permute-start.6) | collective-permute-done | bytes 1048608 | tf_op jit(solution)/shard_map/ppermute | solution.py:483
  86.6 1.2 %copy-done.1 = f32[16,32,450]{2,1,0:T(8,128)S(1)} copy-done((f32[16,32,450]{2,1,0:T(8,128)S(1)}, f32[16,32,450]{2,1,0:T(8,128)}, u32[]{:S(2)}) %copy-start.1) | copy-done | bytes 921624
  87.8 1.9 %finish.1 = f32[16,32,450]{2,1,0:T(8,128)} custom-call(s32[3]{0:T(128)S(1)} %copy-done.4, f32[64,32,128]{2,1,0:T(8,128)S(1)} %collective-permute-done.6.received, f32[16,32,450]{2,1,0:T(8,128)S(1)} %copy-done.1, f32[32,450]{1,0:T(8,128)S(1)} %bitcast.26, s32[32,450]{1,0:T(8,128)S(1)} %copy-done.3), custom_call_target="tpu_custom_call" | custom-call | tf_op jit(solution)/shard_map/finish/pallas_call | solution.py:397
  (29 shorter events, 0.1 us)
Async XLA Ops:
  0.0 8.7 %copy-start = (f32[1,16,32,450]{3,2,1,0:T(8,128)S(1)}, f32[1,16,32,450]{3,2,1,0:T(8,128)}, u32[]{:S(2)}) copy-start(f32[1,16,32,450]{3,2,1,0:T(8,128)} %param.9) | copy-start | bytes 2764804
  0.0 8.7 %copy-start.5 = (s32[1,1,48]{2,1,0:T(1,128)S(1)}, s32[1,1,48]{2,1,0:T(1,128)}, u32[]{:S(2)}) copy-start(s32[1,1,48]{2,1,0:T(1,128)} %param.15) | copy-start | bytes 580
  0.0 8.7 %copy-start.6 = (s32[1,1,48,1]{2,3,1,0:T(1,128)S(1)}, s32[1,1,48,1]{2,3,1,0:T(1,128)}, u32[]{:S(2)}) copy-start(s32[1,1,48,1]{2,3,1,0:T(1,128)} %param.14) | copy-start | bytes 580
  0.0 8.7 %copy-start.7 = (s32[1,1,48]{2,1,0:T(1,128)S(1)}, s32[1,1,48]{2,1,0:T(1,128)}, u32[]{:S(2)}) copy-start(s32[1,1,48]{2,1,0:T(1,128)} %param.16) | copy-start | bytes 580
  2.0 17.8 %collective-permute-start = (f32[24,512]{1,0:T(8,128)}, f32[24,512]{1,0:T(8,128)S(1)}, u32[]{:S(2)}, u32[]{:S(2)}) collective-permute-start(f32[24,512]{1,0:T(8,128)} %get-tuple-element.20), channel_id=1, source_target_pairs={{0,1},{1,2},{2,3},{3,4},{4,5},{5,6},{6,7},{7,0},{8,9},{9,10},{10,1... | collective-permute-start | bytes 147464 | tf_op jit(solution)/shard_map/ppermute | solution.py:418
  6.5 13.4 %collective-permute-start.1 = (f32[24,512]{1,0:T(8,128)}, f32[24,512]{1,0:T(8,128)S(1)}, u32[]{:S(2)}, u32[]{:S(2)}) collective-permute-start(f32[24,512]{1,0:T(8,128)} %get-tuple-element.21), channel_id=1, source_target_pairs={{1,0},{2,1},{3,2},{4,3},{5,4},{6,5},{7,6},{0,7},{9,8},{10,9},{11,1... | collective-permute-start | bytes 147464 | tf_op jit(solution)/shard_map/ppermute | solution.py:418
  19.8 0.6 copy-start.8
  19.9 0.6 copy-start.9
  20.5 31.4 %all-to-all-start = ((f32[64,48,128]{2,1,0:T(8,128)}), f32[64,48,128]{2,1,0:T(8,128)S(1)}, u32[]{:S(2)}, u32[]{:S(2)}) async-start(f32[64,48,128]{2,1,0:T(8,128)} %bitcast.10), calls=%async_computation | async-start | bytes 3145728 | tf_op jit(solution)/shard_map/all_to_all | solution.py:429
  30.7 26.0 %collective-permute-start.2 = (f32[34,768]{1,0:T(8,128)}, f32[34,768]{1,0:T(8,128)S(1)}, u32[]{:S(2)}, u32[]{:S(2)}) collective-permute-start(f32[34,768]{1,0:T(8,128)} %get-tuple-element.25), channel_id=1, source_target_pairs={{0,8},{8,16},{16,24},{24,32},{32,40},{40,48},{48,56},{1,9},{9,17},... | collective-permute-start | bytes 313352 | tf_op jit(solution)/shard_map/ppermute | solution.py:418
  33.6 23.1 %collective-permute-start.3 = (f32[34,768]{1,0:T(8,128)}, f32[34,768]{1,0:T(8,128)S(1)}, u32[]{:S(2)}, u32[]{:S(2)}) collective-permute-start(f32[34,768]{1,0:T(8,128)} %get-tuple-element.26), channel_id=1, source_target_pairs={{8,0},{16,8},{24,16},{32,24},{40,32},{48,40},{56,48},{9,1},{17,9},... | collective-permute-start | bytes 313352 | tf_op jit(solution)/shard_map/ppermute | solution.py:418
  34.9 21.7 %collective-permute-start.5 = (f32[3,16,450]{2,1,0:T(8,128)}, f32[3,16,450]{2,1,0:T(8,128)S(1)}, u32[]{:S(2)}, u32[]{:S(2)}) collective-permute-start(f32[3,16,450]{2,1,0:T(8,128)} %get-tuple-element.27.near), channel_id=1, source_target_pairs={{120,125},{121,126},{122,127},{123,120},{124,121},{125,122},{126,1... | collective-permute-start | bytes 259208 | tf_op jit(solution)/shard_map/ppermute | solution.py:425
  35.6 21.0 %collective-permute-start.4 = (f32[3,16,450]{2,1,0:T(8,128)}, f32[3,16,450]{2,1,0:T(8,128)S(1)}, u32[]{:S(2)}, u32[]{:S(2)}) collective-permute-start(f32[3,16,450]{2,1,0:T(8,128)} %get-tuple-element.27.near), channel_id=1, source_target_pairs={{120,123},{121,124},{122,125},{123,126},{124,127},{125,120},{126,1... | collective-permute-start | bytes 259208 | tf_op jit(solution)/shard_map/ppermute | solution.py:425
  56.7 8.6 %copy-start.12 = (f32[3,16,450]{2,1,0:T(8,128)}, f32[3,16,450]{2,1,0:T(8,128)S(1)}, u32[]{:S(2)}) copy-start(f32[3,16,450]{2,1,0:T(8,128)S(1)} %collective-permute-done.5.ahead) | copy-start | bytes 259204
  56.7 8.6 %copy-start.13 = (f32[3,16,450]{2,1,0:T(8,128)}, f32[3,16,450]{2,1,0:T(8,128)S(1)}, u32[]{:S(2)}) copy-start(f32[3,16,450]{2,1,0:T(8,128)S(1)} %collective-permute-done.4.behind) | copy-start | bytes 259204
  56.7 8.6 %copy-start.10 = (f32[34,768]{1,0:T(8,128)}, f32[34,768]{1,0:T(8,128)S(1)}, u32[]{:S(2)}) copy-start(f32[34,768]{1,0:T(8,128)S(1)} %collective-permute-done.2.south) | copy-start | bytes 313348
  56.7 8.5 %copy-start.11 = (f32[34,768]{1,0:T(8,128)}, f32[34,768]{1,0:T(8,128)S(1)}, u32[]{:S(2)}) copy-start(f32[34,768]{1,0:T(8,128)S(1)} %collective-permute-done.3.north) | copy-start | bytes 313348
  56.7 24.7 %all-to-all-start.1 = ((f32[64,32,128]{2,1,0:T(8,128)}), f32[64,32,128]{2,1,0:T(8,128)S(1)}, u32[]{:S(2)}, u32[]{:S(2)}) async-start(f32[64,32,128]{2,1,0:T(8,128)} %bitcast.12), calls=%async_computation.1 | async-start | bytes 2097152 | tf_op jit(solution)/shard_map/all_to_all | solution.py:429
  64.5 22.0 %copy-start.2 = (f32[1,32,450]{2,1,0:T(8,128)S(1)}, f32[1,32,450]{2,1,0:T(8,128)}, u32[]{:S(2)}) copy-start(f32[1,32,450]{2,1,0:T(8,128)} %param.11) | copy-start | bytes 172804
  64.6 22.0 %copy-start.3 = (s32[32,450]{1,0:T(8,128)S(1)}, s32[32,450]{1,0:T(8,128)}, u32[]{:S(2)}) copy-start(s32[32,450]{1,0:T(8,128)} %mask.3) | copy-start | bytes 172804
  65.2 21.4 %copy-start.4 = (s32[3]{0:T(128)S(1)}, s32[3]{0:T(128)}, u32[]{:S(2)}) copy-start(s32[3]{0:T(128)} %pad_add_fusion.flags) | copy-start | bytes 40
  81.5 5.1 %collective-permute-start.6 = (f32[64,32,128]{2,1,0:T(8,128)S(1)}, f32[64,32,128]{2,1,0:T(8,128)S(1)}, u32[]{:S(2)}, u32[]{:S(2)}) collective-permute-start(f32[64,32,128]{2,1,0:T(8,128)S(1)} %all-to-all-done.1), channel_id=1, source_target_pairs={{0,64},{64,0},{1,65},{65,1},{2,66},{66,2},{3,67},{67,3},{4,68},{68... | collective-permute-start | bytes 3145736 | tf_op jit(solution)/shard_map/ppermute | solution.py:483
  86.6 1.2 %copy-start.1 = (f32[16,32,450]{2,1,0:T(8,128)S(1)}, f32[16,32,450]{2,1,0:T(8,128)}, u32[]{:S(2)}) copy-start(f32[16,32,450]{2,1,0:T(8,128)} %mix.1.base) | copy-start | bytes 2764804

commit v4 on v3

--- a/solution.py
+++ b/solution.py
@@ -16,6 +16,8 @@
 FETCHES = (0, 30, 90, 150, 240, 330)
 ROW_BLOCK = 1024
 VMEM_LIMIT = 40 * 1024 * 1024
+SMALL_LIMIT = 16 * 1024 * 1024
+FULL_LIMIT = 60 * 1024 * 1024
 
 
 def spans(cols):
@@ -23,7 +25,7 @@
 
 
 def contribute_kernel(
-    source, tile, dest, state, weight, out, field, blocks, loose, picks, product, turned, ready, sems, sent
+    source, tile, dest, state, weight, out, blocks, loose, picks, product, turned, ready, sems, sent
 ):
     levels, rows, cols = state.shape
     entries = weight.shape[1]
@@ -32,8 +34,6 @@
     steps = -(-cols // BLOCK)
     lane = lax.broadcasted_iota(jnp.int32, (1, LANES), 1)
 
-    fetch_state = pltpu.make_async_copy(state, field, sent.at[QUARTERS])
-    fetch_state.start()
     fetches = {}
     for number, (low, high) in enumerate(zip(FETCHES, FETCHES[1:] + (cols,))):
         span = pl.ds(low, high - low)
@@ -56,9 +56,8 @@
             dests = jnp.where(here == e, dest[slot * 8 + e], dests)
         tail = jnp.where(below == 6, tiles, jnp.where(below == 7, dests, 0))
         turned[WIDTH:LANES, slot * LANES : (slot + 1) * LANES] = tail.astype(jnp.float32)
-    fetch_state.wait()
     for level in range(levels):
-        picked = jnp.dot(onehot, field[level].astype(jnp.bfloat16), preferred_element_type=jnp.float32)
+        picked = jnp.dot(onehot, state[level].astype(jnp.bfloat16), preferred_element_type=jnp.float32)
         for slot in range(2 * groups):
             loose[slot, level * 8 : level * 8 + 8, :] = picked[slot * 8 : slot * 8 + 8]
     for group in range(groups):
@@ -110,10 +109,9 @@
     away = pl.BlockSpec(memory_space=pltpu.HBM)
     return pl.pallas_call(
         contribute_kernel,
-        in_specs=[scalars, scalars, scalars, away, away],
+        in_specs=[scalars, scalars, scalars, pl.BlockSpec(memory_space=pltpu.VMEM), away],
         out_specs=away,
         scratch_shapes=[
-            pltpu.VMEM((levels, rows, cols), jnp.float32),
             pltpu.VMEM((steps * BLOCK, entries, cols), jnp.bfloat16),
             pltpu.VMEM((2 * groups, LANES, cols), jnp.float32),
             pltpu.VMEM((groups, 2 * LANES, cols), jnp.bfloat16),
@@ -121,7 +119,7 @@
             pltpu.VMEM((LANES, 2 * groups * LANES), jnp.float32),
             pltpu.VMEM((QUARTERS, levels, entries, LANES), jnp.float32),
             pltpu.SemaphoreType.DMA((len(FETCHES),)),
-            pltpu.SemaphoreType.DMA((QUARTERS + 1,)),
+            pltpu.SemaphoreType.DMA((QUARTERS,)),
         ],
         out_shape=jax.ShapeDtypeStruct((levels, QUARTERS, entries, LANES), jnp.float32),
         compiler_params=pltpu.CompilerParams(vmem_limit_bytes=VMEM_LIMIT),
@@ -162,7 +160,7 @@
     return pl.pallas_call(
         functools.partial(gather_rows_kernel, tile_rows),
         grid=(tiles * tile_rows // ROW_BLOCK,),
-        in_specs=[pl.BlockSpec((count, LANES), lambda i: (0, 0))],
+        in_specs=[pl.BlockSpec(memory_space=pltpu.VMEM)],
         out_specs=pl.BlockSpec((ROW_BLOCK, LANES), lambda i: (i, 0)),
         out_shape=jax.ShapeDtypeStruct((tiles * tile_rows, LANES), jnp.float32),
         scratch_shapes=[
@@ -208,6 +206,7 @@
         ],
         out_specs=[message, message],
         out_shape=[out, out],
+        compiler_params=pltpu.CompilerParams(vmem_limit_bytes=FULL_LIMIT),
         name="edges",
     )(field, field, field, diffusion)
 
@@ -218,10 +217,12 @@
     return jnp.concatenate(parts, axis=0)
 
 
-def rims_kernel(first, last, diffusion, west, east, low, high, three):
+def rims_kernel(first, last, diffusion, west, east, low, high, three, sides):
     levels, _, cols = first.shape
     rows = diffusion.shape[0]
     left, right = columns(west, rows), columns(east, rows)
+    sides[0] = left
+    sides[1] = right
     low[...] = jnp.zeros(low.shape, jnp.float32)
     high[...] = jnp.zeros(high.shape, jnp.float32)
     for out, block, start in ((low, first, 0), (high, last, rows - 2)):
@@ -243,6 +244,7 @@
     wide = LANES * (2 + -(-cols // LANES))
     rim = jax.ShapeDtypeStruct((2 * levels + 2, wide), jnp.float32)
     three = jax.ShapeDtypeStruct((3, levels, cols), jnp.float32)
+    sides = jax.ShapeDtypeStruct((2, rows, LANES), jnp.float32)
     whole = lambda shape: pl.BlockSpec(shape, lambda i: (0,) * len(shape))
     return pl.pallas_call(
         rims_kernel,
@@ -254,14 +256,15 @@
             whole(west.shape),
             whole(east.shape),
         ],
-        out_specs=[whole(rim.shape), whole(rim.shape), whole(three.shape)],
-        out_shape=[rim, rim, three],
+        out_specs=[whole(rim.shape), whole(rim.shape), whole(three.shape), whole(sides.shape)],
+        out_shape=[rim, rim, three, sides],
+        compiler_params=pltpu.CompilerParams(vmem_limit_bytes=FULL_LIMIT),
         name="rims",
     )(field, field, diffusion, west, east)
 
 
 def mix_kernel(
-    flags, field, diffusion, rate, mask, west, east, south, north, near, behind, ahead, fold_map, out, ext, coefs, folded, sides
+    flags, field, diffusion, rate, mask, sides, south, north, near, behind, ahead, fold_map, out, ext, coefs, folded
 ):
     part, rows, cols = field.shape
     levels = near.shape[1]
@@ -274,8 +277,6 @@
         ext[...] = jnp.zeros(ext.shape, jnp.float32)
         coefs[...] = jnp.zeros(coefs.shape, jnp.float32)
         coefs[own_rows, own_lanes] = diffusion[...] * active
-        sides[0] = columns(west, rows)
-        sides[1] = columns(east, rows)
         coefs[own_rows, LANES - 2 : LANES] = sides[0, :, 2 * levels : 2 * levels + 2]
         coefs[own_rows, LANES + cols : LANES + cols + 2] = sides[1, :, 2 * levels : 2 * levels + 2]
         coefs[6:8, :] = south[2 * levels : 2 * levels + 2, :]
@@ -331,7 +332,7 @@
         out[local] = twice[own_rows, own_lanes] - rate[...] * active * field[local]
 
 
-def mix(flags, field, diffusion, rate, mask, west, east, south, north, near, behind, ahead, fold_map):
+def mix(flags, field, diffusion, rate, mask, sides, south, north, near, behind, ahead, fold_map):
     levels, rows, cols = field.shape
     part = 4
     wide = south.shape[1]
@@ -346,8 +347,7 @@
             whole((rows, cols)),
             whole((rows, cols)),
             whole((rows, cols)),
-            whole(west.shape),
-            whole(east.shape),
+            whole(sides.shape),
             whole(south.shape),
             whole(north.shape),
             whole(near.shape),
@@ -360,29 +360,23 @@
             pltpu.VMEM((part, rows + 16, wide), jnp.float32),
             pltpu.VMEM((rows + 16, wide), jnp.float32),
             pltpu.VMEM((levels, cols), jnp.float32),
-            pltpu.VMEM((2, rows, LANES), jnp.float32),
         ],
         out_shape=jax.ShapeDtypeStruct(field.shape, jnp.float32),
+        compiler_params=pltpu.CompilerParams(vmem_limit_bytes=SMALL_LIMIT),
         name="mix",
-    )(flags, field, diffusion, rate, mask, west, east, south, north, near, behind, ahead, fold_map[None])
-
-
-def finish_kernel(flags, received, base, rate, mask, out, inner, outer, fetched, stored):
+    )(flags, field, diffusion, rate, mask, sides, south, north, near, behind, ahead, fold_map[None])
+
+
+def finish_kernel(flags, received, base, rate, mask, out, outer, stored):
     levels, rows, cols = base.shape
-    parts = fetched.shape[0]
+    parts = stored.shape[0]
     part = levels // parts
-    fetches = []
-    for number in range(parts):
-        span = pl.ds(number * part, part)
-        fetches.append(pltpu.make_async_copy(base.at[span], inner.at[span], fetched.at[number]))
-        fetches[-1].start()
     pull = coefficient(flags, rate[...], mask[...])
     stores = []
     for number in range(parts):
-        fetches[number].wait()
         for level in range(number * part, (number + 1) * part):
             pieces = [received[level * QUARTERS + q][:, : high - low] for q, (low, high) in enumerate(spans(cols))]
-            outer[level] = inner[level] + pull * jnp.concatenate(pieces, axis=1)
+            outer[level] = base[level] + pull * jnp.concatenate(pieces, axis=1)
         span = pl.ds(number * part, part)
         stores.append(pltpu.make_async_copy(outer.at[span], out.at[span], stored.at[number]))
         stores[-1].start()
@@ -393,19 +387,13 @@
 def finish(flags, received, base, rate, mask):
     parts = 4
     inside = pl.BlockSpec(memory_space=pltpu.VMEM)
-    away = pl.BlockSpec(memory_space=pltpu.HBM)
     return pl.pallas_call(
         finish_kernel,
-        in_specs=[pl.BlockSpec(memory_space=pltpu.SMEM), inside, away, inside, inside],
-        out_specs=away,
+        in_specs=[pl.BlockSpec(memory_space=pltpu.SMEM), inside, inside, inside, inside],
+        out_specs=pl.BlockSpec(memory_space=pltpu.HBM),
         out_shape=jax.ShapeDtypeStruct(base.shape, jnp.float32),
-        scratch_shapes=[
-            pltpu.VMEM(base.shape, jnp.float32),
-            pltpu.VMEM(base.shape, jnp.float32),
-            pltpu.SemaphoreType.DMA((parts,)),
-            pltpu.SemaphoreType.DMA((parts,)),
-        ],
-        compiler_params=pltpu.CompilerParams(vmem_limit_bytes=VMEM_LIMIT),
+        scratch_shapes=[pltpu.VMEM(base.shape, jnp.float32), pltpu.SemaphoreType.DMA((parts,))],
+        compiler_params=pltpu.CompilerParams(vmem_limit_bytes=SMALL_LIMIT),
         name="finish",
     )(flags, received, base, rate, mask)
 
@@ -457,7 +445,7 @@
     pieces, west, east = lax.optimization_barrier((pieces, west, east))
     arrived = spread(pieces.reshape(tiles, entries, LANES), TILE_AXES)
 
-    low, high, near = rims(field, diffusion[0], west, east)
+    low, high, near, sides = rims(field, diffusion[0], west, east)
     south = shift(high, "tx", True, False)
     north = shift(low, "tx", False, False)
     behind = across(near, 3)
@@ -470,8 +458,7 @@
         diffusion[0],
         exchange_rate[0],
         land_mask,
-        west,
-        east,
+        sides,
         south,
         north,
         near,

time: 90.2 us -> 89.1 us (0.988)
  waiting for transfers between devices: 28.2 us -> 30.3 us
  Pallas kernels: 27.7 us -> 26 us
  local copies, waits for them, and re-layouts: 1.87 us -> 0.66 us
    all_to_all x2, waiting for transfers between devices: 25.9 us -> 27.8 us  [spread(): return lax.all_to_all(value, axes, split_axis=0, concat_axis=0, tiled=True)]
    pallas_call x1, Pallas kernels: 5.93 us -> 4.28 us  [mix(): pl.pallas_call(mix_kernel, grid=(levels // part,), in_specs=[pl.BlockSpec...]
    unnamed x28 -> x26, local copies, waits for them, and re-layouts: 1.87 us -> 0.66 us
  transfers between devices with their start and end apart: 9 -> 9, of which waited for: 3 -> 3; matrix products, arithmetic and copies ran while one was open for 1% -> 0% of each run, Pallas kernels for 26% -> 25%
where the time goes in v4:
time: 89.1 us; the launch traced here: 88.7 us
  starting transfers between devices  31.4 us (35%)
  waiting for transfers between devices  30.3 us (34%)
  Pallas kernels  26 us (29%)
    all_to_all x2, waiting for transfers between devices, spread(): return lax.all_to_all(value, axes, split_axis=0, concat_axis=0, tiled=True)  27.8 us
    all_to_all x2, starting transfers between devices, spread(): return lax.all_to_all(value, axes, split_axis=0, concat_axis=0, tiled=True)  16.4 us
    pallas_call x1, Pallas kernels, contribute(): pl.pallas_call(contribute_kernel, in_specs=[scalars, scalars, scalars, pl...  11.3 us
    ppermute x4, starting transfers between devices, shift(): return lax.ppermute(value, axis, pairs)  10.8 us
    pallas_call x1, Pallas kernels, gather_rows(): pl.pallas_call(functools.partial(gather_rows_kernel, tile_rows), grid=(ti...  4.75 us
    pallas_call x1, Pallas kernels, mix(): pl.pallas_call(mix_kernel, grid=(levels // part,), in_specs=[pl.BlockSpec...  4.28 us
    ppermute x1, starting transfers between devices, body(): received = lax.ppermute(received, 'mp', [(0, 1), (1, 0)])  2.92 us
    ppermute x1, waiting for transfers between devices, body(): received = lax.ppermute(received, 'mp', [(0, 1), (1, 0)])  2.5 us
  transfers between devices with their start and end apart: 9, of which 3 were waited for; matrix products, arithmetic and copies ran while one was open for 0% of the time, Pallas kernels for 25%

profile of v4, /device:TPU:1, one launch (start us, length us, event | category | flops | bytes accessed | tf_op | source)
XLA Modules:
  0.0 88.7 jit_solution(3632824713446215018)
XLA Ops:
  0.0 2.0 %edges.1 = (f32[24,512]{1,0:T(8,128)}, f32[24,512]{1,0:T(8,128)}) custom-call(f32[16,32,450]{2,1,0:T(8,128)} %bitcast.17, f32[16,32,450]{2,1,0:T(8,128)} %bitcast.18, f32[16,32,450]{2,1,0:T(8,128)} %bitcast.19, f32[32,450]{1,0:T(8,128)} %bitcast.25), custom_call_target="tpu_custom_call" | custom-call | tf_op jit(solution)/shard_map/edges/pallas_call | solution.py:198
  2.1 4.4 %collective-permute-start = (f32[24,512]{1,0:T(8,128)}, f32[24,512]{1,0:T(8,128)S(1)}, u32[]{:S(2)}, u32[]{:S(2)}) collective-permute-start(f32[24,512]{1,0:T(8,128)} %get-tuple-element.21), channel_id=1, source_target_pairs={{0,1},{1,2},{2,3},{3,4},{4,5},{5,6},{6,7},{7,0},{8,9},{9,10},{10,1... | collective-permute-start | bytes 147464 | tf_op jit(solution)/shard_map/ppermute | solution.py:406
  6.5 2.2 %collective-permute-start.1 = (f32[24,512]{1,0:T(8,128)}, f32[24,512]{1,0:T(8,128)S(1)}, u32[]{:S(2)}, u32[]{:S(2)}) collective-permute-start(f32[24,512]{1,0:T(8,128)} %get-tuple-element.22), channel_id=1, source_target_pairs={{1,0},{2,1},{3,2},{4,3},{5,4},{6,5},{7,6},{0,7},{9,8},{10,9},{11,1... | collective-permute-start | bytes 147464 | tf_op jit(solution)/shard_map/ppermute | solution.py:406
  8.7 11.3 %contribute.1 = f32[16,4,48,128]{3,2,1,0:T(8,128)} custom-call(s32[48]{0:T(128)S(1)} %bitcast.31, s32[48]{0:T(128)S(1)} %bitcast.32, s32[48]{0:T(128)S(1)} %bitcast.33, f32[16,32,450]{2,1,0:T(8,128)S(1)} %bitcast.22, bf16[450,48,450]{2,1,0:T(8,128)(2,1)} %bitcast.34), custom_call_target="tpu_custom_call" | custom-call | flops 311040000 | bytes 19440000 | tf_op jit(solution)/shard_map/contribute/pallas_call | solution.py:110
  20.0 0.0 collective-permute-done.west
  20.0 0.0 copy-start.12
  20.0 0.6 copy-done.11
  20.6 0.0 copy-done.12
  20.6 8.3 %all-to-all-start = ((f32[64,48,128]{2,1,0:T(8,128)}), f32[64,48,128]{2,1,0:T(8,128)S(1)}, u32[]{:S(2)}, u32[]{:S(2)}) async-start(f32[64,48,128]{2,1,0:T(8,128)} %bitcast.10), calls=%async_computation | async-start | bytes 3145728 | tf_op jit(solution)/shard_map/all_to_all | solution.py:417
  29.0 1.9 %rims.1 = (f32[34,768]{1,0:T(8,128)}, f32[34,768]{1,0:T(8,128)}, f32[3,16,450]{2,1,0:T(8,128)}, f32[2,32,128]{2,1,0:T(8,128)}) custom-call(f32[16,32,450]{2,1,0:T(8,128)} %bitcast.20, f32[16,32,450]{2,1,0:T(8,128)} %bitcast.21, f32[32,450]{1,0:T(8,128)} %bitcast.26, f32[24,512]{1,0:T(8,128)} %copy-done.11, f32[24,512]{1,0:T(8,128)} %copy-done.12), custom_call_target="tpu_custom_call" | custom-call | tf_op jit(solution)/shard_map/rims/pallas_call | solution.py:249
  30.9 2.9 %collective-permute-start.2 = (f32[34,768]{1,0:T(8,128)}, f32[34,768]{1,0:T(8,128)S(1)}, u32[]{:S(2)}, u32[]{:S(2)}) collective-permute-start(f32[34,768]{1,0:T(8,128)} %get-tuple-element.26), channel_id=1, source_target_pairs={{0,8},{8,16},{16,24},{24,32},{32,40},{40,48},{48,56},{1,9},{9,17},... | collective-permute-start | bytes 313352 | tf_op jit(solution)/shard_map/ppermute | solution.py:406
  33.8 1.3 %collective-permute-start.3 = (f32[34,768]{1,0:T(8,128)}, f32[34,768]{1,0:T(8,128)S(1)}, u32[]{:S(2)}, u32[]{:S(2)}) collective-permute-start(f32[34,768]{1,0:T(8,128)} %get-tuple-element.27), channel_id=1, source_target_pairs={{8,0},{16,8},{24,16},{32,24},{40,32},{48,40},{56,48},{9,1},{17,9},... | collective-permute-start | bytes 313352 | tf_op jit(solution)/shard_map/ppermute | solution.py:406
  35.1 0.7 collective-permute-start.5
  35.8 0.7 collective-permute-start.4
  36.5 15.6 %all-to-all-done = f32[64,48,128]{2,1,0:T(8,128)S(1)} async-done(((f32[64,48,128]{2,1,0:T(8,128)}), f32[64,48,128]{2,1,0:T(8,128)S(1)}, u32[]{:S(2)}, u32[]{:S(2)}) %all-to-all-start) | async-done | bytes 1572896 | tf_op jit(solution)/shard_map/all_to_all | solution.py:417
  52.1 4.8 %gather_rows.1 = f32[2048,128]{1,0:T(8,128)} custom-call(f32[3072,128]{1,0:T(8,128)S(1)} %bitcast.24), custom_call_target="tpu_custom_call" | custom-call | tf_op jit(solution)/shard_map/gather_rows/pallas_call | solution.py:160
  56.8 0.0 copy-start.7
  56.9 8.0 %all-to-all-start.1 = ((f32[64,32,128]{2,1,0:T(8,128)}), f32[64,32,128]{2,1,0:T(8,128)}, u32[]{:S(2)}, u32[]{:S(2)}) async-start(f32[64,32,128]{2,1,0:T(8,128)} %bitcast.12), calls=%async_computation.1 | async-start | bytes 2097152 | tf_op jit(solution)/shard_map/all_to_all | solution.py:417
  65.0 0.1 pad_add_fusion.flags
  65.1 4.3 %mix.1.base = f32[16,32,450]{2,1,0:T(8,128)S(1)} custom-call(s32[3]{0:T(128)S(1)} %pad_add_fusion.flags, f32[16,32,450]{2,1,0:T(8,128)S(1)} %bitcast.23, f32[32,450]{1,0:T(8,128)S(1)} %bitcast.27, f32[32,450]{1,0:T(8,128)S(1)} %bitcast.28, s32[32,450]{1,0:T(8,128)S(1)} %copy-done.4, f32[2,32,128]{2,1,0:T(8,128)S(1)} %copy-done.6, ...), custom_call_target="tpu_custom_call" | custom-call | tf_op jit(solution)/shard_map/mix/pallas_call | solution.py:341
  69.4 12.2 %all-to-all-done.1 = f32[64,32,128]{2,1,0:T(8,128)} async-done(((f32[64,32,128]{2,1,0:T(8,128)}), f32[64,32,128]{2,1,0:T(8,128)}, u32[]{:S(2)}, u32[]{:S(2)}) %all-to-all-start.1) | async-done | bytes 1048608 | tf_op jit(solution)/shard_map/all_to_all | solution.py:417
  81.6 2.9 %collective-permute-start.6 = (f32[64,32,128]{2,1,0:T(8,128)}, f32[64,32,128]{2,1,0:T(8,128)S(1)}, u32[]{:S(2)}, u32[]{:S(2)}) collective-permute-start(f32[64,32,128]{2,1,0:T(8,128)} %all-to-all-done.1), channel_id=1, source_target_pairs={{0,64},{64,0},{1,65},{65,1},{2,66},{66,2},{3,67},{67,3},{4,68},{68... | collective-permute-start | bytes 3145736 | tf_op jit(solution)/shard_map/ppermute | solution.py:470
  84.6 2.5 %collective-permute-done.6.received = f32[64,32,128]{2,1,0:T(8,128)S(1)} collective-permute-done((f32[64,32,128]{2,1,0:T(8,128)}, f32[64,32,128]{2,1,0:T(8,128)S(1)}, u32[]{:S(2)}, u32[]{:S(2)}) %collective-permute-start.6) | collective-permute-done | bytes 1048608 | tf_op jit(solution)/shard_map/ppermute | solution.py:470
  87.1 1.7 %finish.1 = f32[16,32,450]{2,1,0:T(8,128)} custom-call(s32[3]{0:T(128)S(1)} %pad_add_fusion.flags, f32[64,32,128]{2,1,0:T(8,128)S(1)} %collective-permute-done.6.received, f32[16,32,450]{2,1,0:T(8,128)S(1)} %mix.1.base, f32[32,450]{1,0:T(8,128)S(1)} %bitcast.29, s32[32,450]{1,0:T(8,128)S(1)} %copy-done.4), custom_call_target="tpu_custom_call" | custom-call | tf_op jit(solution)/shard_map/finish/pallas_call | solution.py:390
  (27 shorter events, 0.1 us)
Async XLA Ops:
  0.0 8.7 %copy-start = (f32[1,16,32,450]{3,2,1,0:T(8,128)S(1)}, f32[1,16,32,450]{3,2,1,0:T(8,128)}, u32[]{:S(2)}) copy-start(f32[1,16,32,450]{3,2,1,0:T(8,128)} %param.9) | copy-start | bytes 2764804
  0.0 8.7 %copy-start.8 = (s32[1,1,48]{2,1,0:T(1,128)S(1)}, s32[1,1,48]{2,1,0:T(1,128)}, u32[]{:S(2)}) copy-start(s32[1,1,48]{2,1,0:T(1,128)} %param.15) | copy-start | bytes 580
  0.0 8.7 %copy-start.9 = (s32[1,1,48,1]{2,3,1,0:T(1,128)S(1)}, s32[1,1,48,1]{2,3,1,0:T(1,128)}, u32[]{:S(2)}) copy-start(s32[1,1,48,1]{2,3,1,0:T(1,128)} %param.14) | copy-start | bytes 580
  0.0 8.7 %copy-start.10 = (s32[1,1,48]{2,1,0:T(1,128)S(1)}, s32[1,1,48]{2,1,0:T(1,128)}, u32[]{:S(2)}) copy-start(s32[1,1,48]{2,1,0:T(1,128)} %param.16) | copy-start | bytes 580
  2.1 17.9 %collective-permute-start = (f32[24,512]{1,0:T(8,128)}, f32[24,512]{1,0:T(8,128)S(1)}, u32[]{:S(2)}, u32[]{:S(2)}) collective-permute-start(f32[24,512]{1,0:T(8,128)} %get-tuple-element.21), channel_id=1, source_target_pairs={{0,1},{1,2},{2,3},{3,4},{4,5},{5,6},{6,7},{7,0},{8,9},{9,10},{10,1... | collective-permute-start | bytes 147464 | tf_op jit(solution)/shard_map/ppermute | solution.py:406
  6.5 13.5 %collective-permute-start.1 = (f32[24,512]{1,0:T(8,128)}, f32[24,512]{1,0:T(8,128)S(1)}, u32[]{:S(2)}, u32[]{:S(2)}) collective-permute-start(f32[24,512]{1,0:T(8,128)} %get-tuple-element.22), channel_id=1, source_target_pairs={{1,0},{2,1},{3,2},{4,3},{5,4},{6,5},{7,6},{0,7},{9,8},{10,9},{11,1... | collective-permute-start | bytes 147464 | tf_op jit(solution)/shard_map/ppermute | solution.py:406
  20.0 0.6 copy-start.11
  20.0 0.6 copy-start.12
  20.6 31.4 %all-to-all-start = ((f32[64,48,128]{2,1,0:T(8,128)}), f32[64,48,128]{2,1,0:T(8,128)S(1)}, u32[]{:S(2)}, u32[]{:S(2)}) async-start(f32[64,48,128]{2,1,0:T(8,128)} %bitcast.10), calls=%async_computation | async-start | bytes 3145728 | tf_op jit(solution)/shard_map/all_to_all | solution.py:417
  30.9 26.0 %collective-permute-start.2 = (f32[34,768]{1,0:T(8,128)}, f32[34,768]{1,0:T(8,128)S(1)}, u32[]{:S(2)}, u32[]{:S(2)}) collective-permute-start(f32[34,768]{1,0:T(8,128)} %get-tuple-element.26), channel_id=1, source_target_pairs={{0,8},{8,16},{16,24},{24,32},{32,40},{40,48},{48,56},{1,9},{9,17},... | collective-permute-start | bytes 313352 | tf_op jit(solution)/shard_map/ppermute | solution.py:406
  33.8 23.1 %collective-permute-start.3 = (f32[34,768]{1,0:T(8,128)}, f32[34,768]{1,0:T(8,128)S(1)}, u32[]{:S(2)}, u32[]{:S(2)}) collective-permute-start(f32[34,768]{1,0:T(8,128)} %get-tuple-element.27), channel_id=1, source_target_pairs={{8,0},{16,8},{24,16},{32,24},{40,32},{48,40},{56,48},{9,1},{17,9},... | collective-permute-start | bytes 313352 | tf_op jit(solution)/shard_map/ppermute | solution.py:406
  35.1 21.7 %collective-permute-start.5 = (f32[3,16,450]{2,1,0:T(8,128)}, f32[3,16,450]{2,1,0:T(8,128)S(1)}, u32[]{:S(2)}, u32[]{:S(2)}) collective-permute-start(f32[3,16,450]{2,1,0:T(8,128)} %get-tuple-element.28.near), channel_id=1, source_target_pairs={{120,125},{121,126},{122,127},{123,120},{124,121},{125,122},{126,1... | collective-permute-start | bytes 259208 | tf_op jit(solution)/shard_map/ppermute | solution.py:413
  35.8 21.1 %collective-permute-start.4 = (f32[3,16,450]{2,1,0:T(8,128)}, f32[3,16,450]{2,1,0:T(8,128)S(1)}, u32[]{:S(2)}, u32[]{:S(2)}) collective-permute-start(f32[3,16,450]{2,1,0:T(8,128)} %get-tuple-element.28.near), channel_id=1, source_target_pairs={{120,123},{121,124},{122,125},{123,126},{124,127},{125,120},{126,1... | collective-permute-start | bytes 259208 | tf_op jit(solution)/shard_map/ppermute | solution.py:413
  56.8 8.2 %copy-start.1 = (f32[1,16,32,450]{3,2,1,0:T(8,128)S(1)}, f32[1,16,32,450]{3,2,1,0:T(8,128)}, u32[]{:S(2)}) copy-start(f32[1,16,32,450]{3,2,1,0:T(8,128)} %param.9) | copy-start | bytes 2764804
  56.8 8.2 %copy-start.2 = (f32[1,32,450]{2,1,0:T(8,128)S(1)}, f32[1,32,450]{2,1,0:T(8,128)}, u32[]{:S(2)}) copy-start(f32[1,32,450]{2,1,0:T(8,128)} %param.10) | copy-start | bytes 172804
  56.8 8.2 %copy-start.3 = (f32[1,32,450]{2,1,0:T(8,128)S(1)}, f32[1,32,450]{2,1,0:T(8,128)}, u32[]{:S(2)}) copy-start(f32[1,32,450]{2,1,0:T(8,128)} %param.11) | copy-start | bytes 172804
  56.8 8.2 %copy-start.4 = (s32[32,450]{1,0:T(8,128)S(1)}, s32[32,450]{1,0:T(8,128)}, u32[]{:S(2)}) copy-start(s32[32,450]{1,0:T(8,128)} %mask.3) | copy-start | bytes 172804
  56.8 8.2 %copy-start.5 = (f32[3,16,450]{2,1,0:T(8,128)S(1)}, f32[3,16,450]{2,1,0:T(8,128)}, u32[]{:S(2)}) copy-start(f32[3,16,450]{2,1,0:T(8,128)} %get-tuple-element.28.near) | copy-start | bytes 259204
  56.8 8.2 %copy-start.6 = (f32[2,32,128]{2,1,0:T(8,128)S(1)}, f32[2,32,128]{2,1,0:T(8,128)}, u32[]{:S(2)}) copy-start(f32[2,32,128]{2,1,0:T(8,128)} %get-tuple-element.30.sides) | copy-start | bytes 98308
  56.8 8.2 %copy-start.7 = (s32[450]{0:T(512)S(1)}, s32[450]{0:T(512)}, u32[]{:S(2)}) copy-start(s32[450]{0:T(512)} %param.13) | copy-start | bytes 5404
  56.9 24.7 %all-to-all-start.1 = ((f32[64,32,128]{2,1,0:T(8,128)}), f32[64,32,128]{2,1,0:T(8,128)}, u32[]{:S(2)}, u32[]{:S(2)}) async-start(f32[64,32,128]{2,1,0:T(8,128)} %bitcast.12), calls=%async_computation.1 | async-start | bytes 2097152 | tf_op jit(solution)/shard_map/all_to_all | solution.py:417
  81.6 5.4 %collective-permute-start.6 = (f32[64,32,128]{2,1,0:T(8,128)}, f32[64,32,128]{2,1,0:T(8,128)S(1)}, u32[]{:S(2)}, u32[]{:S(2)}) collective-permute-start(f32[64,32,128]{2,1,0:T(8,128)} %all-to-all-done.1), channel_id=1, source_target_pairs={{0,64},{64,0},{1,65},{65,1},{2,66},{66,2},{3,67},{67,3},{4,68},{68... | collective-permute-start | bytes 3145736 | tf_op jit(solution)/shard_map/ppermute | solution.py:470

commit v5 on v4

--- a/solution.py
+++ b/solution.py
@@ -10,14 +10,15 @@
 TILE_AXES = ("tx", "ty")
 QUARTERS = 4
 LANES = 128
+SIDE = 2
 PACK = 16
 WIDTH = 120
 BLOCK = 30
 FETCHES = (0, 30, 90, 150, 240, 330)
-ROW_BLOCK = 1024
+ROW_BLOCK = 256
 VMEM_LIMIT = 40 * 1024 * 1024
 SMALL_LIMIT = 16 * 1024 * 1024
-FULL_LIMIT = 60 * 1024 * 1024
+FULL_LIMIT = 59 * 1024 * 1024
 
 
 def spans(cols):
@@ -133,35 +134,29 @@
 
 
 def gather_rows_kernel(tile_rows, values, out, halves, labels):
-    block = pl.program_id(0)
-
-    @pl.when(block == 0)
-    def prepare():
-        x = values[...]
-        high = x.astype(jnp.bfloat16)
-        low = (x - high.astype(jnp.float32)).astype(jnp.bfloat16)
-        halves[:, :LANES] = high
-        halves[:, LANES:] = low
-        lane = lax.broadcasted_iota(jnp.int32, (8, LANES), 1)
-        pick = jnp.where(lane == LANES - 2, float(tile_rows), jnp.where(lane == LANES - 1, 1.0, 0.0))
-        labels[...] = lax.dot_general(
-            pick.astype(jnp.bfloat16), high, (((1,), (1,)), ((), ())), preferred_element_type=jnp.float32
-        ).astype(jnp.int32)
-
     count = values.shape[0]
-    row = lax.broadcasted_iota(jnp.int32, (ROW_BLOCK, count), 0) + block * ROW_BLOCK
-    onehot = jnp.where(row == labels[0:1, :], 1.0, 0.0).astype(jnp.bfloat16)
-    sums = jnp.dot(onehot, halves[...], preferred_element_type=jnp.float32)
-    out[...] = sums[:, :LANES] + sums[:, LANES:]
+    x = values[...]
+    high = x.astype(jnp.bfloat16)
+    halves[:, :LANES] = high
+    halves[:, LANES:] = (x - high.astype(jnp.float32)).astype(jnp.bfloat16)
+    lane = lax.broadcasted_iota(jnp.int32, (8, LANES), 1)
+    pick = jnp.where(lane == LANES - 2, float(tile_rows), jnp.where(lane == LANES - 1, 1.0, 0.0))
+    labels[...] = lax.dot_general(
+        pick.astype(jnp.bfloat16), high, (((1,), (1,)), ((), ())), preferred_element_type=jnp.float32
+    ).astype(jnp.int32)
+    for block in range(out.shape[0] // ROW_BLOCK):
+        row = lax.broadcasted_iota(jnp.int32, (ROW_BLOCK, count), 0) + block * ROW_BLOCK
+        onehot = jnp.where(row == labels[0:1, :], 1.0, 0.0).astype(jnp.bfloat16)
+        both = jnp.dot(onehot, halves[...], preferred_element_type=jnp.float32)
+        out[block * ROW_BLOCK : (block + 1) * ROW_BLOCK, :] = both[:, :LANES] + both[:, LANES:]
 
 
 def gather_rows(values, tiles, tile_rows):
     count = values.shape[0]
     return pl.pallas_call(
         functools.partial(gather_rows_kernel, tile_rows),
-        grid=(tiles * tile_rows // ROW_BLOCK,),
         in_specs=[pl.BlockSpec(memory_space=pltpu.VMEM)],
-        out_specs=pl.BlockSpec((ROW_BLOCK, LANES), lambda i: (i, 0)),
+        out_specs=pl.BlockSpec(memory_space=pltpu.VMEM),
         out_shape=jax.ShapeDtypeStruct((tiles * tile_rows, LANES), jnp.float32),
         scratch_shapes=[
             pltpu.VMEM((count, 2 * LANES), jnp.bfloat16),
@@ -229,11 +224,11 @@
         for level in range(levels + 1):
             place = pl.ds(2 * level, 2)
             if level < levels:
-                out[place, LANES : LANES + cols] = block[level, start % 8 : start % 8 + 2, :]
+                out[place, SIDE : SIDE + cols] = block[level, start % 8 : start % 8 + 2, :]
             else:
-                out[place, LANES : LANES + cols] = diffusion[start : start + 2, :]
-            out[place, LANES - 2 : LANES] = left[start : start + 2, 2 * level : 2 * level + 2]
-            out[place, LANES + cols : LANES + cols + 2] = right[start : start + 2, 2 * level : 2 * level + 2]
+                out[place, SIDE : SIDE + cols] = diffusion[start : start + 2, :]
+            out[place, SIDE - 2 : SIDE] = left[start : start + 2, 2 * level : 2 * level + 2]
+            out[place, SIDE + cols : SIDE + cols + 2] = right[start : start + 2, 2 * level : 2 * level + 2]
     three[0] = west[:levels, :cols]
     three[1] = jnp.concatenate([last[level, 7:8, :] for level in range(levels)], axis=0)
     three[2] = east[:levels, :cols]
@@ -241,7 +236,7 @@
 
 def rims(field, diffusion, west, east):
     levels, rows, cols = field.shape
-    wide = LANES * (2 + -(-cols // LANES))
+    wide = LANES * -(-(cols + 2 * SIDE) // LANES)
     rim = jax.ShapeDtypeStruct((2 * levels + 2, wide), jnp.float32)
     three = jax.ShapeDtypeStruct((3, levels, cols), jnp.float32)
     sides = jax.ShapeDtypeStruct((2, rows, LANES), jnp.float32)
@@ -266,23 +261,19 @@
 def mix_kernel(
     flags, field, diffusion, rate, mask, sides, south, north, near, behind, ahead, fold_map, out, ext, coefs, folded
 ):
-    part, rows, cols = field.shape
-    levels = near.shape[1]
-    step = pl.program_id(0)
-    own_rows, own_lanes = slice(8, 8 + rows), slice(LANES, LANES + cols)
+    levels, rows, cols = field.shape
+    own_rows, own_lanes = slice(8, 8 + rows), slice(SIDE, SIDE + cols)
     active = coefficient(flags, 1.0, mask[...])
-
-    @pl.when(step == 0)
-    def prepare():
-        ext[...] = jnp.zeros(ext.shape, jnp.float32)
-        coefs[...] = jnp.zeros(coefs.shape, jnp.float32)
-        coefs[own_rows, own_lanes] = diffusion[...] * active
-        coefs[own_rows, LANES - 2 : LANES] = sides[0, :, 2 * levels : 2 * levels + 2]
-        coefs[own_rows, LANES + cols : LANES + cols + 2] = sides[1, :, 2 * levels : 2 * levels + 2]
-        coefs[6:8, :] = south[2 * levels : 2 * levels + 2, :]
-        coefs[8 + rows : 10 + rows, :] = north[2 * levels : 2 * levels + 2, :]
-
-    @pl.when(jnp.logical_and(step == 0, flags[1] == 1))
+    pull = rate[...] * active
+    ext[...] = jnp.zeros(ext.shape, jnp.float32)
+    coefs[...] = jnp.zeros(coefs.shape, jnp.float32)
+    coefs[own_rows, own_lanes] = diffusion[...] * active
+    coefs[own_rows, SIDE - 2 : SIDE] = sides[0, :, 2 * levels : 2 * levels + 2]
+    coefs[own_rows, SIDE + cols : SIDE + cols + 2] = sides[1, :, 2 * levels : 2 * levels + 2]
+    coefs[6:8, :] = south[2 * levels : 2 * levels + 2, :]
+    coefs[8 + rows : 10 + rows, :] = north[2 * levels : 2 * levels + 2, :]
+
+    @pl.when(flags[1] == 1)
     def fold():
         total = jnp.zeros((3 * levels, cols), jnp.float32)
         place = lax.broadcasted_iota(jnp.int32, (cols, cols), 0)
@@ -305,59 +296,35 @@
         around = around + pltpu.roll(f, 1, 1) + pltpu.roll(f, wide - 1, 1)
         return f + c * (around - 4.0 * f)
 
-    for local in range(part):
-        ext[local, own_rows, own_lanes] = field[local]
-
-    for number in range(levels // part):
-
-        @pl.when(step == number)
-        def outside():
-            for local in range(part):
-                level = number * part + local
-                pair = slice(2 * level, 2 * level + 2)
-                ext[local, own_rows, LANES - 2 : LANES] = sides[0, :, pair]
-                ext[local, own_rows, LANES + cols : LANES + cols + 2] = sides[1, :, pair]
-                ext[local, 6:8, :] = south[pair, :]
-                ext[local, 8 + rows : 10 + rows, :] = north[pair, :]
-
-        @pl.when(jnp.logical_and(step == number, flags[1] == 1))
-        def folded_rows():
-            for local in range(part):
-                level = number * part + local
-                ext[local, 8 + rows : 9 + rows, own_lanes] = folded[level : level + 1, :]
-
-    for local in range(part):
-        once = sweep(ext[local], coefs[...])
+    for level in range(levels):
+        pair = slice(2 * level, 2 * level + 2)
+        ext[level, own_rows, own_lanes] = field[level]
+        ext[level, own_rows, SIDE - 2 : SIDE] = sides[0, :, pair]
+        ext[level, own_rows, SIDE + cols : SIDE + cols + 2] = sides[1, :, pair]
+        ext[level, 6:8, :] = south[pair, :]
+        ext[level, 8 + rows : 10 + rows, :] = north[pair, :]
+
+    @pl.when(flags[1] == 1)
+    def folded_rows():
+        for level in range(levels):
+            ext[level, 8 + rows : 9 + rows, own_lanes] = folded[level : level + 1, :]
+
+    for level in range(levels):
+        once = sweep(ext[level], coefs[...])
         twice = sweep(once, coefs[...] * again)
-        out[local] = twice[own_rows, own_lanes] - rate[...] * active * field[local]
+        out[level] = twice[own_rows, own_lanes] - pull * field[level]
 
 
 def mix(flags, field, diffusion, rate, mask, sides, south, north, near, behind, ahead, fold_map):
     levels, rows, cols = field.shape
-    part = 4
     wide = south.shape[1]
-    whole = lambda shape: pl.BlockSpec(shape, lambda i: (0,) * len(shape))
-    block = pl.BlockSpec((part, rows, cols), lambda i: (i, 0, 0))
+    inside = pl.BlockSpec(memory_space=pltpu.VMEM)
     return pl.pallas_call(
         mix_kernel,
-        grid=(levels // part,),
-        in_specs=[
-            pl.BlockSpec(memory_space=pltpu.SMEM),
-            block,
-            whole((rows, cols)),
-            whole((rows, cols)),
-            whole((rows, cols)),
-            whole(sides.shape),
-            whole(south.shape),
-            whole(north.shape),
-            whole(near.shape),
-            whole(behind.shape),
-            whole(ahead.shape),
-            whole((1, cols)),
-        ],
-        out_specs=block,
+        in_specs=[pl.BlockSpec(memory_space=pltpu.SMEM)] + [inside] * 11,
+        out_specs=inside,
         scratch_shapes=[
-            pltpu.VMEM((part, rows + 16, wide), jnp.float32),
+            pltpu.VMEM((levels, rows + 16, wide), jnp.float32),
             pltpu.VMEM((rows + 16, wide), jnp.float32),
             pltpu.VMEM((levels, cols), jnp.float32),
         ],

time: 89.1 us -> 87.5 us (0.982)
  waiting for transfers between devices: 30.3 us -> 28.3 us
    all_to_all x2, waiting for transfers between devices: 27.8 us -> 25.8 us  [spread(): return lax.all_to_all(value, axes, split_axis=0, concat_axis=0, tiled=True)]
    all_to_all x2, starting transfers between devices: 16.4 us -> 14.7 us  [spread(): return lax.all_to_all(value, axes, split_axis=0, concat_axis=0, tiled=True)]
    ppermute x1, starting transfers between devices: 2.92 us -> 4.12 us  [body(): received = lax.ppermute(received, 'mp', [(0, 1), (1, 0)])]
  transfers between devices with their start and end apart: 9 -> 9, of which waited for: 3 -> 3; matrix products, arithmetic and copies ran while one was open for 0% -> 0% of each run, Pallas kernels for 25% -> 26%
where the time goes in v5:
time: 87.5 us; the launch traced here: 87.1 us
  starting transfers between devices  31.2 us (36%)
  waiting for transfers between devices  28.3 us (32%)
  Pallas kernels  26.5 us (30%)
    all_to_all x2, waiting for transfers between devices, spread(): return lax.all_to_all(value, axes, split_axis=0, concat_axis=0, tiled=True)  25.8 us
    all_to_all x2, starting transfers between devices, spread(): return lax.all_to_all(value, axes, split_axis=0, concat_axis=0, tiled=True)  14.7 us
    pallas_call x1, Pallas kernels, contribute(): pl.pallas_call(contribute_kernel, in_specs=[scalars, scalars, scalars, pl...  11.3 us
    ppermute x4, starting transfers between devices, shift(): return lax.ppermute(value, axis, pairs)  11 us
    pallas_call x1, Pallas kernels, mix(): pl.pallas_call(mix_kernel, in_specs=[pl.BlockSpec(memory_space=pltpu.SMEM...  4.84 us
    pallas_call x1, Pallas kernels, gather_rows(): pl.pallas_call(functools.partial(gather_rows_kernel, tile_rows), in_specs...  4.64 us
    ppermute x1, starting transfers between devices, body(): received = lax.ppermute(received, 'mp', [(0, 1), (1, 0)])  4.12 us
    ppermute x1, waiting for transfers between devices, body(): received = lax.ppermute(received, 'mp', [(0, 1), (1, 0)])  2.5 us
  transfers between devices with their start and end apart: 9, of which 3 were waited for; matrix products, arithmetic and copies ran while one was open for 0% of the time, Pallas kernels for 26%

profile of v5, /device:TPU:1, one launch (start us, length us, event | category | flops | bytes accessed | tf_op | source)
XLA Modules:
  0.0 87.1 jit_solution(6184284201671252642)
XLA Ops:
  0.0 2.0 %edges.1 = (f32[24,512]{1,0:T(8,128)}, f32[24,512]{1,0:T(8,128)}) custom-call(f32[16,32,450]{2,1,0:T(8,128)} %bitcast.17, f32[16,32,450]{2,1,0:T(8,128)} %bitcast.18, f32[16,32,450]{2,1,0:T(8,128)} %bitcast.19, f32[32,450]{1,0:T(8,128)} %bitcast.25), custom_call_target="tpu_custom_call" | custom-call | tf_op jit(solution)/shard_map/edges/pallas_call | solution.py:193
  2.1 4.4 %collective-permute-start = (f32[24,512]{1,0:T(8,128)}, f32[24,512]{1,0:T(8,128)S(1)}, u32[]{:S(2)}, u32[]{:S(2)}) collective-permute-start(f32[24,512]{1,0:T(8,128)} %get-tuple-element.21), channel_id=1, source_target_pairs={{0,1},{1,2},{2,3},{3,4},{4,5},{5,6},{6,7},{7,0},{8,9},{9,10},{10,1... | collective-permute-start | bytes 147464 | tf_op jit(solution)/shard_map/ppermute | solution.py:373
  6.5 2.2 %collective-permute-start.1 = (f32[24,512]{1,0:T(8,128)}, f32[24,512]{1,0:T(8,128)S(1)}, u32[]{:S(2)}, u32[]{:S(2)}) collective-permute-start(f32[24,512]{1,0:T(8,128)} %get-tuple-element.22), channel_id=1, source_target_pairs={{1,0},{2,1},{3,2},{4,3},{5,4},{6,5},{7,6},{0,7},{9,8},{10,9},{11,1... | collective-permute-start | bytes 147464 | tf_op jit(solution)/shard_map/ppermute | solution.py:373
  8.7 11.3 %contribute.1 = f32[16,4,48,128]{3,2,1,0:T(8,128)} custom-call(s32[48]{0:T(128)S(1)} %bitcast.31, s32[48]{0:T(128)S(1)} %bitcast.32, s32[48]{0:T(128)S(1)} %bitcast.33, f32[16,32,450]{2,1,0:T(8,128)S(1)} %bitcast.22, bf16[450,48,450]{2,1,0:T(8,128)(2,1)} %bitcast.34), custom_call_target="tpu_custom_call" | custom-call | flops 311040000 | bytes 19440000 | tf_op jit(solution)/shard_map/contribute/pallas_call | solution.py:111
  20.0 0.0 collective-permute-done.1.east
  20.0 0.0 copy-start.12
  20.0 0.6 copy-done.11
  20.6 0.0 copy-done.12
  20.7 8.3 %all-to-all-start = ((f32[64,48,128]{2,1,0:T(8,128)}), f32[64,48,128]{2,1,0:T(8,128)S(1)}, u32[]{:S(2)}, u32[]{:S(2)}) async-start(f32[64,48,128]{2,1,0:T(8,128)} %bitcast.10), calls=%async_computation | async-start | bytes 3145728 | tf_op jit(solution)/shard_map/all_to_all | solution.py:384
  29.0 2.0 %rims.1 = (f32[34,512]{1,0:T(8,128)}, f32[34,512]{1,0:T(8,128)}, f32[3,16,450]{2,1,0:T(8,128)}, f32[2,32,128]{2,1,0:T(8,128)}) custom-call(f32[16,32,450]{2,1,0:T(8,128)} %bitcast.20, f32[16,32,450]{2,1,0:T(8,128)} %bitcast.21, f32[32,450]{1,0:T(8,128)} %bitcast.26, f32[24,512]{1,0:T(8,128)} %copy-done.11, f32[24,512]{1,0:T(8,128)} %copy-done.12), custom_call_target="tpu_custom_call" | custom-call | tf_op jit(solution)/shard_map/rims/pallas_call | solution.py:244
  31.0 0.7 collective-permute-start.5
  31.7 0.7 collective-permute-start.4
  32.4 2.9 %collective-permute-start.2 = (f32[34,512]{1,0:T(8,128)}, f32[34,512]{1,0:T(8,128)S(1)}, u32[]{:S(2)}, u32[]{:S(2)}) collective-permute-start(f32[34,512]{1,0:T(8,128)} %get-tuple-element.26), channel_id=1, source_target_pairs={{0,8},{8,16},{16,24},{24,32},{32,40},{40,48},{48,56},{1,9},{9,17},... | collective-permute-start | bytes 208904 | tf_op jit(solution)/shard_map/ppermute | solution.py:373
  35.3 1.5 %collective-permute-start.3 = (f32[34,512]{1,0:T(8,128)}, f32[34,512]{1,0:T(8,128)S(1)}, u32[]{:S(2)}, u32[]{:S(2)}) collective-permute-start(f32[34,512]{1,0:T(8,128)} %get-tuple-element.27), channel_id=1, source_target_pairs={{8,0},{16,8},{24,16},{32,24},{40,32},{48,40},{56,48},{9,1},{17,9},... | collective-permute-start | bytes 208904 | tf_op jit(solution)/shard_map/ppermute | solution.py:373
  36.8 15.3 %all-to-all-done = f32[64,48,128]{2,1,0:T(8,128)S(1)} async-done(((f32[64,48,128]{2,1,0:T(8,128)}), f32[64,48,128]{2,1,0:T(8,128)S(1)}, u32[]{:S(2)}, u32[]{:S(2)}) %all-to-all-start) | async-done | bytes 1572896 | tf_op jit(solution)/shard_map/all_to_all | solution.py:384
  52.1 4.6 %gather_rows.1 = f32[2048,128]{1,0:T(8,128)} custom-call(f32[3072,128]{1,0:T(8,128)S(1)} %bitcast.24), custom_call_target="tpu_custom_call" | custom-call | tf_op jit(solution)/shard_map/gather_rows/pallas_call | solution.py:156
  56.8 0.0 copy-start.7
  56.8 6.4 %all-to-all-start.1 = ((f32[64,32,128]{2,1,0:T(8,128)}), f32[64,32,128]{2,1,0:T(8,128)}, u32[]{:S(2)}, u32[]{:S(2)}) async-start(f32[64,32,128]{2,1,0:T(8,128)} %bitcast.12), calls=%async_computation.1 | async-start | bytes 2097152 | tf_op jit(solution)/shard_map/all_to_all | solution.py:384
  63.2 0.1 pad_add_fusion.flags
  63.3 4.8 %mix.1.base = f32[16,32,450]{2,1,0:T(8,128)S(1)} custom-call(s32[3]{0:T(128)S(1)} %pad_add_fusion.flags, f32[16,32,450]{2,1,0:T(8,128)S(1)} %bitcast.23, f32[32,450]{1,0:T(8,128)S(1)} %bitcast.27, f32[32,450]{1,0:T(8,128)S(1)} %bitcast.28, s32[32,450]{1,0:T(8,128)S(1)} %copy-done.4, f32[2,32,128]{2,1,0:T(8,128)S(1)} %copy-done.6, ...), custom_call_target="tpu_custom_call" | custom-call | tf_op jit(solution)/shard_map/mix/pallas_call | solution.py:322
  68.2 10.5 %all-to-all-done.1 = f32[64,32,128]{2,1,0:T(8,128)} async-done(((f32[64,32,128]{2,1,0:T(8,128)}), f32[64,32,128]{2,1,0:T(8,128)}, u32[]{:S(2)}, u32[]{:S(2)}) %all-to-all-start.1) | async-done | bytes 1048608 | tf_op jit(solution)/shard_map/all_to_all | solution.py:384
  78.7 4.1 %collective-permute-start.6 = (f32[64,32,128]{2,1,0:T(8,128)}, f32[64,32,128]{2,1,0:T(8,128)S(1)}, u32[]{:S(2)}, u32[]{:S(2)}) collective-permute-start(f32[64,32,128]{2,1,0:T(8,128)} %all-to-all-done.1), channel_id=1, source_target_pairs={{0,64},{64,0},{1,65},{65,1},{2,66},{66,2},{3,67},{67,3},{4,68},{68... | collective-permute-start | bytes 3145736 | tf_op jit(solution)/shard_map/ppermute | solution.py:437
  82.8 2.5 %collective-permute-done.6.received = f32[64,32,128]{2,1,0:T(8,128)S(1)} collective-permute-done((f32[64,32,128]{2,1,0:T(8,128)}, f32[64,32,128]{2,1,0:T(8,128)S(1)}, u32[]{:S(2)}, u32[]{:S(2)}) %collective-permute-start.6) | collective-permute-done | bytes 1048608 | tf_op jit(solution)/shard_map/ppermute | solution.py:437
  85.3 1.7 %finish.1 = f32[16,32,450]{2,1,0:T(8,128)} custom-call(s32[3]{0:T(128)S(1)} %pad_add_fusion.flags, f32[64,32,128]{2,1,0:T(8,128)S(1)} %collective-permute-done.6.received, f32[16,32,450]{2,1,0:T(8,128)S(1)} %mix.1.base, f32[32,450]{1,0:T(8,128)S(1)} %bitcast.29, s32[32,450]{1,0:T(8,128)S(1)} %copy-done.4), custom_call_target="tpu_custom_call" | custom-call | tf_op jit(solution)/shard_map/finish/pallas_call | solution.py:357
  (27 shorter events, 0.1 us)
Async XLA Ops:
  0.0 8.7 %copy-start = (f32[1,16,32,450]{3,2,1,0:T(8,128)S(1)}, f32[1,16,32,450]{3,2,1,0:T(8,128)}, u32[]{:S(2)}) copy-start(f32[1,16,32,450]{3,2,1,0:T(8,128)} %param.9) | copy-start | bytes 2764804
  0.0 8.7 %copy-start.8 = (s32[1,1,48]{2,1,0:T(1,128)S(1)}, s32[1,1,48]{2,1,0:T(1,128)}, u32[]{:S(2)}) copy-start(s32[1,1,48]{2,1,0:T(1,128)} %param.15) | copy-start | bytes 580
  0.0 8.7 %copy-start.9 = (s32[1,1,48,1]{2,3,1,0:T(1,128)S(1)}, s32[1,1,48,1]{2,3,1,0:T(1,128)}, u32[]{:S(2)}) copy-start(s32[1,1,48,1]{2,3,1,0:T(1,128)} %param.14) | copy-start | bytes 580
  0.0 8.7 %copy-start.10 = (s32[1,1,48]{2,1,0:T(1,128)S(1)}, s32[1,1,48]{2,1,0:T(1,128)}, u32[]{:S(2)}) copy-start(s32[1,1,48]{2,1,0:T(1,128)} %param.16) | copy-start | bytes 580
  2.1 18.0 %collective-permute-start = (f32[24,512]{1,0:T(8,128)}, f32[24,512]{1,0:T(8,128)S(1)}, u32[]{:S(2)}, u32[]{:S(2)}) collective-permute-start(f32[24,512]{1,0:T(8,128)} %get-tuple-element.21), channel_id=1, source_target_pairs={{0,1},{1,2},{2,3},{3,4},{4,5},{5,6},{6,7},{7,0},{8,9},{9,10},{10,1... | collective-permute-start | bytes 147464 | tf_op jit(solution)/shard_map/ppermute | solution.py:373
  6.5 13.5 %collective-permute-start.1 = (f32[24,512]{1,0:T(8,128)}, f32[24,512]{1,0:T(8,128)S(1)}, u32[]{:S(2)}, u32[]{:S(2)}) collective-permute-start(f32[24,512]{1,0:T(8,128)} %get-tuple-element.22), channel_id=1, source_target_pairs={{1,0},{2,1},{3,2},{4,3},{5,4},{6,5},{7,6},{0,7},{9,8},{10,9},{11,1... | collective-permute-start | bytes 147464 | tf_op jit(solution)/shard_map/ppermute | solution.py:373
  20.0 0.6 copy-start.11
  20.0 0.6 copy-start.12
  20.7 31.4 %all-to-all-start = ((f32[64,48,128]{2,1,0:T(8,128)}), f32[64,48,128]{2,1,0:T(8,128)S(1)}, u32[]{:S(2)}, u32[]{:S(2)}) async-start(f32[64,48,128]{2,1,0:T(8,128)} %bitcast.10), calls=%async_computation | async-start | bytes 3145728 | tf_op jit(solution)/shard_map/all_to_all | solution.py:384
  31.0 25.8 %collective-permute-start.5 = (f32[3,16,450]{2,1,0:T(8,128)}, f32[3,16,450]{2,1,0:T(8,128)S(1)}, u32[]{:S(2)}, u32[]{:S(2)}) collective-permute-start(f32[3,16,450]{2,1,0:T(8,128)} %get-tuple-element.28.near), channel_id=1, source_target_pairs={{120,125},{121,126},{122,127},{123,120},{124,121},{125,122},{126,1... | collective-permute-start | bytes 259208 | tf_op jit(solution)/shard_map/ppermute | solution.py:380
  31.7 25.1 %collective-permute-start.4 = (f32[3,16,450]{2,1,0:T(8,128)}, f32[3,16,450]{2,1,0:T(8,128)S(1)}, u32[]{:S(2)}, u32[]{:S(2)}) collective-permute-start(f32[3,16,450]{2,1,0:T(8,128)} %get-tuple-element.28.near), channel_id=1, source_target_pairs={{120,123},{121,124},{122,125},{123,126},{124,127},{125,120},{126,1... | collective-permute-start | bytes 259208 | tf_op jit(solution)/shard_map/ppermute | solution.py:380
  32.4 24.4 %collective-permute-start.2 = (f32[34,512]{1,0:T(8,128)}, f32[34,512]{1,0:T(8,128)S(1)}, u32[]{:S(2)}, u32[]{:S(2)}) collective-permute-start(f32[34,512]{1,0:T(8,128)} %get-tuple-element.26), channel_id=1, source_target_pairs={{0,8},{8,16},{16,24},{24,32},{32,40},{40,48},{48,56},{1,9},{9,17},... | collective-permute-start | bytes 208904 | tf_op jit(solution)/shard_map/ppermute | solution.py:373
  35.3 21.5 %collective-permute-start.3 = (f32[34,512]{1,0:T(8,128)}, f32[34,512]{1,0:T(8,128)S(1)}, u32[]{:S(2)}, u32[]{:S(2)}) collective-permute-start(f32[34,512]{1,0:T(8,128)} %get-tuple-element.27), channel_id=1, source_target_pairs={{8,0},{16,8},{24,16},{32,24},{40,32},{48,40},{56,48},{9,1},{17,9},... | collective-permute-start | bytes 208904 | tf_op jit(solution)/shard_map/ppermute | solution.py:373
  56.7 6.6 %copy-start.1 = (f32[1,16,32,450]{3,2,1,0:T(8,128)S(1)}, f32[1,16,32,450]{3,2,1,0:T(8,128)}, u32[]{:S(2)}) copy-start(f32[1,16,32,450]{3,2,1,0:T(8,128)} %param.9) | copy-start | bytes 2764804
  56.7 6.6 %copy-start.2 = (f32[1,32,450]{2,1,0:T(8,128)S(1)}, f32[1,32,450]{2,1,0:T(8,128)}, u32[]{:S(2)}) copy-start(f32[1,32,450]{2,1,0:T(8,128)} %param.10) | copy-start | bytes 172804
  56.7 6.6 %copy-start.3 = (f32[1,32,450]{2,1,0:T(8,128)S(1)}, f32[1,32,450]{2,1,0:T(8,128)}, u32[]{:S(2)}) copy-start(f32[1,32,450]{2,1,0:T(8,128)} %param.11) | copy-start | bytes 172804
  56.7 6.6 %copy-start.4 = (s32[32,450]{1,0:T(8,128)S(1)}, s32[32,450]{1,0:T(8,128)}, u32[]{:S(2)}) copy-start(s32[32,450]{1,0:T(8,128)} %mask.3) | copy-start | bytes 172804
  56.7 6.6 %copy-start.5 = (f32[3,16,450]{2,1,0:T(8,128)S(1)}, f32[3,16,450]{2,1,0:T(8,128)}, u32[]{:S(2)}) copy-start(f32[3,16,450]{2,1,0:T(8,128)} %get-tuple-element.28.near) | copy-start | bytes 259204
  56.7 6.6 %copy-start.6 = (f32[2,32,128]{2,1,0:T(8,128)S(1)}, f32[2,32,128]{2,1,0:T(8,128)}, u32[]{:S(2)}) copy-start(f32[2,32,128]{2,1,0:T(8,128)} %get-tuple-element.30.sides) | copy-start | bytes 98308
  56.8 6.6 %copy-start.7 = (s32[450]{0:T(512)S(1)}, s32[450]{0:T(512)}, u32[]{:S(2)}) copy-start(s32[450]{0:T(512)} %param.13) | copy-start | bytes 5404
  56.8 21.9 %all-to-all-start.1 = ((f32[64,32,128]{2,1,0:T(8,128)}), f32[64,32,128]{2,1,0:T(8,128)}, u32[]{:S(2)}, u32[]{:S(2)}) async-start(f32[64,32,128]{2,1,0:T(8,128)} %bitcast.12), calls=%async_computation.1 | async-start | bytes 2097152 | tf_op jit(solution)/shard_map/all_to_all | solution.py:384
  78.7 6.6 %collective-permute-start.6 = (f32[64,32,128]{2,1,0:T(8,128)}, f32[64,32,128]{2,1,0:T(8,128)S(1)}, u32[]{:S(2)}, u32[]{:S(2)}) collective-permute-start(f32[64,32,128]{2,1,0:T(8,128)} %all-to-all-done.1), channel_id=1, source_target_pairs={{0,64},{64,0},{1,65},{65,1},{2,66},{66,2},{3,67},{67,3},{4,68},{68... | collective-permute-start | bytes 3145736 | tf_op jit(solution)/shard_map/ppermute | solution.py:437

commit v6 on v5

--- a/solution.py
+++ b/solution.py
@@ -133,7 +133,7 @@
     )(source, tile, dest, state, weight)
 
 
-def gather_rows_kernel(tile_rows, values, out, halves, labels):
+def gather_rows_kernel(tile_rows, values, out, halves, labels, sums, stored):
     count = values.shape[0]
     x = values[...]
     high = x.astype(jnp.bfloat16)
@@ -144,11 +144,17 @@
     labels[...] = lax.dot_general(
         pick.astype(jnp.bfloat16), high, (((1,), (1,)), ((), ())), preferred_element_type=jnp.float32
     ).astype(jnp.int32)
+    stores = []
     for block in range(out.shape[0] // ROW_BLOCK):
         row = lax.broadcasted_iota(jnp.int32, (ROW_BLOCK, count), 0) + block * ROW_BLOCK
         onehot = jnp.where(row == labels[0:1, :], 1.0, 0.0).astype(jnp.bfloat16)
         both = jnp.dot(onehot, halves[...], preferred_element_type=jnp.float32)
-        out[block * ROW_BLOCK : (block + 1) * ROW_BLOCK, :] = both[:, :LANES] + both[:, LANES:]
+        span = pl.ds(block * ROW_BLOCK, ROW_BLOCK)
+        sums[span, :] = both[:, :LANES] + both[:, LANES:]
+        stores.append(pltpu.make_async_copy(sums.at[span], out.at[span], stored.at[block]))
+        stores[-1].start()
+    for store in stores:
+        store.wait()
 
 
 def gather_rows(values, tiles, tile_rows):
@@ -156,11 +162,13 @@
     return pl.pallas_call(
         functools.partial(gather_rows_kernel, tile_rows),
         in_specs=[pl.BlockSpec(memory_space=pltpu.VMEM)],
-        out_specs=pl.BlockSpec(memory_space=pltpu.VMEM),
+        out_specs=pl.BlockSpec(memory_space=pltpu.HBM),
         out_shape=jax.ShapeDtypeStruct((tiles * tile_rows, LANES), jnp.float32),
         scratch_shapes=[
             pltpu.VMEM((count, 2 * LANES), jnp.bfloat16),
             pltpu.VMEM((8, count), jnp.int32),
+            pltpu.VMEM((tiles * tile_rows, LANES), jnp.float32),
+            pltpu.SemaphoreType.DMA((tiles * tile_rows // ROW_BLOCK,)),
         ],
         compiler_params=pltpu.CompilerParams(vmem_limit_bytes=VMEM_LIMIT),
         name="gather_rows",

time: 87.5 us -> 87.5 us (level)
  no operation moved by 1% of the time
where the time goes in v6:
time: 87.5 us; the launch traced here: 87.1 us
  starting transfers between devices  31.3 us (36%)
  waiting for transfers between devices  28.3 us (32%)
  Pallas kernels  26.3 us (30%)
    all_to_all x2, waiting for transfers between devices, spread(): return lax.all_to_all(value, axes, split_axis=0, concat_axis=0, tiled=True)  25.8 us
    all_to_all x2, starting transfers between devices, spread(): return lax.all_to_all(value, axes, split_axis=0, concat_axis=0, tiled=True)  14.9 us
    pallas_call x1, Pallas kernels, contribute(): pl.pallas_call(contribute_kernel, in_specs=[scalars, scalars, scalars, pl...  11.3 us
    ppermute x4, starting transfers between devices, shift(): return lax.ppermute(value, axis, pairs)  11 us
    pallas_call x1, Pallas kernels, mix(): pl.pallas_call(mix_kernel, in_specs=[pl.BlockSpec(memory_space=pltpu.SMEM...  4.84 us
    pallas_call x1, Pallas kernels, gather_rows(): pl.pallas_call(functools.partial(gather_rows_kernel, tile_rows), in_specs...  4.45 us
    ppermute x1, starting transfers between devices, body(): received = lax.ppermute(received, 'mp', [(0, 1), (1, 0)])  4.14 us
    ppermute x1, waiting for transfers between devices, body(): received = lax.ppermute(received, 'mp', [(0, 1), (1, 0)])  2.5 us
  transfers between devices with their start and end apart: 9, of which 3 were waited for; matrix products, arithmetic and copies ran while one was open for 0% of the time, Pallas kernels for 26%

profile of v6, /device:TPU:1, one launch (start us, length us, event | category | flops | bytes accessed | tf_op | source)
XLA Modules:
  0.0 87.1 jit_solution(3549148292355632488)
XLA Ops:
  0.0 2.0 %edges.1 = (f32[24,512]{1,0:T(8,128)}, f32[24,512]{1,0:T(8,128)}) custom-call(f32[16,32,450]{2,1,0:T(8,128)} %bitcast.17, f32[16,32,450]{2,1,0:T(8,128)} %bitcast.18, f32[16,32,450]{2,1,0:T(8,128)} %bitcast.19, f32[32,450]{1,0:T(8,128)} %bitcast.25), custom_call_target="tpu_custom_call" | custom-call | tf_op jit(solution)/shard_map/edges/pallas_call | solution.py:201
  2.1 4.4 %collective-permute-start = (f32[24,512]{1,0:T(8,128)}, f32[24,512]{1,0:T(8,128)S(1)}, u32[]{:S(2)}, u32[]{:S(2)}) collective-permute-start(f32[24,512]{1,0:T(8,128)} %get-tuple-element.21), channel_id=1, source_target_pairs={{0,1},{1,2},{2,3},{3,4},{4,5},{5,6},{6,7},{7,0},{8,9},{9,10},{10,1... | collective-permute-start | bytes 147464 | tf_op jit(solution)/shard_map/ppermute | solution.py:381
  6.5 2.2 %collective-permute-start.1 = (f32[24,512]{1,0:T(8,128)}, f32[24,512]{1,0:T(8,128)S(1)}, u32[]{:S(2)}, u32[]{:S(2)}) collective-permute-start(f32[24,512]{1,0:T(8,128)} %get-tuple-element.22), channel_id=1, source_target_pairs={{1,0},{2,1},{3,2},{4,3},{5,4},{6,5},{7,6},{0,7},{9,8},{10,9},{11,1... | collective-permute-start | bytes 147464 | tf_op jit(solution)/shard_map/ppermute | solution.py:381
  8.7 11.3 %contribute.1 = f32[16,4,48,128]{3,2,1,0:T(8,128)} custom-call(s32[48]{0:T(128)S(1)} %bitcast.31, s32[48]{0:T(128)S(1)} %bitcast.32, s32[48]{0:T(128)S(1)} %bitcast.33, f32[16,32,450]{2,1,0:T(8,128)S(1)} %bitcast.22, bf16[450,48,450]{2,1,0:T(8,128)(2,1)} %bitcast.34), custom_call_target="tpu_custom_call" | custom-call | flops 311040000 | bytes 19440000 | tf_op jit(solution)/shard_map/contribute/pallas_call | solution.py:111
  20.0 0.0 copy-start.12
  20.0 0.6 copy-done.11
  20.6 0.0 copy-done.12
  20.7 8.3 %all-to-all-start = ((f32[64,48,128]{2,1,0:T(8,128)}), f32[64,48,128]{2,1,0:T(8,128)S(1)}, u32[]{:S(2)}, u32[]{:S(2)}) async-start(f32[64,48,128]{2,1,0:T(8,128)} %bitcast.10), calls=%async_computation | async-start | bytes 3145728 | tf_op jit(solution)/shard_map/all_to_all | solution.py:392
  29.0 2.0 %rims.1 = (f32[34,512]{1,0:T(8,128)}, f32[34,512]{1,0:T(8,128)}, f32[3,16,450]{2,1,0:T(8,128)}, f32[2,32,128]{2,1,0:T(8,128)}) custom-call(f32[16,32,450]{2,1,0:T(8,128)} %bitcast.20, f32[16,32,450]{2,1,0:T(8,128)} %bitcast.21, f32[32,450]{1,0:T(8,128)} %bitcast.26, f32[24,512]{1,0:T(8,128)} %copy-done.11, f32[24,512]{1,0:T(8,128)} %copy-done.12), custom_call_target="tpu_custom_call" | custom-call | tf_op jit(solution)/shard_map/rims/pallas_call | solution.py:252
  31.0 0.7 collective-permute-start.5
  31.7 0.7 collective-permute-start.4
  32.4 2.9 %collective-permute-start.2 = (f32[34,512]{1,0:T(8,128)}, f32[34,512]{1,0:T(8,128)S(1)}, u32[]{:S(2)}, u32[]{:S(2)}) collective-permute-start(f32[34,512]{1,0:T(8,128)} %get-tuple-element.26), channel_id=1, source_target_pairs={{0,8},{8,16},{16,24},{24,32},{32,40},{40,48},{48,56},{1,9},{9,17},... | collective-permute-start | bytes 208904 | tf_op jit(solution)/shard_map/ppermute | solution.py:381
  35.3 1.5 %collective-permute-start.3 = (f32[34,512]{1,0:T(8,128)}, f32[34,512]{1,0:T(8,128)S(1)}, u32[]{:S(2)}, u32[]{:S(2)}) collective-permute-start(f32[34,512]{1,0:T(8,128)} %get-tuple-element.27), channel_id=1, source_target_pairs={{8,0},{16,8},{24,16},{32,24},{40,32},{48,40},{56,48},{9,1},{17,9},... | collective-permute-start | bytes 208904 | tf_op jit(solution)/shard_map/ppermute | solution.py:381
  36.8 15.3 %all-to-all-done = f32[64,48,128]{2,1,0:T(8,128)S(1)} async-done(((f32[64,48,128]{2,1,0:T(8,128)}), f32[64,48,128]{2,1,0:T(8,128)S(1)}, u32[]{:S(2)}, u32[]{:S(2)}) %all-to-all-start) | async-done | bytes 1572896 | tf_op jit(solution)/shard_map/all_to_all | solution.py:392
  52.1 4.4 %gather_rows.1 = f32[2048,128]{1,0:T(8,128)} custom-call(f32[3072,128]{1,0:T(8,128)S(1)} %bitcast.24), custom_call_target="tpu_custom_call" | custom-call | tf_op jit(solution)/shard_map/gather_rows/pallas_call | solution.py:162
  56.6 0.0 copy-start.3
  56.6 0.0 copy-start.4
  56.7 6.5 %all-to-all-start.1 = ((f32[64,32,128]{2,1,0:T(8,128)}), f32[64,32,128]{2,1,0:T(8,128)}, u32[]{:S(2)}, u32[]{:S(2)}) async-start(f32[64,32,128]{2,1,0:T(8,128)} %bitcast.12), calls=%async_computation.1 | async-start | bytes 2097152 | tf_op jit(solution)/shard_map/all_to_all | solution.py:392
  63.2 0.1 pad_add_fusion.flags
  63.3 4.8 %mix.1.base = f32[16,32,450]{2,1,0:T(8,128)S(1)} custom-call(s32[3]{0:T(128)S(1)} %pad_add_fusion.flags, f32[16,32,450]{2,1,0:T(8,128)S(1)} %bitcast.23, f32[32,450]{1,0:T(8,128)S(1)} %bitcast.27, f32[32,450]{1,0:T(8,128)S(1)} %bitcast.28, s32[32,450]{1,0:T(8,128)S(1)} %copy-done.4, f32[2,32,128]{2,1,0:T(8,128)S(1)} %copy-done.6, ...), custom_call_target="tpu_custom_call" | custom-call | tf_op jit(solution)/shard_map/mix/pallas_call | solution.py:330
  68.2 10.5 %all-to-all-done.1 = f32[64,32,128]{2,1,0:T(8,128)} async-done(((f32[64,32,128]{2,1,0:T(8,128)}), f32[64,32,128]{2,1,0:T(8,128)}, u32[]{:S(2)}, u32[]{:S(2)}) %all-to-all-start.1) | async-done | bytes 1048608 | tf_op jit(solution)/shard_map/all_to_all | solution.py:392
  78.7 4.1 %collective-permute-start.6 = (f32[64,32,128]{2,1,0:T(8,128)}, f32[64,32,128]{2,1,0:T(8,128)S(1)}, u32[]{:S(2)}, u32[]{:S(2)}) collective-permute-start(f32[64,32,128]{2,1,0:T(8,128)} %all-to-all-done.1), channel_id=1, source_target_pairs={{0,64},{64,0},{1,65},{65,1},{2,66},{66,2},{3,67},{67,3},{4,68},{68... | collective-permute-start | bytes 3145736 | tf_op jit(solution)/shard_map/ppermute | solution.py:445
  82.8 2.5 %collective-permute-done.6.received = f32[64,32,128]{2,1,0:T(8,128)S(1)} collective-permute-done((f32[64,32,128]{2,1,0:T(8,128)}, f32[64,32,128]{2,1,0:T(8,128)S(1)}, u32[]{:S(2)}, u32[]{:S(2)}) %collective-permute-start.6) | collective-permute-done | bytes 1048608 | tf_op jit(solution)/shard_map/ppermute | solution.py:445
  85.3 1.7 %finish.1 = f32[16,32,450]{2,1,0:T(8,128)} custom-call(s32[3]{0:T(128)S(1)} %pad_add_fusion.flags, f32[64,32,128]{2,1,0:T(8,128)S(1)} %collective-permute-done.6.received, f32[16,32,450]{2,1,0:T(8,128)S(1)} %mix.1.base, f32[32,450]{1,0:T(8,128)S(1)} %bitcast.29, s32[32,450]{1,0:T(8,128)S(1)} %copy-done.4), custom_call_target="tpu_custom_call" | custom-call | tf_op jit(solution)/shard_map/finish/pallas_call | solution.py:365
  (27 shorter events, 0.1 us)
Async XLA Ops:
  0.0 8.7 %copy-start = (f32[1,16,32,450]{3,2,1,0:T(8,128)S(1)}, f32[1,16,32,450]{3,2,1,0:T(8,128)}, u32[]{:S(2)}) copy-start(f32[1,16,32,450]{3,2,1,0:T(8,128)} %param.9) | copy-start | bytes 2764804
  0.0 8.7 %copy-start.8 = (s32[1,1,48]{2,1,0:T(1,128)S(1)}, s32[1,1,48]{2,1,0:T(1,128)}, u32[]{:S(2)}) copy-start(s32[1,1,48]{2,1,0:T(1,128)} %param.15) | copy-start | bytes 580
  0.0 8.7 %copy-start.9 = (s32[1,1,48,1]{2,3,1,0:T(1,128)S(1)}, s32[1,1,48,1]{2,3,1,0:T(1,128)}, u32[]{:S(2)}) copy-start(s32[1,1,48,1]{2,3,1,0:T(1,128)} %param.14) | copy-start | bytes 580
  0.0 8.7 %copy-start.10 = (s32[1,1,48]{2,1,0:T(1,128)S(1)}, s32[1,1,48]{2,1,0:T(1,128)}, u32[]{:S(2)}) copy-start(s32[1,1,48]{2,1,0:T(1,128)} %param.16) | copy-start | bytes 580
  2.1 18.0 %collective-permute-start = (f32[24,512]{1,0:T(8,128)}, f32[24,512]{1,0:T(8,128)S(1)}, u32[]{:S(2)}, u32[]{:S(2)}) collective-permute-start(f32[24,512]{1,0:T(8,128)} %get-tuple-element.21), channel_id=1, source_target_pairs={{0,1},{1,2},{2,3},{3,4},{4,5},{5,6},{6,7},{7,0},{8,9},{9,10},{10,1... | collective-permute-start | bytes 147464 | tf_op jit(solution)/shard_map/ppermute | solution.py:381
  6.5 13.5 %collective-permute-start.1 = (f32[24,512]{1,0:T(8,128)}, f32[24,512]{1,0:T(8,128)S(1)}, u32[]{:S(2)}, u32[]{:S(2)}) collective-permute-start(f32[24,512]{1,0:T(8,128)} %get-tuple-element.22), channel_id=1, source_target_pairs={{1,0},{2,1},{3,2},{4,3},{5,4},{6,5},{7,6},{0,7},{9,8},{10,9},{11,1... | collective-permute-start | bytes 147464 | tf_op jit(solution)/shard_map/ppermute | solution.py:381
  20.0 0.6 copy-start.11
  20.0 0.6 copy-start.12
  20.7 31.4 %all-to-all-start = ((f32[64,48,128]{2,1,0:T(8,128)}), f32[64,48,128]{2,1,0:T(8,128)S(1)}, u32[]{:S(2)}, u32[]{:S(2)}) async-start(f32[64,48,128]{2,1,0:T(8,128)} %bitcast.10), calls=%async_computation | async-start | bytes 3145728 | tf_op jit(solution)/shard_map/all_to_all | solution.py:392
  31.0 25.6 %collective-permute-start.5 = (f32[3,16,450]{2,1,0:T(8,128)}, f32[3,16,450]{2,1,0:T(8,128)S(1)}, u32[]{:S(2)}, u32[]{:S(2)}) collective-permute-start(f32[3,16,450]{2,1,0:T(8,128)} %get-tuple-element.28.near), channel_id=1, source_target_pairs={{120,125},{121,126},{122,127},{123,120},{124,121},{125,122},{126,1... | collective-permute-start | bytes 259208 | tf_op jit(solution)/shard_map/ppermute | solution.py:388
  31.7 25.0 %collective-permute-start.4 = (f32[3,16,450]{2,1,0:T(8,128)}, f32[3,16,450]{2,1,0:T(8,128)S(1)}, u32[]{:S(2)}, u32[]{:S(2)}) collective-permute-start(f32[3,16,450]{2,1,0:T(8,128)} %get-tuple-element.28.near), channel_id=1, source_target_pairs={{120,123},{121,124},{122,125},{123,126},{124,127},{125,120},{126,1... | collective-permute-start | bytes 259208 | tf_op jit(solution)/shard_map/ppermute | solution.py:388
  32.4 24.3 %collective-permute-start.2 = (f32[34,512]{1,0:T(8,128)}, f32[34,512]{1,0:T(8,128)S(1)}, u32[]{:S(2)}, u32[]{:S(2)}) collective-permute-start(f32[34,512]{1,0:T(8,128)} %get-tuple-element.26), channel_id=1, source_target_pairs={{0,8},{8,16},{16,24},{24,32},{32,40},{40,48},{48,56},{1,9},{9,17},... | collective-permute-start | bytes 208904 | tf_op jit(solution)/shard_map/ppermute | solution.py:381
  35.3 21.3 %collective-permute-start.3 = (f32[34,512]{1,0:T(8,128)}, f32[34,512]{1,0:T(8,128)S(1)}, u32[]{:S(2)}, u32[]{:S(2)}) collective-permute-start(f32[34,512]{1,0:T(8,128)} %get-tuple-element.27), channel_id=1, source_target_pairs={{8,0},{16,8},{24,16},{32,24},{40,32},{48,40},{56,48},{9,1},{17,9},... | collective-permute-start | bytes 208904 | tf_op jit(solution)/shard_map/ppermute | solution.py:381
  56.5 6.8 %copy-start.1 = (f32[1,16,32,450]{3,2,1,0:T(8,128)S(1)}, f32[1,16,32,450]{3,2,1,0:T(8,128)}, u32[]{:S(2)}) copy-start(f32[1,16,32,450]{3,2,1,0:T(8,128)} %param.9) | copy-start | bytes 2764804
  56.5 6.7 %copy-start.2 = (f32[1,32,450]{2,1,0:T(8,128)S(1)}, f32[1,32,450]{2,1,0:T(8,128)}, u32[]{:S(2)}) copy-start(f32[1,32,450]{2,1,0:T(8,128)} %param.10) | copy-start | bytes 172804
  56.6 6.7 %copy-start.3 = (f32[1,32,450]{2,1,0:T(8,128)S(1)}, f32[1,32,450]{2,1,0:T(8,128)}, u32[]{:S(2)}) copy-start(f32[1,32,450]{2,1,0:T(8,128)} %param.11) | copy-start | bytes 172804
  56.6 6.7 %copy-start.4 = (s32[32,450]{1,0:T(8,128)S(1)}, s32[32,450]{1,0:T(8,128)}, u32[]{:S(2)}) copy-start(s32[32,450]{1,0:T(8,128)} %mask.3) | copy-start | bytes 172804
  56.6 6.7 %copy-start.5 = (f32[3,16,450]{2,1,0:T(8,128)S(1)}, f32[3,16,450]{2,1,0:T(8,128)}, u32[]{:S(2)}) copy-start(f32[3,16,450]{2,1,0:T(8,128)} %get-tuple-element.28.near) | copy-start | bytes 259204
  56.6 6.7 %copy-start.6 = (f32[2,32,128]{2,1,0:T(8,128)S(1)}, f32[2,32,128]{2,1,0:T(8,128)}, u32[]{:S(2)}) copy-start(f32[2,32,128]{2,1,0:T(8,128)} %get-tuple-element.30.sides) | copy-start | bytes 98308
  56.6 6.7 %copy-start.7 = (s32[450]{0:T(512)S(1)}, s32[450]{0:T(512)}, u32[]{:S(2)}) copy-start(s32[450]{0:T(512)} %param.13) | copy-start | bytes 5404
  56.7 22.0 %all-to-all-start.1 = ((f32[64,32,128]{2,1,0:T(8,128)}), f32[64,32,128]{2,1,0:T(8,128)}, u32[]{:S(2)}, u32[]{:S(2)}) async-start(f32[64,32,128]{2,1,0:T(8,128)} %bitcast.12), calls=%async_computation.1 | async-start | bytes 2097152 | tf_op jit(solution)/shard_map/all_to_all | solution.py:392
  78.7 6.6 %collective-permute-start.6 = (f32[64,32,128]{2,1,0:T(8,128)}, f32[64,32,128]{2,1,0:T(8,128)S(1)}, u32[]{:S(2)}, u32[]{:S(2)}) collective-permute-start(f32[64,32,128]{2,1,0:T(8,128)} %all-to-all-done.1), channel_id=1, source_target_pairs={{0,64},{64,0},{1,65},{65,1},{2,66},{66,2},{3,67},{67,3},{4,68},{68... | collective-permute-start | bytes 3145736 | tf_op jit(solution)/shard_map/ppermute | solution.py:445
